TPU v7x, 32 devices: a whole 2x2x4 slice. The times are simulated.
32 devices in a mesh: batch: 8 (over z, x), module: 4 (over y, core).
Axes of the slice: x: 2, y: 2, z: 4, core: 2. Of those that a mesh axis runs over, the one named last changes fastest.
Arguments:
- tokens: bfloat16 [16384, 256], P(('batch', 'module')), may hold values from -6 to 6
- seg_lengths: int32 [8, 8], P('batch'), may hold values from 1 to 1024, 2048 in all within a row
- valid: int32 [16384], P('batch'), may hold values 0 or 1
- cotangent: bfloat16 [16384, 256], P(('batch', 'module')), may hold values from -6 to 6
- gain_one: float32 [256], replicated, may hold values from 0.5 to 1.5
- w_query: bfloat16 [256, 256], replicated, may hold values from -0.375 to 0.375
- w_key: bfloat16 [256, 256], replicated, may hold values from -0.375 to 0.375
- w_value: bfloat16 [256, 256], replicated, may hold values from -0.375 to 0.375
- w_attn_out: bfloat16 [256, 256], replicated, may hold values from -2 to 2
- w_cross: bfloat16 [256, 256], replicated, may hold values from -0.375 to 0.375
- b_cross: float32 [256], replicated, may hold values from -3 to 3
- w_mix: bfloat16 [256, 256], replicated, may hold values from -3 to 3
- w_ens1: bfloat16 [1024, 256], replicated, may hold values from -0.1875 to 0.1875
- gain_two: float32 [256], replicated, may hold values from 0.5 to 1.5
- w_up: bfloat16 [256, 1024], replicated, may hold values from -0.375 to 0.375
- b_up: float32 [1024], replicated, may hold values from -3 to 3
- w_ens2: bfloat16 [1280, 256], replicated, may hold values from -0.15625 to 0.15625
Outputs:
- out_rows: float32 [16384, 256], P(('batch', 'module'))
- grad_tokens: float32 [16384, 256], P(('batch', 'module'))
- grad_gain_one: float32 [256], replicated
- grad_query: float32 [256, 256], replicated
- grad_key: float32 [256, 256], replicated
- grad_value: float32 [256, 256], replicated
- grad_attn_out: float32 [256, 256], replicated
- grad_cross: float32 [256, 256], replicated
- grad_b_cross: float32 [256], replicated
- grad_mix: float32 [256, 256], replicated
- grad_ens1: float32 [1024, 256], replicated
- grad_gain_two: float32 [256], replicated
- grad_up: float32 [256, 1024], replicated
- grad_b_up: float32 [1024], replicated
- grad_ens2: float32 [1280, 256], replicated
Inputs may be any that keep to these rules, and one draw needn't show every extreme that they name: `seg_lengths`: each row's 8 lengths sum to 2048 and the longest is exactly 1024.
All inputs are finite; a program needn't handle non-finite values. No bound on the sum of `valid` on one device may be relied on, other than what follows from the above.
Results may differ from a plain program's by a relative error of at most 0.014.
Values may be sent and summed in bfloat16 or wider, within the bound.
No kernel may reach another device: no remote copies, remote signals or barrier semaphores. Data moves between devices by JAX's collectives and lax.ppermute only.
A program may use at most 64 MiB of HBM per device.

v0:
```python
import functools

import jax
import jax.numpy as jnp
from jax import lax
from jax.experimental import pallas as pl
from jax.experimental.pallas import tpu as pltpu
from jax.sharding import PartitionSpec as P

D = 256
HEADS = 4
HEAD_DIM = 64
FF = 1024
SEGS = 8
LANES = 128
WIDE = HEADS * LANES
HUGE = -1e30
BF = jnp.bfloat16
F32 = jnp.float32
MIB = 1024 * 1024


def low(v):
    return v.astype(BF)


def high(v):
    return v.astype(F32)


def dot(a, b):
    return jnp.dot(a, b, preferred_element_type=F32)


def dot_nt(a, b):
    return lax.dot_general(a, b, (((1,), (1,)), ((), ())), preferred_element_type=F32)


def dot_tn(a, b):
    return lax.dot_general(a, b, (((0,), (0,)), ((), ())), preferred_element_type=F32)


def head_sums(selector, product):
    upper = low(product)
    lower = low(product - high(upper))
    return dot_nt(selector, upper) + dot_nt(selector, lower)


def unit_rows(values):
    center = values - jnp.mean(values, axis=1, keepdims=True)
    scale = lax.rsqrt(jnp.mean(center * center, axis=1, keepdims=True) + 1e-05)
    return center * scale, scale


def norm_back(grad, unit, scale, gain):
    scaled = grad * gain
    first_mean = jnp.mean(scaled, axis=1, keepdims=True)
    second_mean = jnp.mean(scaled * unit, axis=1, keepdims=True)
    return scale * (scaled - first_mean - unit * second_mean)


def in_vmem():
    return pl.BlockSpec(memory_space=pltpu.VMEM)


def in_smem():
    return pl.BlockSpec(memory_space=pltpu.SMEM)


def call(body, outs, n_smem, n_vmem, scratch=(), limit=48, flops=0):
    return pl.pallas_call(
        body,
        out_shape=[jax.ShapeDtypeStruct(shape, kind) for shape, kind in outs],
        in_specs=[in_smem()] * n_smem + [in_vmem()] * n_vmem,
        out_specs=[in_vmem()] * len(outs),
        scratch_shapes=list(scratch),
        compiler_params=pltpu.CompilerParams(vmem_limit_bytes=limit * MIB),
        cost_estimate=pl.CostEstimate(flops=flops, bytes_accessed=1 * MIB, transcendentals=0),
    )


def widen(weight):
    rows = weight.shape[0]
    gap = jnp.zeros((rows, LANES - HEAD_DIM), weight.dtype)
    pieces = []
    for head in range(HEADS):
        pieces += [weight[:, head * HEAD_DIM : (head + 1) * HEAD_DIM], gap]
    return jnp.concatenate(pieces, axis=1)


def widen_rows(weight):
    gap = jnp.zeros((LANES - HEAD_DIM, weight.shape[1]), weight.dtype)
    pieces = []
    for head in range(HEADS):
        pieces += [weight[head * HEAD_DIM : (head + 1) * HEAD_DIM], gap]
    return jnp.concatenate(pieces, axis=0)


def narrow(wide):
    return jnp.concatenate(
        [wide[:, h * LANES : h * LANES + HEAD_DIM] for h in range(HEADS)], axis=1
    )


def narrow_rows(wide):
    return jnp.concatenate([wide[h * LANES : h * LANES + HEAD_DIM] for h in range(HEADS)], axis=0)


def segment_rows(seg_ref, first_place, count):
    spread = lax.broadcasted_iota(jnp.int32, (16, count), 0)
    places = lax.broadcasted_iota(jnp.int32, (16, count), 1) + first_place
    begin = jnp.zeros((16, count), jnp.int32)
    end = jnp.zeros((16, count), jnp.int32)
    edge = jnp.int32(0)
    for j in range(SEGS):
        begin = jnp.where(spread == j, edge, begin)
        edge = edge + seg_ref[0, j]
        end = jnp.where(spread == j, edge, end)
    return spread, (places >= begin) & (places < end)


def lane_selector(top):
    rows = lax.broadcasted_iota(jnp.int32, (16, WIDE), 0)
    lanes = lax.broadcasted_iota(jnp.int32, (16, WIDE), 1)
    return ((lanes & (LANES - 1)) == rows + HEAD_DIM) & (rows < top)


def head_selector():
    rows = lax.broadcasted_iota(jnp.int32, (16, WIDE), 0)
    lanes = lax.broadcasted_iota(jnp.int32, (16, WIDE), 1)
    return low(jnp.where((lanes >> 7) == rows, 1.0, 0.0))


def prep_kernel(wq, wk, wv, wo, wq_pad, wk_pad, wv_pad, wo_pad, wk_t, wv_t):
    wq_pad[...] = low(widen(high(wq[...])))
    wk_pad[...] = low(widen(high(wk[...])))
    wv_pad[...] = low(widen(high(wv[...])))
    wo_pad[...] = low(widen_rows(high(wo[...])))
    wk_t[...] = low(high(wk[...]).T)
    wv_t[...] = low(high(wv[...]).T)


def forward_kernel(
    own_rows, rows, chunk,
    me_ref, seg_ref,
    t0, t1, t2, t3, valid, cot,
    gain_one, wq_pad, wk_pad, wv_pad, wo_pad, wk_t, wv_t,
    w_cross, b_cross, w_mix, w_ens1, gain_two, w_up, b_up, w_ens2,
    out_rows, d_first_out, dn_own, payload, vectors,
    normed, q_aug, k_aug, v_pad, kt, grad_att, lse_out, delta_out, pself_out, dself_out, seg_grad_out,
    vt, scores, o_t,
):
    me = me_ref[0]
    base = pl.multiple_of(me * own_rows, own_rows)
    gain = gain_one[...]
    for delta, piece in enumerate((t0, t1, t2, t3)):
        unit, _ = unit_rows(high(piece[...]))
        at = pl.multiple_of((me ^ delta) * own_rows, own_rows)
        normed[pl.ds(at, own_rows), :] = low(unit * gain)
    normed_own = normed[pl.ds(base, own_rows), :]

    valid_row = valid[...]
    spread, inside = segment_rows(seg_ref, 0, rows)
    real = valid_row > 0
    inside_valid = jnp.where(inside & real, 1.0, 0.0)
    counts = jnp.maximum(jnp.sum(inside_valid, axis=1, keepdims=True), 1.0)
    code = jnp.where(inside, HUGE, 0.0)
    code = jnp.where(spread == SEGS, jnp.where(real, 0.0, HUGE), code)
    lanes9 = low(jnp.where(lane_selector(SEGS + 1), 1.0, 0.0))
    k_wide = dot(normed[...], wk_pad[...])
    k_aug[...] = low(k_wide + dot_tn(low(code), lanes9))
    _, inside_own = segment_rows(seg_ref, base, own_rows)
    own_code = jnp.where(inside_own, 0.0, 1.0)
    q_wide = dot(normed_own, wq_pad[...])
    q_aug[...] = low(q_wide * 0.125 + dot_tn(low(own_code), lanes9))
    v_pad[...] = low(dot(normed[...], wv_pad[...]))
    kt[...] = low(dot_nt(wk_t[...], normed[...]))
    vt[...] = low(dot_nt(wv_t[...], normed[...]))

    heads16 = head_selector()
    lanes_own = lax.broadcasted_iota(jnp.int32, (own_rows, WIDE), 1) & (LANES - 1)
    k_own = k_aug[pl.ds(base, own_rows), :]
    v_own = v_pad[pl.ds(base, own_rows), :]
    self_product = jnp.where(lanes_own < HEAD_DIM, high(q_aug[...]) * high(k_own), 0.0)
    self_scores = head_sums(heads16, self_product)
    own_real = valid[:, pl.ds(base, own_rows)] > 0
    vt_own = vt[:, pl.ds(base, own_rows)]
    o_t[...] = jnp.zeros_like(o_t)
    lse_out[...] = jnp.zeros_like(lse_out)
    for h in range(HEADS):
        lanes = slice(h * LANES, (h + 1) * LANES)
        q_h = q_aug[:, lanes]
        top = jnp.where(own_real, HUGE, self_scores[h : h + 1])
        self_h = top
        for c in range(rows // chunk):
            part = dot_nt(k_aug[c * chunk : (c + 1) * chunk, lanes], q_h)
            scores[c * chunk : (c + 1) * chunk, :] = part
            top = jnp.maximum(top, jnp.max(part, axis=0, keepdims=True))
        p_self = jnp.exp(self_h - top)
        total = p_self
        acc = high(low(p_self)) * high(vt_own[h * HEAD_DIM : (h + 1) * HEAD_DIM])
        for c in range(rows // chunk):
            p = jnp.exp(scores[c * chunk : (c + 1) * chunk, :] - top)
            total = total + jnp.sum(p, axis=0, keepdims=True)
            acc = acc + dot(
                vt[h * HEAD_DIM : (h + 1) * HEAD_DIM, c * chunk : (c + 1) * chunk], low(p)
            )
        o_t[h * LANES : h * LANES + HEAD_DIM, :] = acc / total
        lse_out[h : h + 1, :] = top + jnp.log(total)
    att = o_t[...].T
    att_low = low(att)

    modules = []
    for g in range(2):
        lanes = slice(g * 256, (g + 1) * 256)
        modules.append(low(dot(att_low[:, lanes], wo_pad[lanes, :])))
    crossed = dot(normed_own, w_cross[...]) + b_cross[...]
    modules.append(low(high(normed_own) * crossed))
    seg_mean = low(dot(low(inside_valid), normed[...]) / counts)
    own_member = low(jnp.where(inside_own, 1.0, 0.0))
    mixed = low(dot_tn(own_member, seg_mean))
    modules.append(low(dot(mixed, w_mix[...])))
    first = high(t0[...])
    for i in range(4):
        first = first + dot(modules[i], w_ens1[i * D : (i + 1) * D, :])
    unit_two, scale_two = unit_rows(first)
    normed_two = low(unit_two * gain_two[...])
    inner = dot(normed_two, w_up[...]) + b_up[...]
    cdf = 0.5 * (1.0 + lax.erf(inner * 0.7071067811865476))
    active = low(inner * cdf)
    slope = cdf + inner * jnp.exp(-0.5 * inner * inner) * 0.3989422804014327
    out_rows[...] = first + (dot(active, w_ens2[:FF, :]) + dot(normed_two, w_ens2[FF:, :]))

    half = payload.shape[0] // 2

    def put(at, grad):
        middle = grad.shape[0] // 2
        payload[at : at + middle, :] = low(grad[:middle])
        payload[half + at : half + at + middle, :] = low(grad[middle:])
        return at + middle

    e2 = cot[...]
    at = put(0, dot_tn(active, e2))
    at = put(at, dot_tn(normed_two, e2))
    d_inner = low(dot_nt(e2, w_ens2[:FF, :]) * slope)
    b_up_grad = jnp.sum(high(d_inner), axis=0, keepdims=True)
    grad_up = dot_tn(normed_two, d_inner)
    for i in range(FF // D):
        at = put(at, grad_up[:, i * D : (i + 1) * D])
    d_norm2 = dot_nt(e2, w_ens2[FF:, :]) + dot_nt(d_inner, w_up[...])
    d_first = high(e2) + norm_back(d_norm2, unit_two, scale_two, gain_two[...])
    d_first_out[...] = d_first
    e1 = low(d_first)
    d_modules = []
    for i in range(4):
        at = put(at, dot_tn(modules[i], e1))
        d_modules.append(low(dot_nt(e1, w_ens1[i * D : (i + 1) * D, :])))
    out_grads = []
    for g in range(2):
        lanes = slice(g * 256, (g + 1) * 256)
        out_grads.append(dot_tn(att_low[:, lanes], d_modules[g]))
        grad_att[:, lanes] = low(dot_nt(d_modules[g], wo_pad[lanes, :]))
    at = put(at, narrow_rows(jnp.concatenate(out_grads, axis=0)))
    d_cross = low(high(d_modules[2]) * high(normed_own))
    at = put(at, dot_tn(normed_own, d_cross))
    at = put(at, dot_tn(mixed, d_modules[3]))
    dn_own[...] = high(d_modules[2]) * crossed + dot_nt(d_cross, w_cross[...])
    d_mixed = dot_nt(d_modules[3], w_mix[...])
    mixed_up = low(d_mixed)
    mixed_down = low(d_mixed - high(mixed_up))
    seg_grad_out[...] = (dot(own_member, mixed_up) + dot(own_member, mixed_down)) / counts
    vectors[...] = jnp.zeros_like(vectors)
    for i in range(FF // D):
        vectors[i : i + 1, :] = b_up_grad[:, i * D : (i + 1) * D]
    vectors[4:5, :] = jnp.sum(high(d_cross), axis=0, keepdims=True)
    vectors[5:6, :] = jnp.sum(d_norm2 * unit_two, axis=0, keepdims=True)

    d_att = high(grad_att[...])
    delta = head_sums(heads16, d_att * att)
    delta_out[...] = delta
    p_self = jnp.where(own_real, 0.0, jnp.exp(self_scores - lse_out[...]))
    dp_self = head_sums(heads16, d_att * high(v_own))
    pself_out[...] = low(p_self)
    dself_out[...] = low(p_self * (dp_self - delta))


def backward_kernel(
    own_rows, rows, chunk,
    me_ref, seg_ref,
    normed, q_aug, k_aug, v_pad, kt, grad_att, lse, delta, pself, dself, seg_grad, dn_own, valid,
    gain_one, wq_pad, wk_pad, wv_pad, vectors,
    keep, send,
    dk, dv, dq_t, dn, both,
):
    me = me_ref[0]
    base = pl.multiple_of(me * own_rows, own_rows)
    heads16 = head_selector()
    dq_t[...] = jnp.zeros_like(dq_t)
    kt_own = kt[:, pl.ds(base, own_rows)]
    for h in range(HEADS):
        lanes = slice(h * LANES, (h + 1) * LANES)
        q_h = q_aug[:, lanes]
        g_h = grad_att[:, lanes]
        lse_h = lse[h : h + 1, :]
        delta_h = delta[h : h + 1, :]
        acc = high(dself[h : h + 1, :]) * high(kt_own[h * HEAD_DIM : (h + 1) * HEAD_DIM])
        for c in range(rows // chunk):
            at = slice(c * chunk, (c + 1) * chunk)
            p = jnp.exp(dot_nt(k_aug[at, lanes], q_h) - lse_h)
            ds = low(p * (dot_nt(v_pad[at, lanes], g_h) - delta_h))
            dv[at, lanes] = dot(low(p), g_h)
            dk[at, lanes] = dot(ds, q_h)
            acc = acc + dot(kt[h * HEAD_DIM : (h + 1) * HEAD_DIM, at], ds)
        dq_t[h * LANES : h * LANES + HEAD_DIM, :] = acc
    own = pl.ds(base, own_rows)
    dk[own, :] = dk[own, :] + dot_tn(dself[...], heads16) * high(q_aug[...])
    dv[own, :] = dv[own, :] + dot_tn(pself[...], heads16) * high(grad_att[...])
    dq = low(dq_t[...].T * 0.125)
    dk_low = low(dk[...])
    dv_low = low(dv[...])
    _, inside = segment_rows(seg_ref, 0, rows)
    member = low(jnp.where(inside & (valid[...] > 0), 1.0, 0.0))
    up = low(seg_grad[...])
    down = low(seg_grad[...] - high(up))
    mixing = dot_tn(member, up) + dot_tn(member, down)
    dn[...] = dot_nt(dk_low, wk_pad[...]) + dot_nt(dv_low, wv_pad[...]) + mixing
    dn[own, :] = dn[own, :] + dot_nt(dq, wq_pad[...]) + dn_own[...]
    gain_grad = jnp.sum(dn[...] * high(normed[...]), axis=0, keepdims=True) / gain_one[...]

    def rows_of(step):
        return dn[pl.ds(pl.multiple_of((me ^ step) * own_rows, own_rows), own_rows), :]

    keep[:own_rows, :] = low(rows_of(0))
    send[:own_rows, :] = low(rows_of(1))
    keep[own_rows : 2 * own_rows, :] = low(rows_of(2))
    send[own_rows : 2 * own_rows, :] = low(rows_of(3))
    normed_own = normed[own, :]
    third = D // 2
    for i, grad in enumerate(
        (
            narrow(dot_tn(normed_own, dq)),
            narrow(dot_tn(normed[...], dk_low)),
            narrow(dot_tn(normed[...], dv_low)),
        )
    ):
        both[i * third : (i + 1) * third, :] = low(grad[:third])
        both[(3 + i) * third : (4 + i) * third, :] = low(grad[third:])
    core = me & 1
    mine = pl.ds(pl.multiple_of(core * 3 * third, third), 3 * third)
    other = pl.ds(pl.multiple_of((1 - core) * 3 * third, third), 3 * third)
    keep[2 * own_rows : 2 * own_rows + 3 * third, :] = both[mine, :]
    send[2 * own_rows : 2 * own_rows + 3 * third, :] = both[other, :]
    tail = lax.broadcasted_iota(jnp.int32, (16, D), 0)
    row = jnp.where(tail == 6, gain_grad, vectors[...])
    keep[2 * own_rows + 3 * third :, :] = low(row)
    send[2 * own_rows + 3 * third :, :] = low(row)


def finish_kernel(mine, other, tokens, d_first, gain_one, grad_tokens):
    unit, scale = unit_rows(high(tokens[...]))
    total = high(mine[...]) + high(other[...])
    grad_tokens[...] = d_first[...] + norm_back(total, unit, scale, gain_one[...])


def swap(value, axis, count, step):
    return lax.ppermute(value, axis, [(i, i ^ step) for i in range(count)])


def split(value, bit):
    half = value.shape[0] // 2
    return (
        lax.dynamic_slice_in_dim(value, bit * half, half, 0),
        lax.dynamic_slice_in_dim(value, (1 - bit) * half, half, 0),
    )


def join(mine, other, bit):
    return jnp.where(
        bit == 0, jnp.concatenate([mine, other], 0), jnp.concatenate([other, mine], 0)
    )


def added(one, two):
    return low(high(one) + high(two))


def shards(
    n_batch,
    n_module,
    tokens,
    seg_lengths,
    valid,
    cotangent,
    gain_one,
    w_query,
    w_key,
    w_value,
    w_attn_out,
    w_cross,
    b_cross,
    w_mix,
    w_ens1,
    gain_two,
    w_up,
    b_up,
    w_ens2,
):
    module = lax.axis_index("module")
    batch = lax.axis_index("batch")
    core = module & 1
    y_bit = (module >> 1) & 1
    x_bit = batch & 1
    own_rows = tokens.shape[0]
    rows = valid.shape[0]
    chunk = 512
    me = jnp.reshape(module, (1,)).astype(jnp.int32)

    def by_core(value):
        return swap(value, "module", n_module, 1)

    def by_y(value):
        return swap(value, "module", n_module, 2)

    def by_batch(value, step):
        return swap(value, "batch", n_batch, step)

    from_y = by_y(tokens)
    from_core = by_core(tokens)
    from_far = by_core(from_y)
    bf_square = ((D, D), BF)
    wq_pad, wk_pad, wv_pad, wo_pad, wk_t, wv_t = call(
        prep_kernel, [((D, WIDE), BF)] * 3 + [((WIDE, D), BF)] + [bf_square] * 2, 0, 4
    )(w_query, w_key, w_value, w_attn_out)
    valid_row = valid.reshape(1, rows)
    gain_row = gain_one.reshape(1, D)
    (
        out_rows, d_first, dn_own, payload, vectors,
        normed, q_aug, k_aug, v_pad, kt, grad_att, lse, delta, pself, dself, seg_grad,
    ) = call(
        functools.partial(forward_kernel, own_rows, rows, chunk),
        [
            ((own_rows, D), F32), ((own_rows, D), F32), ((own_rows, D), F32), ((16 * D, D), BF), ((16, D), F32),
            ((rows, D), BF), ((own_rows, WIDE), BF), ((rows, WIDE), BF), ((rows, WIDE), BF), ((D, rows), BF),
            ((own_rows, WIDE), BF), ((16, own_rows), F32), ((16, own_rows), F32), ((16, own_rows), BF),
            ((16, own_rows), BF), ((16, D), F32),
        ],
        2, 21,
        [pltpu.VMEM((D, rows), BF), pltpu.VMEM((rows, own_rows), F32), pltpu.VMEM((WIDE, own_rows), F32)],
    )(
        me, seg_lengths, tokens, from_core, from_y, from_far, valid_row, cotangent,
        gain_row, wq_pad, wk_pad, wv_pad, wo_pad, wk_t, wv_t,
        w_cross, b_cross.reshape(1, D), w_mix, w_ens1, gain_two.reshape(1, D), w_up, b_up.reshape(1, FF), w_ens2,
    )

    keep, send = split(payload, core)
    big = added(keep, by_core(send))
    middle = big.shape[0] // 2
    a_keep, a_send = split(big[:middle], y_bit)
    b_keep, b_send = split(big[middle:], x_bit)
    a = added(a_keep, by_y(a_send))
    b = added(b_keep, by_batch(b_send, 1))
    a_keep, a_send = split(a, x_bit)
    b_keep, b_send = split(b, y_bit)
    a = added(a_keep, by_batch(a_send, 1))
    b = added(b_keep, by_y(b_send))

    def through_batch(value):
        steps = []
        step = 2
        while step < n_batch:
            steps.append(step)
            step *= 2
        if not steps:
            return value
        low_bit = (batch >> 1) & 1
        kept, sent = split(value, low_bit)
        value = added(kept, by_batch(sent, steps[0]))
        for step in steps[1:]:
            value = added(value, by_batch(value, step))
        return join(value, by_batch(value, steps[0]), low_bit)

    ab = through_batch(jnp.concatenate([a, b], axis=0))
    a, b = ab[: middle // 4], ab[middle // 4 :]
    a = join(a, by_batch(a, 1), x_bit)
    b = join(b, by_y(b), y_bit)
    a = join(a, by_y(a), y_bit)
    b = join(b, by_batch(b, 1), x_bit)
    big = jnp.concatenate([a, b], axis=0)
    big = join(big, by_core(big), core)

    third = D // 2
    small = 2 * own_rows + 3 * third + 16
    keep, send = call(
        functools.partial(backward_kernel, own_rows, rows, chunk),
        [((small, D), BF)] * 2,
        2, 18,
        [
            pltpu.VMEM((rows, WIDE), F32), pltpu.VMEM((rows, WIDE), F32), pltpu.VMEM((WIDE, own_rows), F32),
            pltpu.VMEM((rows, D), F32), pltpu.VMEM((6 * third, D), BF),
        ],
    )(
        me, seg_lengths, normed, q_aug, k_aug, v_pad, kt, grad_att, lse, delta, pself, dself, seg_grad,
        dn_own, valid_row, gain_row, wq_pad, wk_pad, wv_pad, vectors,
    )
    total = added(keep, by_core(send))
    dn_mine, dn_other = total[:own_rows], total[own_rows : 2 * own_rows]
    qkv_keep, qkv_send = split(total[2 * own_rows : 2 * own_rows + 3 * third], y_bit)
    vec = total[2 * own_rows + 3 * third :]
    got = by_y(jnp.concatenate([dn_other, qkv_send, vec], axis=0))
    (grad_tokens,) = call(finish_kernel, [((own_rows, D), F32)], 0, 5)(
        dn_mine, got[:own_rows], tokens, d_first, gain_row
    )
    qkv = added(qkv_keep, got[own_rows:-16])
    vec = added(vec, got[-16:])
    qkv_keep, qkv_send = split(qkv, x_bit)
    got = by_batch(jnp.concatenate([qkv_send, vec], axis=0), 1)
    qkv = added(qkv_keep, got[:-16])
    vec = added(vec, got[-16:])
    step = 2
    while step < n_batch:
        both = jnp.concatenate([qkv, vec], axis=0)
        both = added(both, by_batch(both, step))
        qkv, vec = both[:-16], both[-16:]
        step *= 2
    qkv = join(qkv, by_batch(qkv, 1), x_bit)
    qkv = join(qkv, by_y(qkv), y_bit)
    qkv = join(qkv, by_core(qkv), core)

    half = big.shape[0] // 2
    place = [0]

    def take(source, count, split_at):
        at = place[0]
        place[0] = at + count // 2
        return high(
            jnp.concatenate(
                [source[at : at + count // 2], source[split_at + at : split_at + at + count // 2]],
                axis=0,
            )
        )

    ens2 = jnp.concatenate([take(big, FF, half), take(big, D, half)], axis=0)
    up = jnp.concatenate([take(big, D, half) for _ in range(FF // D)], axis=1)
    ens1 = jnp.concatenate([take(big, D, half) for _ in range(4)], axis=0)
    attn_out = take(big, D, half)
    cross = take(big, D, half)
    mix = take(big, D, half)
    place[0] = 0
    query, key, value = [take(qkv, D, 3 * third) for _ in range(3)]
    vec = high(vec)
    return (
        out_rows, grad_tokens, vec[6], query, key, value, attn_out, cross, vec[4], mix, ens1, vec[5],
        up, vec[:4].reshape(FF), ens2,
    )


def solution(mesh):
    rows = P(("batch", "module"), None)
    in_specs = (rows, P("batch", None), P("batch"), rows) + (P(),) * 13
    out_specs = (rows, rows) + (P(),) * 13
    body = functools.partial(shards, mesh.shape["batch"], mesh.shape["module"])
    return jax.shard_map(body, mesh=mesh, in_specs=in_specs, out_specs=out_specs, check_vma=False)
```

profile of v0, /device:TPU:0, one launch (start us, length us, event | category | flops | bytes accessed | tf_op | source)
XLA Modules:
  0.0 133.5 jit_solution(15679694015287213657)
XLA Ops:
  0.6 3.0 %collective-permute-start.1 = (bf16[512,256]{1,0:T(8,128)(2,1)}, bf16[512,256]{1,0:T(8,128)(2,1)S(1)}, u32[]{:S(2)}, u32[]{:S(2)}) collective-permute-start(bf16[512,256]{1,0:T(8,128)(2,1)} %tokens.1), channel_id=1, source_target_pairs={{0,2},{1,3},{2,0},{3,1},{4,6},{5,7},{6,4},{7,5},{8,10},{9,11},{10,... | collective-permute-start | bytes 786440 | tf_op jit(solution)/shard_map/ppermute | solution.py:366
  3.7 6.5 %collective-permute-done.1.t2 = bf16[512,256]{1,0:T(8,128)(2,1)S(1)} collective-permute-done((bf16[512,256]{1,0:T(8,128)(2,1)}, bf16[512,256]{1,0:T(8,128)(2,1)S(1)}, u32[]{:S(2)}, u32[]{:S(2)}) %collective-permute-start.1) | collective-permute-done | bytes 262176 | tf_op jit(solution)/shard_map/ppermute | solution.py:366
  24.0 19.4 %shard_map.281 = (f32[512,256]{1,0:T(8,128)}, f32[512,256]{1,0:T(8,128)S(1)}, f32[512,256]{1,0:T(8,128)S(1)}, bf16[4096,256]{1,0:T(8,128)(2,1)}, f32[16,256]{1,0...) custom-call(s32[1]{0:T(128)} %bitcast.me_ref, ...), custom_call_target="tpu_custom_call" | custom-call | bytes 1048576 | tf_op jit(solution)/shard_map/pallas_call | solution.py:439
  45.9 17.1 %shard_map.282 = (bf16[1424,256]{1,0:T(8,128)(2,1)S(1)}, bf16[1424,256]{1,0:T(8,128)(2,1)S(1)}) custom-call(s32[1]{0:T(128)} %bitcast.me_ref, s32[1,8]{1,0:T(1,128)S(1)} %copy-done.18, bf16[2048,256]{1,0:T(8,128)(2,1)S(1)} %copy-done.2, bf16[512,512]{1,0:T(8,128)(2,1)S(1)} %get-tuple-element.47.q_aug, bf16[2048,512]{1,0:T(8,128)(2,1)} %get-tuple-element.48.k_aug, ...), custom_call_target="tpu_custom_call" | custom-call | bytes 1048576 | tf_op jit(solution)/shard_map/pallas_call | solution.py:493
  67.2 1.8 %collective-permute-start.4 = (bf16[720,256]{1,0:T(8,128)(2,1)S(1)}, bf16[720,256]{1,0:T(8,128)(2,1)S(1)}, u32[]{:S(2)}, u32[]{:S(2)}) collective-permute-start(bf16[720,256]{1,0:T(8,128)(2,1)S(1)} %pad_maximum_fusion.1), channel_id=1, source_target_pairs={{0,2},{1,3},{2,0},{3,1},{4,6},{5,7},{6,4},{7,5},{8,10},{9,11},{10,... | collective-permute-start | bytes 1105928 | tf_op jit(solution)/shard_map/ppermute | solution.py:366
  69.0 1.6 %add_convert_fusion = bf16[2048,256]{1,0:T(8,128)(2,1)S(1)} fusion(bf16[2048,256]{1,0:T(8,128)(2,1)} %collective-permute-done.11, bf16[4096,256]{1,0:T(8,128)(2,1)S(1)} %copy-done.21, s32[]{:T(128)S(6)} %select_n.128), kind=kLoop, calls=%fused_computation.1 | loop fusion | flops 2097152 | bytes 3145732 | tf_op jit(solution)/shard_map/convert_element_type | solution.py:24
  71.2 1.6 %collective-permute-start.14 = (bf16[512,256]{1,0:T(8,128)(2,1)S(1)}, bf16[512,256]{1,0:T(8,128)(2,1)S(1)}, u32[]{:S(2)}, u32[]{:S(2)}) collective-permute-start(bf16[512,256]{1,0:T(8,128)(2,1)S(1)} %constant_dynamic-slice_fusion.1), channel_id=1, source_target_pairs={{0,4},{4,0},{8,12},{12,8},{16,20},{20,16},{24,28},{28,24},{1,5},{5... | collective-permute-start | bytes 786440 | tf_op jit(solution)/shard_map/ppermute | solution.py:366
  72.8 5.8 %collective-permute-done.4 = bf16[720,256]{1,0:T(8,128)(2,1)S(1)} collective-permute-done((bf16[720,256]{1,0:T(8,128)(2,1)S(1)}, bf16[720,256]{1,0:T(8,128)(2,1)S(1)}, u32[]{:S(2)}, u32[]{:S(2)}) %collective-permute-start.4) | collective-permute-done | bytes 368672 | tf_op jit(solution)/shard_map/ppermute | solution.py:366
  78.7 1.8 %collective-permute-start.5 = (bf16[112,256]{1,0:T(8,128)(2,1)S(1)}, bf16[112,256]{1,0:T(8,128)(2,1)S(1)}, u32[]{:S(2)}, u32[]{:S(2)}) collective-permute-start(bf16[112,256]{1,0:T(8,128)(2,1)S(1)} %pad_maximum_fusion.2), channel_id=1, source_target_pairs={{0,4},{4,0},{8,12},{12,8},{16,20},{20,16},{24,28},{28,24},{1,5},{5... | collective-permute-start | bytes 172040 | tf_op jit(solution)/shard_map/ppermute | solution.py:366
  81.8 2.0 %collective-permute-done.12 = bf16[512,256]{1,0:T(8,128)(2,1)S(1)} collective-permute-done((bf16[512,256]{1,0:T(8,128)(2,1)S(1)}, bf16[512,256]{1,0:T(8,128)(2,1)S(1)}, u32[]{:S(2)}, u32[]{:S(2)}) %collective-permute-start.12) | collective-permute-done | bytes 262176 | tf_op jit(solution)/shard_map/ppermute | solution.py:366
  83.8 1.8 %collective-permute-start.13 = (bf16[256,256]{1,0:T(8,128)(2,1)S(1)}, bf16[256,256]{1,0:T(8,128)(2,1)S(1)}, u32[]{:S(2)}, u32[]{:S(2)}) collective-permute-start(bf16[256,256]{1,0:T(8,128)(2,1)S(1)} %constant_dynamic-slice_fusion.2), channel_id=1, source_target_pairs={{0,4},{4,0},{8,12},{12,8},{16,20},{20,16},{24,28},{28,24},{1,5},{5... | collective-permute-start | bytes 393224 | tf_op jit(solution)/shard_map/ppermute | solution.py:366
  85.7 1.6 %collective-permute-start.15 = (bf16[256,256]{1,0:T(8,128)(2,1)S(1)}, bf16[256,256]{1,0:T(8,128)(2,1)S(1)}, u32[]{:S(2)}, u32[]{:S(2)}) collective-permute-start(bf16[256,256]{1,0:T(8,128)(2,1)S(1)} %constant_dynamic-slice_fusion), channel_id=1, source_target_pairs={{0,2},{1,3},{2,0},{3,1},{4,6},{5,7},{6,4},{7,5},{8,10},{9,11},{10,... | collective-permute-start | bytes 393224 | tf_op jit(solution)/shard_map/ppermute | solution.py:366
  87.3 1.6 %collective-permute-done.13 = bf16[256,256]{1,0:T(8,128)(2,1)S(1)} collective-permute-done((bf16[256,256]{1,0:T(8,128)(2,1)S(1)}, bf16[256,256]{1,0:T(8,128)(2,1)S(1)}, u32[]{:S(2)}, u32[]{:S(2)}) %collective-permute-start.13) | collective-permute-done | bytes 131104 | tf_op jit(solution)/shard_map/ppermute | solution.py:366
  88.9 1.8 %collective-permute-done.15 = bf16[256,256]{1,0:T(8,128)(2,1)S(1)} collective-permute-done((bf16[256,256]{1,0:T(8,128)(2,1)S(1)}, bf16[256,256]{1,0:T(8,128)(2,1)S(1)}, u32[]{:S(2)}, u32[]{:S(2)}) %collective-permute-start.15) | collective-permute-done | bytes 131104 | tf_op jit(solution)/shard_map/ppermute | solution.py:366
  91.1 1.6 %collective-permute-start.16 = (bf16[256,256]{1,0:T(8,128)(2,1)S(1)}, bf16[256,256]{1,0:T(8,128)(2,1)S(1)}, u32[]{:S(2)}, u32[]{:S(2)}) collective-permute-start(bf16[256,256]{1,0:T(8,128)(2,1)S(1)} %fusion), channel_id=1, source_target_pairs={{0,8},{4,12},{8,0},{12,4},{16,24},{20,28},{24,16},{28,20},{1,9},{5... | collective-permute-start | bytes 393224 | tf_op jit(solution)/shard_map/ppermute | solution.py:366
  92.7 3.4 %collective-permute-done.16 = bf16[256,256]{1,0:T(8,128)(2,1)S(1)} collective-permute-done((bf16[256,256]{1,0:T(8,128)(2,1)S(1)}, bf16[256,256]{1,0:T(8,128)(2,1)S(1)}, u32[]{:S(2)}, u32[]{:S(2)}) %collective-permute-start.16) | collective-permute-done | bytes 131104 | tf_op jit(solution)/shard_map/ppermute | solution.py:366
  96.4 2.7 %collective-permute-start.17 = (bf16[256,256]{1,0:T(8,128)(2,1)S(1)}, bf16[256,256]{1,0:T(8,128)(2,1)S(1)}, u32[]{:S(2)}, u32[]{:S(2)}) collective-permute-start(bf16[256,256]{1,0:T(8,128)(2,1)S(1)} %add_convert_fusion.5), channel_id=1, source_target_pairs={{0,16},{4,20},{8,24},{12,28},{16,0},{20,4},{24,8},{28,12},{1,17},{... | collective-permute-start | bytes 393224 | tf_op jit(solution)/shard_map/ppermute | solution.py:366
  99.1 1.6 %collective-permute-start.6 = (bf16[112,256]{1,0:T(8,128)(2,1)S(1)}, bf16[112,256]{1,0:T(8,128)(2,1)S(1)}, u32[]{:S(2)}, u32[]{:S(2)}) collective-permute-start(bf16[112,256]{1,0:T(8,128)(2,1)S(1)} %pad_maximum_fusion.3), channel_id=1, source_target_pairs={{0,8},{4,12},{8,0},{12,4},{16,24},{20,28},{24,16},{28,20},{1,9},{5... | collective-permute-start | bytes 172040 | tf_op jit(solution)/shard_map/ppermute | solution.py:366
  100.7 3.1 %collective-permute-done.17 = bf16[256,256]{1,0:T(8,128)(2,1)S(1)} collective-permute-done((bf16[256,256]{1,0:T(8,128)(2,1)S(1)}, bf16[256,256]{1,0:T(8,128)(2,1)S(1)}, u32[]{:S(2)}, u32[]{:S(2)}) %collective-permute-start.17) | collective-permute-done | bytes 131104 | tf_op jit(solution)/shard_map/ppermute | solution.py:366
  104.6 3.5 %collective-permute-start.7 = (bf16[112,256]{1,0:T(8,128)(2,1)S(1)}, bf16[112,256]{1,0:T(8,128)(2,1)S(1)}, u32[]{:S(2)}, u32[]{:S(2)}) collective-permute-start(bf16[112,256]{1,0:T(8,128)(2,1)S(1)} %add_convert_fusion.10), channel_id=1, source_target_pairs={{0,16},{4,20},{8,24},{12,28},{16,0},{20,4},{24,8},{28,12},{1,17},{... | collective-permute-start | bytes 172040 | tf_op jit(solution)/shard_map/ppermute | solution.py:366
  109.1 1.6 %collective-permute-start.21 = (bf16[256,256]{1,0:T(8,128)(2,1)S(1)}, bf16[256,256]{1,0:T(8,128)(2,1)S(1)}, u32[]{:S(2)}, u32[]{:S(2)}) collective-permute-start(bf16[256,256]{1,0:T(8,128)(2,1)S(1)} %get-tuple-element.93), channel_id=1, source_target_pairs={{0,2},{1,3},{2,0},{3,1},{4,6},{5,7},{6,4},{7,5},{8,10},{9,11},{10,... | collective-permute-start | bytes 393224 | tf_op jit(solution)/shard_map/ppermute | solution.py:366
  111.2 1.6 %collective-permute-start.8 = (bf16[96,256]{1,0:T(8,128)(2,1)S(1)}, bf16[96,256]{1,0:T(8,128)(2,1)S(1)}, u32[]{:S(2)}, u32[]{:S(2)}) collective-permute-start(bf16[96,256]{1,0:T(8,128)(2,1)S(1)} %slice.218), channel_id=1, source_target_pairs={{0,4},{4,0},{8,12},{12,8},{16,20},{20,16},{24,28},{28,24},{1,5},{5... | collective-permute-start | bytes 147464 | tf_op jit(solution)/shard_map/ppermute | solution.py:366
  112.8 2.1 %collective-permute-done.21 = bf16[256,256]{1,0:T(8,128)(2,1)S(1)} collective-permute-done((bf16[256,256]{1,0:T(8,128)(2,1)S(1)}, bf16[256,256]{1,0:T(8,128)(2,1)S(1)}, u32[]{:S(2)}, u32[]{:S(2)}) %collective-permute-start.21) | collective-permute-done | bytes 131104 | tf_op jit(solution)/shard_map/ppermute | solution.py:366
  118.6 2.9 %collective-permute-done.22 = bf16[512,256]{1,0:T(8,128)(2,1)S(1)} collective-permute-done((bf16[512,256]{1,0:T(8,128)(2,1)S(1)}, bf16[512,256]{1,0:T(8,128)(2,1)S(1)}, u32[]{:S(2)}, u32[]{:S(2)}) %collective-permute-start.22) | collective-permute-done | bytes 262176 | tf_op jit(solution)/shard_map/ppermute | solution.py:366
  (135 shorter events, 41.0 us)
Async XLA Ops:
  0.6 9.6 %collective-permute-start.1 = (bf16[512,256]{1,0:T(8,128)(2,1)}, bf16[512,256]{1,0:T(8,128)(2,1)S(1)}, u32[]{:S(2)}, u32[]{:S(2)}) collective-permute-start(bf16[512,256]{1,0:T(8,128)(2,1)} %tokens.1), channel_id=1, source_target_pairs={{0,2},{1,3},{2,0},{3,1},{4,6},{5,7},{6,4},{7,5},{8,10},{9,11},{10,... | collective-permute-start | bytes 786440 | tf_op jit(solution)/shard_map/ppermute | solution.py:366
  3.7 10.4 %collective-permute-start = (bf16[512,256]{1,0:T(8,128)(2,1)}, bf16[512,256]{1,0:T(8,128)(2,1)S(1)}, u32[]{:S(2)}, u32[]{:S(2)}) collective-permute-start(bf16[512,256]{1,0:T(8,128)(2,1)} %tokens.1), channel_id=1, source_target_pairs={{0,1},{1,0},{2,3},{3,2},{4,5},{5,4},{6,7},{7,6},{8,9},{9,8},{10,11... | collective-permute-start | bytes 786440 | tf_op jit(solution)/shard_map/ppermute | solution.py:366
  10.2 3.9 %collective-permute-start.2 = (bf16[512,256]{1,0:T(8,128)(2,1)S(1)}, bf16[512,256]{1,0:T(8,128)(2,1)S(1)}, u32[]{:S(2)}, u32[]{:S(2)}) collective-permute-start(bf16[512,256]{1,0:T(8,128)(2,1)S(1)} %collective-permute-done.1.t2), channel_id=1, source_target_pairs={{0,1},{1,0},{2,3},{3,2},{4,5},{5,4},{6,7},{7,6},{8,9},{9,8},{10,11... | collective-permute-start | bytes 786440 | tf_op jit(solution)/shard_map/ppermute | solution.py:366
  63.0 2.6 %collective-permute-start.3 = (bf16[1424,256]{1,0:T(8,128)(2,1)S(1)}, bf16[1424,256]{1,0:T(8,128)(2,1)}, u32[]{:S(2)}, u32[]{:S(2)}) collective-permute-start(bf16[1424,256]{1,0:T(8,128)(2,1)S(1)} %get-tuple-element.60), channel_id=1, source_target_pairs={{0,1},{1,0},{2,3},{3,2},{4,5},{5,4},{6,7},{7,6},{8,9},{9,8},{10,11... | collective-permute-start | bytes 2187272 | tf_op jit(solution)/shard_map/ppermute | solution.py:366
  64.9 4.1 %collective-permute-start.11 = (bf16[2048,256]{1,0:T(8,128)(2,1)S(1)}, bf16[2048,256]{1,0:T(8,128)(2,1)}, u32[]{:S(2)}, u32[]{:S(2)}) collective-permute-start(bf16[2048,256]{1,0:T(8,128)(2,1)S(1)} %constant_dynamic-slice_fusion.4), channel_id=1, source_target_pairs={{0,1},{1,0},{2,3},{3,2},{4,5},{5,4},{6,7},{7,6},{8,9},{9,8},{10,11... | collective-permute-start | bytes 3145736 | tf_op jit(solution)/shard_map/ppermute | solution.py:366
  67.2 11.5 %collective-permute-start.4 = (bf16[720,256]{1,0:T(8,128)(2,1)S(1)}, bf16[720,256]{1,0:T(8,128)(2,1)S(1)}, u32[]{:S(2)}, u32[]{:S(2)}) collective-permute-start(bf16[720,256]{1,0:T(8,128)(2,1)S(1)} %pad_maximum_fusion.1), channel_id=1, source_target_pairs={{0,2},{1,3},{2,0},{3,1},{4,6},{5,7},{6,4},{7,5},{8,10},{9,11},{10,... | collective-permute-start | bytes 1105928 | tf_op jit(solution)/shard_map/ppermute | solution.py:366
  70.7 13.1 %collective-permute-start.12 = (bf16[512,256]{1,0:T(8,128)(2,1)S(1)}, bf16[512,256]{1,0:T(8,128)(2,1)S(1)}, u32[]{:S(2)}, u32[]{:S(2)}) collective-permute-start(bf16[512,256]{1,0:T(8,128)(2,1)S(1)} %constant_dynamic-slice_fusion.3), channel_id=1, source_target_pairs={{0,2},{1,3},{2,0},{3,1},{4,6},{5,7},{6,4},{7,5},{8,10},{9,11},{10,... | collective-permute-start | bytes 786440 | tf_op jit(solution)/shard_map/ppermute | solution.py:366
  71.2 14.4 %collective-permute-start.14 = (bf16[512,256]{1,0:T(8,128)(2,1)S(1)}, bf16[512,256]{1,0:T(8,128)(2,1)S(1)}, u32[]{:S(2)}, u32[]{:S(2)}) collective-permute-start(bf16[512,256]{1,0:T(8,128)(2,1)S(1)} %constant_dynamic-slice_fusion.1), channel_id=1, source_target_pairs={{0,4},{4,0},{8,12},{12,8},{16,20},{20,16},{24,28},{28,24},{1,5},{5... | collective-permute-start | bytes 786440 | tf_op jit(solution)/shard_map/ppermute | solution.py:366
  78.7 14.0 %collective-permute-start.5 = (bf16[112,256]{1,0:T(8,128)(2,1)S(1)}, bf16[112,256]{1,0:T(8,128)(2,1)S(1)}, u32[]{:S(2)}, u32[]{:S(2)}) collective-permute-start(bf16[112,256]{1,0:T(8,128)(2,1)S(1)} %pad_maximum_fusion.2), channel_id=1, source_target_pairs={{0,4},{4,0},{8,12},{12,8},{16,20},{20,16},{24,28},{28,24},{1,5},{5... | collective-permute-start | bytes 172040 | tf_op jit(solution)/shard_map/ppermute | solution.py:366
  83.8 5.0 %collective-permute-start.13 = (bf16[256,256]{1,0:T(8,128)(2,1)S(1)}, bf16[256,256]{1,0:T(8,128)(2,1)S(1)}, u32[]{:S(2)}, u32[]{:S(2)}) collective-permute-start(bf16[256,256]{1,0:T(8,128)(2,1)S(1)} %constant_dynamic-slice_fusion.2), channel_id=1, source_target_pairs={{0,4},{4,0},{8,12},{12,8},{16,20},{20,16},{24,28},{28,24},{1,5},{5... | collective-permute-start | bytes 393224 | tf_op jit(solution)/shard_map/ppermute | solution.py:366
  85.7 5.0 %collective-permute-start.15 = (bf16[256,256]{1,0:T(8,128)(2,1)S(1)}, bf16[256,256]{1,0:T(8,128)(2,1)S(1)}, u32[]{:S(2)}, u32[]{:S(2)}) collective-permute-start(bf16[256,256]{1,0:T(8,128)(2,1)S(1)} %constant_dynamic-slice_fusion), channel_id=1, source_target_pairs={{0,2},{1,3},{2,0},{3,1},{4,6},{5,7},{6,4},{7,5},{8,10},{9,11},{10,... | collective-permute-start | bytes 393224 | tf_op jit(solution)/shard_map/ppermute | solution.py:366
  91.1 5.0 %collective-permute-start.16 = (bf16[256,256]{1,0:T(8,128)(2,1)S(1)}, bf16[256,256]{1,0:T(8,128)(2,1)S(1)}, u32[]{:S(2)}, u32[]{:S(2)}) collective-permute-start(bf16[256,256]{1,0:T(8,128)(2,1)S(1)} %fusion), channel_id=1, source_target_pairs={{0,8},{4,12},{8,0},{12,4},{16,24},{20,28},{24,16},{28,20},{1,9},{5... | collective-permute-start | bytes 393224 | tf_op jit(solution)/shard_map/ppermute | solution.py:366
  96.4 7.4 %collective-permute-start.17 = (bf16[256,256]{1,0:T(8,128)(2,1)S(1)}, bf16[256,256]{1,0:T(8,128)(2,1)S(1)}, u32[]{:S(2)}, u32[]{:S(2)}) collective-permute-start(bf16[256,256]{1,0:T(8,128)(2,1)S(1)} %add_convert_fusion.5), channel_id=1, source_target_pairs={{0,16},{4,20},{8,24},{12,28},{16,0},{20,4},{24,8},{28,12},{1,17},{... | collective-permute-start | bytes 393224 | tf_op jit(solution)/shard_map/ppermute | solution.py:366
  99.1 5.5 %collective-permute-start.6 = (bf16[112,256]{1,0:T(8,128)(2,1)S(1)}, bf16[112,256]{1,0:T(8,128)(2,1)S(1)}, u32[]{:S(2)}, u32[]{:S(2)}) collective-permute-start(bf16[112,256]{1,0:T(8,128)(2,1)S(1)} %pad_maximum_fusion.3), channel_id=1, source_target_pairs={{0,8},{4,12},{8,0},{12,4},{16,24},{20,28},{24,16},{28,20},{1,9},{5... | collective-permute-start | bytes 172040 | tf_op jit(solution)/shard_map/ppermute | solution.py:366
  103.9 5.0 %collective-permute-start.18 = (bf16[256,256]{1,0:T(8,128)(2,1)S(1)}, bf16[256,256]{1,0:T(8,128)(2,1)S(1)}, u32[]{:S(2)}, u32[]{:S(2)}) collective-permute-start(bf16[256,256]{1,0:T(8,128)(2,1)S(1)} %add_convert_fusion.4), channel_id=1, source_target_pairs={{0,8},{4,12},{8,0},{12,4},{16,24},{20,28},{24,16},{28,20},{1,9},{5... | collective-permute-start | bytes 393224 | tf_op jit(solution)/shard_map/ppermute | solution.py:366
  104.6 6.5 %collective-permute-start.7 = (bf16[112,256]{1,0:T(8,128)(2,1)S(1)}, bf16[112,256]{1,0:T(8,128)(2,1)S(1)}, u32[]{:S(2)}, u32[]{:S(2)}) collective-permute-start(bf16[112,256]{1,0:T(8,128)(2,1)S(1)} %add_convert_fusion.10), channel_id=1, source_target_pairs={{0,16},{4,20},{8,24},{12,28},{16,0},{20,4},{24,8},{28,12},{1,17},{... | collective-permute-start | bytes 172040 | tf_op jit(solution)/shard_map/ppermute | solution.py:366
  109.1 5.8 %collective-permute-start.21 = (bf16[256,256]{1,0:T(8,128)(2,1)S(1)}, bf16[256,256]{1,0:T(8,128)(2,1)S(1)}, u32[]{:S(2)}, u32[]{:S(2)}) collective-permute-start(bf16[256,256]{1,0:T(8,128)(2,1)S(1)} %get-tuple-element.93), channel_id=1, source_target_pairs={{0,2},{1,3},{2,0},{3,1},{4,6},{5,7},{6,4},{7,5},{8,10},{9,11},{10,... | collective-permute-start | bytes 393224 | tf_op jit(solution)/shard_map/ppermute | solution.py:366
  110.6 5.6 %collective-permute-start.19 = (bf16[256,256]{1,0:T(8,128)(2,1)S(1)}, bf16[256,256]{1,0:T(8,128)(2,1)S(1)}, u32[]{:S(2)}, u32[]{:S(2)}) collective-permute-start(bf16[256,256]{1,0:T(8,128)(2,1)S(1)} %get-tuple-element.92), channel_id=1, source_target_pairs={{0,4},{4,0},{8,12},{12,8},{16,20},{20,16},{24,28},{28,24},{1,5},{5... | collective-permute-start | bytes 393224 | tf_op jit(solution)/shard_map/ppermute | solution.py:366
  111.2 6.5 %collective-permute-start.8 = (bf16[96,256]{1,0:T(8,128)(2,1)S(1)}, bf16[96,256]{1,0:T(8,128)(2,1)S(1)}, u32[]{:S(2)}, u32[]{:S(2)}) collective-permute-start(bf16[96,256]{1,0:T(8,128)(2,1)S(1)} %slice.218), channel_id=1, source_target_pairs={{0,4},{4,0},{8,12},{12,8},{16,20},{20,16},{24,28},{28,24},{1,5},{5... | collective-permute-start | bytes 147464 | tf_op jit(solution)/shard_map/ppermute | solution.py:366
  115.0 6.4 %collective-permute-start.22 = (bf16[512,256]{1,0:T(8,128)(2,1)S(1)}, bf16[512,256]{1,0:T(8,128)(2,1)S(1)}, u32[]{:S(2)}, u32[]{:S(2)}) collective-permute-start(bf16[512,256]{1,0:T(8,128)(2,1)S(1)} %maximum_select_fusion.6), channel_id=1, source_target_pairs={{0,4},{4,0},{8,12},{12,8},{16,20},{20,16},{24,28},{28,24},{1,5},{5... | collective-permute-start | bytes 786440 | tf_op jit(solution)/shard_map/ppermute | solution.py:366
  116.4 6.4 %collective-permute-start.20 = (bf16[512,256]{1,0:T(8,128)(2,1)S(1)}, bf16[512,256]{1,0:T(8,128)(2,1)S(1)}, u32[]{:S(2)}, u32[]{:S(2)}) collective-permute-start(bf16[512,256]{1,0:T(8,128)(2,1)S(1)} %maximum_select_fusion.5), channel_id=1, source_target_pairs={{0,2},{1,3},{2,0},{3,1},{4,6},{5,7},{6,4},{7,5},{8,10},{9,11},{10,... | collective-permute-start | bytes 786440 | tf_op jit(solution)/shard_map/ppermute | solution.py:366
  117.7 6.1 %collective-permute-start.9 = (bf16[192,256]{1,0:T(8,128)(2,1)S(1)}, bf16[192,256]{1,0:T(8,128)(2,1)S(1)}, u32[]{:S(2)}, u32[]{:S(2)}) collective-permute-start(bf16[192,256]{1,0:T(8,128)(2,1)S(1)} %maximum_select_fusion.8), channel_id=1, source_target_pairs={{0,2},{1,3},{2,0},{3,1},{4,6},{5,7},{6,4},{7,5},{8,10},{9,11},{10,... | collective-permute-start | bytes 294920 | tf_op jit(solution)/shard_map/ppermute | solution.py:366
  123.1 4.8 %collective-permute-start.23 = (bf16[2048,256]{1,0:T(8,128)(2,1)S(1)}, bf16[2048,256]{1,0:T(8,128)(2,1)S(1)}, u32[]{:S(2)}, u32[]{:S(2)}) collective-permute-start(bf16[2048,256]{1,0:T(8,128)(2,1)S(1)} %pad_maximum_fusion), channel_id=1, source_target_pairs={{0,1},{1,0},{2,3},{3,2},{4,5},{5,4},{6,7},{7,6},{8,9},{9,8},{10,11... | collective-permute-start | bytes 3145736 | tf_op jit(solution)/shard_map/ppermute | solution.py:366
  123.9 2.2 %collective-permute-start.10 = (bf16[384,256]{1,0:T(8,128)(2,1)S(1)}, bf16[384,256]{1,0:T(8,128)(2,1)S(1)}, u32[]{:S(2)}, u32[]{:S(2)}) collective-permute-start(bf16[384,256]{1,0:T(8,128)(2,1)S(1)} %maximum_select_fusion.7), channel_id=1, source_target_pairs={{0,1},{1,0},{2,3},{3,2},{4,5},{5,4},{6,7},{7,6},{8,9},{9,8},{10,11... | collective-permute-start | bytes 589832 | tf_op jit(solution)/shard_map/ppermute | solution.py:366
  (22 other events, 68.2 us)
where the time goes:
time: 134 us
  Pallas kernels  38 us (28%)
  waiting for transfers between devices  34 us (25%)
  starting transfers between devices  29.5 us (22%)
  local copies, waits for them, and re-layouts  18.9 us (14%)
  other arithmetic  12.1 us (9%)
    ppermute x24, waiting for transfers between devices, swap(): return lax.ppermute(value, axis, [(i, i ^ step) for i in range(count)])  34 us
    ppermute x24, starting transfers between devices, swap(): return lax.ppermute(value, axis, [(i, i ^ step) for i in range(count)])  29.5 us
    pallas_call x1, Pallas kernels, shards(): call(functools.partial(forward_kernel, own_rows, rows, chunk), [((own_row...  19.4 us
    pallas_call x1, Pallas kernels, shards(): call(functools.partial(backward_kernel, own_rows, rows, chunk), [((small,...  17.1 us
    unnamed x53, local copies, waits for them, and re-layouts  16.6 us
    convert_element_type x14, other arithmetic, low(): return v.astype(BF)  3.68 us
    convert_element_type x5, other arithmetic, high(): return v.astype(F32)  3.09 us
  transfers between devices with their start and end apart: 24, of which 15 were waited for; matrix products, arithmetic and copies ran while one was open for 7% of the time, Pallas kernels for 1%

commit v1 on v0

v1 whole, which is shorter than its diff:
```python
import functools

import jax
import jax.numpy as jnp
from jax import lax
from jax.experimental import pallas as pl
from jax.experimental.pallas import tpu as pltpu
from jax.sharding import PartitionSpec as P

D = 256
HEADS = 4
HEAD_DIM = 64
FF = 1024
SEGS = 8
LANES = 128
WIDE = HEADS * LANES
HUGE = -1e30
BF = jnp.bfloat16
F32 = jnp.float32
MIB = 1024 * 1024


def low(v):
    return v.astype(BF)


def high(v):
    return v.astype(F32)


def dot(a, b):
    return jnp.dot(a, b, preferred_element_type=F32)


def dot_nt(a, b):
    return lax.dot_general(a, b, (((1,), (1,)), ((), ())), preferred_element_type=F32)


def dot_tn(a, b):
    return lax.dot_general(a, b, (((0,), (0,)), ((), ())), preferred_element_type=F32)


def head_sums(selector, product):
    upper = low(product)
    lower = low(product - high(upper))
    return dot_nt(selector, upper) + dot_nt(selector, lower)


def unit_rows(values):
    center = values - jnp.mean(values, axis=1, keepdims=True)
    scale = lax.rsqrt(jnp.mean(center * center, axis=1, keepdims=True) + 1e-05)
    return center * scale, scale


def norm_back(grad, unit, scale, gain):
    scaled = grad * gain
    first_mean = jnp.mean(scaled, axis=1, keepdims=True)
    second_mean = jnp.mean(scaled * unit, axis=1, keepdims=True)
    return scale * (scaled - first_mean - unit * second_mean)


def call(body, outs, scratch, places, limit, microseconds):
    spaces = {"s": pltpu.SMEM, "v": pltpu.VMEM, "h": pltpu.HBM}
    return pl.pallas_call(
        body,
        out_shape=[jax.ShapeDtypeStruct(shape, kind) for shape, kind in outs],
        in_specs=[pl.BlockSpec(memory_space=spaces[place]) for place in places],
        out_specs=[pl.BlockSpec(memory_space=pltpu.VMEM)] * len(outs),
        scratch_shapes=list(scratch),
        compiler_params=pltpu.CompilerParams(vmem_limit_bytes=limit * MIB),
        cost_estimate=pl.CostEstimate(
            flops=microseconds * 10**9, bytes_accessed=1 * MIB, transcendentals=0
        ),
    )


def widen(weight):
    rows = weight.shape[0]
    gap = jnp.zeros((rows, LANES - HEAD_DIM), weight.dtype)
    pieces = []
    for head in range(HEADS):
        pieces += [weight[:, head * HEAD_DIM : (head + 1) * HEAD_DIM], gap]
    return jnp.concatenate(pieces, axis=1)


def widen_rows(weight):
    gap = jnp.zeros((LANES - HEAD_DIM, weight.shape[1]), weight.dtype)
    pieces = []
    for head in range(HEADS):
        pieces += [weight[head * HEAD_DIM : (head + 1) * HEAD_DIM], gap]
    return jnp.concatenate(pieces, axis=0)


def narrow(wide):
    return jnp.concatenate(
        [wide[:, h * LANES : h * LANES + HEAD_DIM] for h in range(HEADS)], axis=1
    )


def narrow_rows(wide):
    return jnp.concatenate([wide[h * LANES : h * LANES + HEAD_DIM] for h in range(HEADS)], axis=0)


def segment_rows(seg_ref, first_place, count):
    spread = lax.broadcasted_iota(jnp.int32, (16, count), 0)
    places = lax.broadcasted_iota(jnp.int32, (16, count), 1) + first_place
    begin = jnp.zeros((16, count), jnp.int32)
    end = jnp.zeros((16, count), jnp.int32)
    edge = jnp.int32(0)
    for j in range(SEGS):
        begin = jnp.where(spread == j, edge, begin)
        edge = edge + seg_ref[0, j]
        end = jnp.where(spread == j, edge, end)
    return spread, (places >= begin) & (places < end)


def head_selector():
    rows = lax.broadcasted_iota(jnp.int32, (16, WIDE), 0)
    lanes = lax.broadcasted_iota(jnp.int32, (16, WIDE), 1)
    return low(jnp.where((lanes >> 7) == rows, 1.0, 0.0))


def start_kernel(me_ref, token):
    token[...] = jnp.zeros_like(token)


def project(rows_in, gain, code, wk_pad, wv_pad, wk_t, wv_t, at, normed, normed_t, k_aug, v_pad, kt, vt):
    count = rows_in.shape[0]
    unit, _ = unit_rows(high(rows_in))
    value = low(unit * gain)
    flipped = value.T
    normed[at : at + count, :] = value
    normed_t[:, at : at + count] = flipped
    wide = low(dot(value, wk_pad))
    k_aug[at : at + count, :] = wide + jnp.concatenate([code] * HEADS, axis=1)
    v_pad[at : at + count, :] = low(dot(value, wv_pad))
    kt[:, at : at + count] = low(dot(wk_t, flipped))
    vt[:, at : at + count] = low(dot(wv_t, flipped))


def lane_codes(rows_code):
    picked = lax.broadcasted_iota(jnp.int32, (16, LANES), 1) - HEAD_DIM
    picked = (picked == lax.broadcasted_iota(jnp.int32, (16, LANES), 0)) & (picked <= SEGS)
    return low(dot_tn(low(rows_code), low(jnp.where(picked, 1.0, 0.0))))


def first_kernel(
    own_rows,
    me_ref, seg, token, core_rows, tokens, valid, gain_one, wq, wk, wv, wo,
    wq_pad, wk_pad, wv_pad, wo_pad, wk_t, wv_t, codes, real, counted,
    normed, normed_t, q_aug, k_aug, v_pad, kt, vt,
):
    me = me_ref[0]
    for step in range(4):
        at = pl.multiple_of((me ^ step) * own_rows, own_rows)
        spread, inside = segment_rows(seg, at, own_rows)
        ok = valid[:, pl.ds(at, own_rows)] > 0
        code = jnp.where(inside, HUGE, 0.0)
        code = jnp.where(spread == SEGS, jnp.where(ok, 0.0, HUGE), code)
        codes[step * own_rows : (step + 1) * own_rows, :] = lane_codes(code)
        real[:, step * own_rows : (step + 1) * own_rows] = jnp.where(ok, 1.0, 0.0)
        counted[:, step * own_rows : (step + 1) * own_rows] = low(jnp.where(inside & ok, 1.0, 0.0))
    wq_pad[...] = low(widen(high(wq[...])))
    wk_pad[...] = low(widen(high(wk[...])))
    wv_pad[...] = low(widen(high(wv[...])))
    wo_pad[...] = low(widen_rows(high(wo[...])))
    wk_t[...] = wk[...].T
    wv_t[...] = wv[...].T
    gain = gain_one[...]
    for step, rows_in in enumerate((tokens, core_rows)):
        at = step * own_rows
        project(
            rows_in[...], gain, codes[at : at + own_rows, :], wk_pad[...], wv_pad[...], wk_t[...], wv_t[...], at,
            normed, normed_t, k_aug, v_pad, kt, vt,
        )
    spread, inside = segment_rows(seg, pl.multiple_of(me * own_rows, own_rows), own_rows)
    own_code = lane_codes(jnp.where(inside, 0.0, 1.0))
    scaled = low(dot(normed[:own_rows, :], wq_pad[...]) * 0.125)
    q_aug[...] = scaled + jnp.concatenate([own_code] * HEADS, axis=1)


def forward_kernel(
    own_rows,
    me_ref, y_rows, far_rows, codes, real, counted, tokens, cot,
    gain_one, wk_pad, wv_pad, wo_pad, wk_t, wv_t,
    w_cross, b_cross, w_mix, w_ens1, gain_two, w_up, b_up, w_ens2,
    normed_a, normed_ta, q_aug, k_a, v_a, kt_a, vt_a,
    out_rows, d_first_out, dn_own, payload, vectors,
    normed_b, normed_tb, k_b, v_b, kt_b,
    grad_att, lse_out, delta_out, pself_out, dself_out, seg_grad_out,
    vt_b, scores, o_t,
):
    gain = gain_one[...]
    for step, rows_in in enumerate((y_rows[...], far_rows[:own_rows, :])):
        at = step * own_rows
        project(
            rows_in, gain, codes[at + 2 * own_rows : at + 3 * own_rows, :],
            wk_pad[...], wv_pad[...], wk_t[...], wv_t[...], at,
            normed_b, normed_tb, k_b, v_b, kt_b, vt_b,
        )
    normed_own = normed_a[:own_rows, :]
    heads16 = head_selector()
    lanes_own = lax.broadcasted_iota(jnp.int32, (own_rows, WIDE), 1) & (LANES - 1)
    v_own = v_a[:own_rows, :]
    self_product = jnp.where(
        lanes_own < HEAD_DIM, high(q_aug[...]) * high(k_a[:own_rows, :]), 0.0
    )
    self_scores = head_sums(heads16, self_product)
    own_real = real[:, :own_rows] > 0
    o_t[...] = jnp.zeros_like(o_t)
    lse_out[...] = jnp.zeros_like(lse_out)
    half_keys = 2 * own_rows
    for h in range(HEADS):
        lanes = slice(h * LANES, (h + 1) * LANES)
        rows_h = slice(h * HEAD_DIM, (h + 1) * HEAD_DIM)
        q_h = q_aug[:, lanes]
        top = jnp.where(own_real, HUGE, self_scores[h : h + 1])
        self_h = top
        for c, k_half in enumerate((k_a, k_b)):
            part = dot_nt(k_half[:, lanes], q_h)
            scores[c * half_keys : (c + 1) * half_keys, :] = part
            top = jnp.maximum(top, jnp.max(part, axis=0, keepdims=True))
        p_self = jnp.exp(self_h - top)
        total = p_self
        acc = high(low(p_self)) * high(vt_a[rows_h, :own_rows])
        for c, vt_half in enumerate((vt_a, vt_b)):
            p = jnp.exp(scores[c * half_keys : (c + 1) * half_keys, :] - top)
            total = total + jnp.sum(p, axis=0, keepdims=True)
            acc = acc + dot(vt_half[rows_h, :], low(p))
        o_t[h * LANES : h * LANES + HEAD_DIM, :] = acc / total
        lse_out[h : h + 1, :] = top + jnp.log(total)
    att = o_t[...].T
    att_low = low(att)

    modules = []
    for g in range(2):
        lanes = slice(g * 256, (g + 1) * 256)
        modules.append(low(dot(att_low[:, lanes], wo_pad[lanes, :])))
    crossed = dot(normed_own, w_cross[...]) + b_cross[...]
    modules.append(low(high(normed_own) * crossed))
    counts = jnp.sum(high(counted[...]), axis=1, keepdims=True)
    counts = jnp.maximum(counts, 1.0)
    seg_sums = dot(counted[:, :half_keys], normed_a[...]) + dot(counted[:, half_keys:], normed_b[...])
    seg_mean = low(seg_sums / counts)
    picked = lax.broadcasted_iota(jnp.int32, (LANES, 16), 0) - HEAD_DIM
    picked = (picked == lax.broadcasted_iota(jnp.int32, (LANES, 16), 1)) & (picked < SEGS)
    own_member = 1.0 - dot(q_aug[:, :LANES], low(jnp.where(picked, 1.0, 0.0)))
    own_lane = lax.broadcasted_iota(jnp.int32, (own_rows, 16), 1)
    own_member = low(jnp.where(own_lane < SEGS, own_member, 0.0))
    mixed = low(dot(own_member, seg_mean))
    modules.append(low(dot(mixed, w_mix[...])))
    first = high(tokens[...])
    for i in range(4):
        first = first + dot(modules[i], w_ens1[i * D : (i + 1) * D, :])
    unit_two, scale_two = unit_rows(first)
    normed_two = low(unit_two * gain_two[...])
    inner = dot(normed_two, w_up[...]) + b_up[...]
    cdf = 0.5 * (1.0 + lax.erf(inner * 0.7071067811865476))
    active = low(inner * cdf)
    slope = cdf + inner * jnp.exp(-0.5 * inner * inner) * 0.3989422804014327
    out_rows[...] = first + (dot(active, w_ens2[:FF, :]) + dot(normed_two, w_ens2[FF:, :]))

    core, y_bit, x_bit, z_bit = bits_of(me_ref)
    orders = (y_bit * 4 + x_bit * 2 + z_bit, x_bit * 4 + y_bit * 2 + z_bit)
    block = payload.shape[0] // 32
    place = [0]

    def put(grad):
        middle = grad.shape[0] // 2
        for i in range(middle // block):
            n = place[0]
            place[0] = n + 1
            spot = (n // 8) * 8 + ((n % 8) ^ orders[n // 8])
            for side in range(2):
                start = pl.multiple_of(((side ^ core) * 16 + spot) * block, block)
                first = side * middle + i * block
                payload[pl.ds(start, block), :] = low(grad[first : first + block])

    e2 = cot[...]
    put(dot_tn(active, e2))
    put(dot_tn(normed_two, e2))
    d_inner = low(dot_nt(e2, w_ens2[:FF, :]) * slope)
    b_up_grad = jnp.sum(high(d_inner), axis=0, keepdims=True)
    grad_up = dot_tn(normed_two, d_inner)
    for i in range(FF // D):
        put(grad_up[:, i * D : (i + 1) * D])
    d_norm2 = dot_nt(e2, w_ens2[FF:, :]) + dot_nt(d_inner, w_up[...])
    d_first = high(e2) + norm_back(d_norm2, unit_two, scale_two, gain_two[...])
    d_first_out[...] = d_first
    e1 = low(d_first)
    d_modules = []
    for i in range(4):
        put(dot_tn(modules[i], e1))
        d_modules.append(low(dot_nt(e1, w_ens1[i * D : (i + 1) * D, :])))
    out_grads = []
    for g in range(2):
        lanes = slice(g * 256, (g + 1) * 256)
        out_grads.append(dot_tn(att_low[:, lanes], d_modules[g]))
        grad_att[:, lanes] = low(dot_nt(d_modules[g], wo_pad[lanes, :]))
    put(narrow_rows(jnp.concatenate(out_grads, axis=0)))
    d_cross = low(high(d_modules[2]) * high(normed_own))
    put(dot_tn(normed_own, d_cross))
    put(dot_tn(mixed, d_modules[3]))
    dn_own[...] = high(d_modules[2]) * crossed + dot_nt(d_cross, w_cross[...])
    d_mixed = dot_nt(d_modules[3], w_mix[...])
    mixed_up = low(d_mixed)
    mixed_down = low(d_mixed - high(mixed_up))
    seg_grad_out[...] = (dot_tn(own_member, mixed_up) + dot_tn(own_member, mixed_down)) / counts
    vectors[...] = jnp.zeros_like(vectors)
    for i in range(FF // D):
        vectors[i : i + 1, :] = b_up_grad[:, i * D : (i + 1) * D]
    vectors[4:5, :] = jnp.sum(high(d_cross), axis=0, keepdims=True)
    vectors[5:6, :] = jnp.sum(d_norm2 * unit_two, axis=0, keepdims=True)

    d_att = high(grad_att[...])
    delta = head_sums(heads16, d_att * att)
    delta_out[...] = delta
    p_self = jnp.where(own_real, 0.0, jnp.exp(self_scores - lse_out[...]))
    dp_self = head_sums(heads16, d_att * high(v_own))
    pself_out[...] = low(p_self)
    dself_out[...] = low(p_self * (dp_self - delta))


def head_kernel(
    own_rows, h,
    q_aug, k_a, k_b, v_a, v_b, kt_a, kt_b, grad_att, lse, delta, pself, dself, after_one, after_two,
    dk_out, dv_out, dq_out,
):
    half_keys = 2 * own_rows
    row16 = lax.broadcasted_iota(jnp.int32, (16, LANES), 0)
    spread = low(jnp.where(row16 == h, 1.0, 0.0))
    lanes = slice(h * LANES, (h + 1) * LANES)
    rows_h = slice(h * HEAD_DIM, (h + 1) * HEAD_DIM)
    q_h = q_aug[:, lanes]
    g_h = grad_att[:, lanes]
    lse_h = lse[h : h + 1, :]
    delta_h = delta[h : h + 1, :]
    acc = high(dself[h : h + 1, :]) * high(kt_a[rows_h, :own_rows])
    for c, (k_half, v_half, kt_half) in enumerate(((k_a, v_a, kt_a), (k_b, v_b, kt_b))):
        at = slice(c * half_keys, (c + 1) * half_keys)
        p = jnp.exp(dot_nt(k_half[:, lanes], q_h) - lse_h)
        ds = low(p * (dot_nt(v_half[:, lanes], g_h) - delta_h))
        dv = dot(low(p), g_h)
        dk = dot(ds, q_h)
        if c == 0:
            dk_self = dot_tn(dself[...], spread) * high(q_h)
            dv_self = dot_tn(pself[...], spread) * high(g_h)
            dk_out[:own_rows, :] = low(dk[:own_rows] + dk_self)
            dv_out[:own_rows, :] = low(dv[:own_rows] + dv_self)
            dk_out[own_rows:half_keys, :] = low(dk[own_rows:])
            dv_out[own_rows:half_keys, :] = low(dv[own_rows:])
        else:
            dk_out[at, :] = low(dk)
            dv_out[at, :] = low(dv)
        acc = acc + dot(kt_half[rows_h, :], ds)
    dq_out[...] = low(acc * 0.125)


def rows_kernel(
    own_rows,
    dk0, dk1, dk2, dk3, dv0, dv1, dv2, dv3, dq0, dq1, dq2, dq3, after, normed_a, normed_b, counted, seg_grad, dn_own,
    gain_one, wq, wk_pad, wv_pad, vectors,
    out, dq_out,
    dn,
):
    half_keys = 2 * own_rows
    dq = jnp.concatenate([high(part[...]) for part in (dq0, dq1, dq2, dq3)], axis=0)
    dq_rows = low(dq.T)
    dq_out[...] = dq_rows
    dk_pairs = [jnp.concatenate([dk0[...], dk1[...]], axis=1), jnp.concatenate([dk2[...], dk3[...]], axis=1)]
    dv_pairs = [jnp.concatenate([dv0[...], dv1[...]], axis=1), jnp.concatenate([dv2[...], dv3[...]], axis=1)]
    up = low(seg_grad[...])
    down = low(seg_grad[...] - high(up))
    for c in range(2):
        at = slice(c * half_keys, (c + 1) * half_keys)
        mixing = dot_tn(counted[:, at], up) + dot_tn(counted[:, at], down)
        dn[at, :] = mixing + (
            dot_nt(dk_pairs[0][at, :], wk_pad[:, :256])
            + dot_nt(dk_pairs[1][at, :], wk_pad[:, 256:])
            + dot_nt(dv_pairs[0][at, :], wv_pad[:, :256])
            + dot_nt(dv_pairs[1][at, :], wv_pad[:, 256:])
        )
    dn[:own_rows, :] = dn[:own_rows, :] + (dot_nt(dq_rows, wq[...]) + dn_own[...])
    gain_grad = jnp.sum(dn[:half_keys, :] * high(normed_a[...]), axis=0, keepdims=True)
    gain_grad += jnp.sum(dn[half_keys:, :] * high(normed_b[...]), axis=0, keepdims=True)
    gain_grad = gain_grad / gain_one[...]
    count = out.shape[0] // 2
    for step in range(4):
        at = (step % 2) * count + (step // 2) * own_rows
        out[at : at + own_rows, :] = low(dn[step * own_rows : (step + 1) * own_rows, :])
    tail = lax.broadcasted_iota(jnp.int32, (16, D), 0)
    row = jnp.where(tail == 6, gain_grad, vectors[...])
    out[count - 16 : count, :] = low(row)
    out[2 * count - 16 :, :] = low(row)


def weights_kernel(
    own_rows,
    me_ref,
    dk0, dk1, dk2, dk3, dv0, dv1, dv2, dv3, dq_rows, normed_ta, normed_tb, after,
    out,
):
    half_keys = 2 * own_rows

    def key_grad(parts):
        pairs = [jnp.concatenate([parts[i][...], parts[i + 1][...]], axis=1) for i in (0, 2)]
        return narrow(
            jnp.concatenate(
                [
                    dot(normed_ta[...], pair[:half_keys]) + dot(normed_tb[...], pair[half_keys:])
                    for pair in pairs
                ],
                axis=1,
            )
        )

    core, y_bit, x_bit, _ = bits_of(me_ref)
    order = core * 4 + y_bit * 2 + x_bit
    part = D // 8
    for i, grad in enumerate(
        (
            dot(normed_ta[:, :own_rows], dq_rows[...]),
            key_grad((dk0, dk1, dk2, dk3)),
            key_grad((dv0, dv1, dv2, dv3)),
        )
    ):
        for n in range(8):
            at = ((n ^ order) * 3 + i) * part
            out[pl.ds(pl.multiple_of(at, part), part), :] = low(grad[n * part : (n + 1) * part])


def finish_kernel(mine, other, tokens, d_first, gain_one, after, grad_tokens, done):
    unit, scale = unit_rows(high(tokens[...]))
    total = high(mine[...]) + high(other[...])
    grad_tokens[...] = d_first[...] + norm_back(total, unit, scale, gain_one[...])
    done[...] = after[:16, :]


def unpack_kernel(me_ref, mine, other, after, attn_out, cross, mix, ens1, up, ens2):
    core, y_bit, x_bit, z_bit = bits_of(me_ref)
    orders = (y_bit * 4 + x_bit * 2 + z_bit, x_bit * 4 + y_bit * 2 + z_bit)
    block = mine.shape[0] // 16
    every = slice(None)
    jobs = [(ens2, 0, FF, every), (ens2, FF, D, every)]
    jobs += [(up, 0, D, slice(i * D, (i + 1) * D)) for i in range(FF // D)]
    jobs += [(ens1, i * D, D, every) for i in range(4)]
    jobs += [(attn_out, 0, D, every), (cross, 0, D, every), (mix, 0, D, every)]
    n = 0
    for to, first, count, columns in jobs:
        for i in range(count // 2 // block):
            spot = (n // 8) * 8 + ((n % 8) ^ orders[n // 8])
            n += 1
            for side, source in ((core, mine), (1 - core, other)):
                at = pl.multiple_of(first + side * (count // 2) + i * block, block)
                value = source[pl.ds(pl.multiple_of(spot * block, block), block), :]
                to[pl.ds(at, block), columns] = high(value)


def unpack_small_kernel(
    me_ref, mine, other, vec, gain_one, query, key, value, b_cross, gain_two, b_up
):
    core, y_bit, x_bit, _ = bits_of(me_ref)
    order = y_bit * 2 + x_bit
    part = D // 8
    for side, source in ((core, mine), (1 - core, other)):
        for n in range(4):
            for i, to in enumerate((query, key, value)):
                at = pl.multiple_of((n ^ order) * 3 * part + i * part, part)
                here = pl.ds(pl.multiple_of((side * 4 + n) * part, part), part)
                to[here, :] = high(source[pl.ds(at, part), :])
    wide = high(vec[...])
    for i in range(FF // D):
        b_up[:, i * D : (i + 1) * D] = wide[i : i + 1]
    b_cross[...] = wide[4:5]
    gain_two[...] = wide[5:6]
    gain_one[...] = wide[6:7]


def swap(value, axis, count, step):
    return lax.ppermute(value, axis, [(i, i ^ step) for i in range(count)])


def bits_of(me_ref):
    module, batch = me_ref[0], me_ref[1]
    return module & 1, (module >> 1) & 1, batch & 1, (batch >> 1) & 1


def sum_kernel(jobs, afters, *refs):
    inputs, outs = refs[: 2 * len(jobs)], refs[2 * len(jobs) + afters :]
    o = 0
    for j, cuts in enumerate(jobs):
        mine, got = inputs[2 * j], inputs[2 * j + 1]
        for spans in cuts:
            to = 0
            for first, count in spans:
                here = slice(first, first + count)
                outs[o][to : to + count, :] = added(mine[here, :], got[here, :])
                to += count
            o += 1


def join_kernel(jobs, afters, *refs):
    out = refs[-1]
    at = 0
    for ref in refs[:jobs]:
        count = ref.shape[0]
        out[at : at + count, :] = ref[...]
        at += count


def added(one, two):
    return low(high(one) + high(two))


def shards(
    n_batch,
    n_module,
    tokens,
    seg_lengths,
    valid,
    cotangent,
    gain_one,
    w_query,
    w_key,
    w_value,
    w_attn_out,
    w_cross,
    b_cross,
    w_mix,
    w_ens1,
    gain_two,
    w_up,
    b_up,
    w_ens2,
):
    module = lax.axis_index("module")
    batch = lax.axis_index("batch")
    own = tokens.shape[0]
    rows = valid.shape[0]
    me = jnp.stack([module, batch]).astype(jnp.int32)

    def by_core(value):
        return swap(value, "module", n_module, 1)

    def by_y(value):
        return swap(value, "module", n_module, 2)

    def by_batch(value, step):
        return swap(value, "batch", n_batch, step)

    from_core = by_core(tokens)
    from_y = by_y(tokens)
    square = ((D, D), BF)
    keys = 2 * own
    row = ((1, D), F32)
    gain_row, valid_row = gain_one.reshape(1, D), valid.reshape(1, rows)
    (token,) = call(start_kernel, [((8, LANES), F32)], [], "s", 4, 20)(me)
    (
        wq_pad, wk_pad, wv_pad, wo_pad, wk_t, wv_t, codes, real, counted,
        normed_a, normed_ta, q_aug, k_a, v_a, kt_a, vt_a,
    ) = call(
        functools.partial(first_kernel, own),
        [
            ((D, WIDE), BF), ((D, WIDE), BF), ((D, WIDE), BF), ((WIDE, D), BF), square, square,
            ((rows, LANES), BF), ((1, rows), F32), ((16, rows), BF),
            ((keys, D), BF), ((D, keys), BF), ((own, WIDE), BF), ((keys, WIDE), BF), ((keys, WIDE), BF),
            ((D, keys), BF), ((D, keys), BF),
        ],
        [], "ss" + "v" * 9, 16, 5,
    )(
        me, seg_lengths, token, from_core, tokens, valid_row, gain_row, w_query, w_key, w_value, w_attn_out
    )
    from_far = by_core(jnp.concatenate([from_y, normed_a[:16]], axis=0))
    (
        out_rows, d_first, dn_own, payload, vectors, normed_b, normed_tb, k_b, v_b, kt_b,
        grad_att, lse, delta, pself, dself, seg_grad,
    ) = call(
        functools.partial(forward_kernel, own),
        [
            ((own, D), F32), ((own, D), F32), ((own, D), F32), ((16 * D, D), BF), ((16, D), F32),
            ((keys, D), BF), ((D, keys), BF), ((keys, WIDE), BF), ((keys, WIDE), BF), ((D, keys), BF),
            ((own, WIDE), BF), ((16, own), F32), ((16, own), F32), ((16, own), BF), ((16, own), BF), ((16, D), F32),
        ],
        [pltpu.VMEM((D, keys), BF), pltpu.VMEM((rows, own), F32), pltpu.VMEM((WIDE, own), F32)],
        "s" + "v" * 28, 32, 18,
    )(
        me, from_y, from_far, codes, real, counted, tokens, cotangent, gain_row, wk_pad, wv_pad, wo_pad, wk_t, wv_t,
        w_cross, b_cross.reshape(1, D), w_mix, w_ens1, gain_two.reshape(1, D), w_up, b_up.reshape(1, FF), w_ens2,
        normed_a, normed_ta, q_aug, k_a, v_a, kt_a, vt_a,
    )

    def head(index, after_one, after_two):
        return call(
            functools.partial(head_kernel, own, index),
            [((rows, LANES), BF), ((rows, LANES), BF), ((HEAD_DIM, own), BF)],
            [], "v" * 14, 16, 3,
        )(
            q_aug, k_a, k_b, v_a, v_b, kt_a, kt_b, grad_att, lse, delta, pself, dself, after_one[:16], after_two[:16]
        )

    def sums(jobs, pairs, *after):
        outs = [((sum(count for _, count in spans), D), BF) for cuts in jobs for spans in cuts]
        args = [value for pair in pairs for value in pair] + list(after)
        body = functools.partial(sum_kernel, jobs, len(after))
        return call(body, outs, [], "v" * len(args), 8, 1)(*args)

    def joined(parts, *after):
        count = sum(part.shape[0] for part in parts)
        body = functools.partial(join_kernel, len(parts), len(after))
        args = list(parts) + list(after)
        return call(body, [((count, D), BF)], [], "v" * len(args), 8, 1)(*args)[0]

    size = payload.shape[0] // 8
    got = by_core(payload[4 * size :])
    dk0, dv0, dq0 = head(0, lse, lse)
    quarters = [[(i * size, size)] for i in range(4)]
    a, a_send, b, b_send = sums([quarters], [(payload, got)])
    dk1, dv1, dq1 = head(1, a, dq0)
    dk2, dv2, dq2 = head(2, b, dq1)
    a_got, b_got = by_y(a_send), by_batch(b_send, 1)
    halves = [[(0, size // 2)], [(size // 2, size // 2)]]
    a, a_send, b, b_send = sums([halves] * 2, [(a, a_got), (b, b_got)])
    dk3, dv3, dq3 = head(3, a, dq2)
    a_got, b_got = by_batch(a_send, 1), by_y(b_send)
    eighth = size // 4
    eighths = [[(0, eighth)], [(eighth, eighth)]]
    a, a_send, b, b_send = sums([eighths] * 2, [(a, a_got), (b, b_got)])
    ab, ab_send = joined([a, b]), joined([a_send, b_send])
    ab_got = by_batch(ab_send, 2)

    steps = [1 << place for place in range(1, n_batch.bit_length() - 1)]
    part = D // 8
    count = 2 * own + 16
    shared, dq_rows = call(
        functools.partial(rows_kernel, own),
        [((2 * count, D), BF), ((own, D), BF)],
        [pltpu.VMEM((rows, D), F32)],
        "v" * 23, 16, 3,
    )(
        dk0, dk1, dk2, dk3, dv0, dv1, dv2, dv3, dq0, dq1, dq2, dq3, ab, normed_a, normed_b, counted, seg_grad, dn_own,
        gain_row, w_query, wk_pad, wv_pad, vectors,
    )
    shared_got = by_core(shared[count:])
    every = [[[(0, 2 * eighth)]]]
    (ab,) = sums(every, [(ab, ab_got)], shared)
    ab_got = by_batch(ab, steps[1]) if len(steps) > 1 else ab
    (q,) = call(functools.partial(weights_kernel, own), [((24 * part, D), BF)], [], "s" + "v" * 12, 16, 3)(
        me, dk0, dk1, dk2, dk3, dv0, dv1, dv2, dv3, dq_rows, normed_ta, normed_tb, ab
    )
    q_got = by_core(q[12 * part :])
    dn, dn_send, vec = sums([[[(0, own)], [(own, own)], [(2 * own, 16)]]], [(shared, shared_got)], q)
    q, q_send = sums([[[(0, 6 * part)], [(6 * part, 6 * part)]]], [(q, q_got)], vec)
    q_got = by_y(joined([q_send, vec]))
    dn_got = by_y(dn_send)
    six = 6 * part
    q, q_send = sums(
        [[[(0, 3 * part), (six, 16)], [(3 * part, 3 * part + 16)]]], [(joined([q, vec]), q_got)]
    )
    q_got = by_batch(q_send, 1)
    for i in range(1, len(steps)):
        (ab,) = sums(every, [(ab, ab_got)], q)
        if i + 1 < len(steps):
            ab_got = by_batch(ab, steps[i + 1])
    ab_got = by_batch(ab, steps[0])
    whole = [[[(0, 3 * part + 16)]]]
    (q,) = sums(whole, [(q, q_got)], ab)
    q_got = by_batch(q, steps[0])
    a = joined([ab[:eighth], ab_got[:eighth]], q)
    b = joined([ab[eighth:], ab_got[eighth:]], q)
    a_got, b_got = by_batch(a, 1), by_y(b)
    for step in steps[1:]:
        (q,) = sums(whole, [(q, q_got)], a, b)
        q_got = by_batch(q, step)
    grad_tokens, done = call(
        finish_kernel, [((own, D), F32), ((16, D), BF)], [], "v" * 6, 16, 2
    )(dn, dn_got, tokens, d_first, gain_row, q)
    a = joined([a, a_got], done)
    b = joined([b, b_got], done)
    a_got, b_got = by_y(a), by_batch(b, 1)
    (q,) = sums(whole, [(q, q_got)], a, b)
    q, vec = q[: 3 * part], q[3 * part :]
    q_got = by_batch(q, 1)
    q = joined([q, q_got])
    q_got = by_y(q)
    big = joined([a, a_got, b, b_got], q)
    big_got = by_core(big)
    q = joined([q, q_got], big)
    q_got = by_core(q)
    wide = ((D, D), F32)
    attn_out, cross, mix, ens1, up, ens2 = call(
        unpack_kernel,
        [wide, wide, wide, ((4 * D, D), F32), ((D, FF), F32), ((FF + D, D), F32)],
        [], "svvv", 16, 3,
    )(me, big, big_got, q)
    gain_one_g, query, key, value, b_cross_g, gain_two_g, b_up_g = call(
        unpack_small_kernel, [row, wide, wide, wide, row, row, ((1, FF), F32)], [], "svvv", 16, 1
    )(me, q, q_got, vec)
    return (
        out_rows, grad_tokens, gain_one_g.reshape(D), query, key, value, attn_out, cross, b_cross_g.reshape(D), mix,
        ens1, gain_two_g.reshape(D), up, b_up_g.reshape(FF), ens2,
    )


def solution(mesh):
    rows = P(("batch", "module"), None)
    in_specs = (rows, P("batch", None), P("batch"), rows) + (P(),) * 13
    out_specs = (rows, rows) + (P(),) * 13
    body = functools.partial(shards, mesh.shape["batch"], mesh.shape["module"])
    return jax.shard_map(body, mesh=mesh, in_specs=in_specs, out_specs=out_specs, check_vma=False)
```

time: 134 us -> 97.8 us (0.73)
  local copies, waits for them, and re-layouts: 18.9 us -> 0.78 us
  other arithmetic: 12.1 us -> 0.09 us
  waiting for transfers between devices: 34 us -> 27.6 us
  Pallas kernels: 38 us -> 40.5 us
  starting transfers between devices: 29.5 us -> 27.4 us
    unnamed x53 -> x34, local copies, waits for them, and re-layouts: 16.6 us -> 0.61 us
    convert_element_type x19 -> x0, other arithmetic: 6.77 us -> none  [the longest x14 3.68 us: low(): return v.astype(BF)]
    ppermute x24 -> x26, waiting for transfers between devices: 34 us -> 27.6 us  [swap(): return lax.ppermute(value, axis, [(i, i ^ step) for i in range(count)])]
    concatenate x8 -> x1, other arithmetic: 3.7 us -> 0.02 us  [shards(): from_far = by_core(jnp.concatenate([from_y, normed_a[:16]], axis=0))]
    pallas_call x4 -> x34, Pallas kernels: 38 us -> 40.5 us  [the longest x1 15.2 us: shards(): call(functools.partial(forward_kernel, own), [((own, D), F32), ((own, D),...]
    ppermute x24 -> x26, starting transfers between devices: 29.5 us -> 27.4 us  [swap(): return lax.ppermute(value, axis, [(i, i ^ step) for i in range(count)])]
    select_n x9 -> x0, other arithmetic: 1.6 us -> none  [join(): jnp.where(bit == 0, jnp.concatenate([mine, other], 0), jnp.concatenate([o...]
    dynamic_slice x7 -> x0, local copies, waits for them, and re-layouts: 1.41 us -> none  [split(): lax.dynamic_slice_in_dim(value, (1 - bit) * half, half, 0)]
  transfers between devices with their start and end apart: 24 -> 26, of which waited for: 15 -> 12; matrix products, arithmetic and copies ran while one was open for 7% -> 0% of each run, Pallas kernels for 1% -> 23%
where the time goes in v1:
time: 97.8 us; the launch traced here: 97.6 us
  Pallas kernels  40.5 us (41%)
  waiting for transfers between devices  27.6 us (28%)
  starting transfers between devices  27.4 us (28%)
  between operations  1.18 us (1%)
    ppermute x26, waiting for transfers between devices, swap(): return lax.ppermute(value, axis, [(i, i ^ step) for i in range(count)])  27.6 us
    ppermute x26, starting transfers between devices, swap(): return lax.ppermute(value, axis, [(i, i ^ step) for i in range(count)])  27.4 us
    pallas_call x1, Pallas kernels, shards(): call(functools.partial(forward_kernel, own), [((own, D), F32), ((own, D),...  15.2 us
    pallas_call x4, Pallas kernels, head(): call(functools.partial(head_kernel, own, index), [((rows, LANES), BF), ((...  11.3 us
    pallas_call x1, Pallas kernels, shards(): call(functools.partial(first_kernel, own), [((D, WIDE), BF), ((D, WIDE),...  3.15 us
    pallas_call x1, Pallas kernels, shards(): call(unpack_kernel, [wide, wide, wide, ((4 * D, D), F32), ((D, FF), F32),...  2.74 us
    pallas_call x1, Pallas kernels, shards(): call(functools.partial(rows_kernel, own), [((2 * count, D), BF), ((own, D...  1.99 us
  transfers between devices with their start and end apart: 26, of which 12 were waited for; matrix products, arithmetic and copies ran while one was open for 0% of the time, Pallas kernels for 23%

profile of v1, /device:TPU:0, one launch (start us, length us, event | category | flops | bytes accessed | tf_op | source)
XLA Modules:
  0.0 97.6 jit_solution(18312734626130048456)
XLA Ops:
  1.2 2.6 %collective-permute-start = (bf16[512,256]{1,0:T(8,128)(2,1)}, bf16[512,256]{1,0:T(8,128)(2,1)S(1)}, u32[]{:S(2)}, u32[]{:S(2)}) collective-permute-start(bf16[512,256]{1,0:T(8,128)(2,1)} %tokens.5), channel_id=1, source_target_pairs={{0,2},{1,3},{2,0},{3,1},{4,6},{5,7},{6,4},{7,5},{8,10},{9,11},{10,... | collective-permute-start | bytes 786440 | tf_op jit(solution)/shard_map/ppermute | solution.py:480
  5.1 3.1 %shard_map.281 = (bf16[256,512]{1,0:T(8,128)(2,1)}, bf16[256,512]{1,0:T(8,128)(2,1)S(1)}, bf16[256,512]{1,0:T(8,128)(2,1)S(1)}, bf16[512,256]{1,0:T(8,128)(2,1)S...) custom-call(s32[2]{0:T(128)S(1)} %pad_add_fusion.me_ref, ...), custom_call_target="tpu_custom_call" | custom-call | flops 5000000000 | bytes 1048576 | tf_op jit(solution)/shard_map/pallas_call | solution.py:561
  8.2 2.6 %collective-permute-done.y_rows = bf16[512,256]{1,0:T(8,128)(2,1)S(1)} collective-permute-done((bf16[512,256]{1,0:T(8,128)(2,1)}, bf16[512,256]{1,0:T(8,128)(2,1)S(1)}, u32[]{:S(2)}, u32[]{:S(2)}) %collective-permute-start) | collective-permute-done | bytes 262176 | tf_op jit(solution)/shard_map/ppermute | solution.py:480
  11.0 1.5 %collective-permute-done.2.far_rows = bf16[528,256]{1,0:T(8,128)(2,1)S(1)} collective-permute-done((bf16[528,256]{1,0:T(8,128)(2,1)S(1)}, bf16[528,256]{1,0:T(8,128)(2,1)S(1)}, u32[]{:S(2)}, u32[]{:S(2)}) %collective-permute-start.2) | collective-permute-done | bytes 270368 | tf_op jit(solution)/shard_map/ppermute | solution.py:480
  12.6 15.2 %shard_map.282 = (f32[512,256]{1,0:T(8,128)}, f32[512,256]{1,0:T(8,128)S(1)}, f32[512,256]{1,0:T(8,128)S(1)}, bf16[4096,256]{1,0:T(8,128)(2,1)S(1)}, f32[16,256]...) custom-call(s32[2]{0:T(128)S(1)} %pad_add_fusion.me_ref, ...), custom_call_target="tpu_custom_call" | custom-call | flops 17999998976 | bytes 1048576 | tf_op jit(solution)/shard_map/pallas_call | solution.py:577
  28.1 2.8 %shard_map.283 = (bf16[2048,128]{1,0:T(8,128)(2,1)S(1)}, bf16[2048,128]{1,0:T(8,128)(2,1)S(1)}, bf16[64,512]{1,0:T(8,128)(2,1)S(1)}) custom-call(bf16[512,512]{1,0:T(8,128)(2,1)S(1)} %get-tuple-element.104.q_aug, bf16[1024,512]{1,0:T(8,128)(2,1)S(1)} %get-tuple-element.105.k_a, bf16[1024,512]{1,0:T(8,128)(2,1)S(1)} %get-tuple-element.110.k_b, ...), custom_call_target="tpu_custom_call" | custom-call | flops 3000000000 | bytes 1048576 | tf_op jit(solution)/shard_map/pallas_call | solution.py:593
  31.1 1.8 %collective-permute-start.4 = (bf16[512,256]{1,0:T(8,128)(2,1)S(1)}, bf16[512,256]{1,0:T(8,128)(2,1)S(1)}, u32[]{:S(2)}, u32[]{:S(2)}) collective-permute-start(bf16[512,256]{1,0:T(8,128)(2,1)S(1)} %get-tuple-element.126), channel_id=1, source_target_pairs={{0,2},{1,3},{2,0},{3,1},{4,6},{5,7},{6,4},{7,5},{8,10},{9,11},{10,... | collective-permute-start | bytes 786440 | tf_op jit(solution)/shard_map/ppermute | solution.py:480
  34.5 2.8 %shard_map.285 = (bf16[2048,128]{1,0:T(8,128)(2,1)S(1)}, bf16[2048,128]{1,0:T(8,128)(2,1)S(1)}, bf16[64,512]{1,0:T(8,128)(2,1)S(1)}) custom-call(bf16[512,512]{1,0:T(8,128)(2,1)S(1)} %get-tuple-element.104.q_aug, bf16[1024,512]{1,0:T(8,128)(2,1)S(1)} %get-tuple-element.105.k_a, bf16[1024,512]{1,0:T(8,128)(2,1)S(1)} %get-tuple-element.110.k_b, ...), custom_call_target="tpu_custom_call" | custom-call | flops 3000000000 | bytes 1048576 | tf_op jit(solution)/shard_map/pallas_call | solution.py:593
  37.3 2.8 %shard_map.286 = (bf16[2048,128]{1,0:T(8,128)(2,1)S(1)}, bf16[2048,128]{1,0:T(8,128)(2,1)S(1)}, bf16[64,512]{1,0:T(8,128)(2,1)S(1)}) custom-call(bf16[512,512]{1,0:T(8,128)(2,1)S(1)} %get-tuple-element.104.q_aug, bf16[1024,512]{1,0:T(8,128)(2,1)S(1)} %get-tuple-element.105.k_a, bf16[1024,512]{1,0:T(8,128)(2,1)S(1)} %get-tuple-element.110.k_b, ...), custom_call_target="tpu_custom_call" | custom-call | flops 3000000000 | bytes 1048576 | tf_op jit(solution)/shard_map/pallas_call | solution.py:593
  41.4 1.6 %collective-permute-start.6 = (bf16[256,256]{1,0:T(8,128)(2,1)S(1)}, bf16[256,256]{1,0:T(8,128)(2,1)S(1)}, u32[]{:S(2)}, u32[]{:S(2)}) collective-permute-start(bf16[256,256]{1,0:T(8,128)(2,1)S(1)} %get-tuple-element.136), channel_id=1, source_target_pairs={{0,4},{4,0},{8,12},{12,8},{16,20},{20,16},{24,28},{28,24},{1,5},{5... | collective-permute-start | bytes 393224 | tf_op jit(solution)/shard_map/ppermute | solution.py:480
  43.5 3.0 %shard_map.288 = (bf16[2048,128]{1,0:T(8,128)(2,1)S(1)}, bf16[2048,128]{1,0:T(8,128)(2,1)S(1)}, bf16[64,512]{1,0:T(8,128)(2,1)S(1)}) custom-call(bf16[512,512]{1,0:T(8,128)(2,1)S(1)} %get-tuple-element.104.q_aug, bf16[1024,512]{1,0:T(8,128)(2,1)S(1)} %get-tuple-element.105.k_a, bf16[1024,512]{1,0:T(8,128)(2,1)S(1)} %get-tuple-element.110.k_b, ...), custom_call_target="tpu_custom_call" | custom-call | flops 3000000000 | bytes 1048576 | tf_op jit(solution)/shard_map/pallas_call | solution.py:593
  48.0 1.6 %collective-permute-start.9 = (bf16[256,256]{1,0:T(8,128)(2,1)S(1)}, bf16[256,256]{1,0:T(8,128)(2,1)S(1)}, u32[]{:S(2)}, u32[]{:S(2)}) collective-permute-start(bf16[256,256]{1,0:T(8,128)(2,1)S(1)} %shard_map.292), channel_id=1, source_target_pairs={{0,8},{4,12},{8,0},{12,4},{16,24},{20,28},{24,16},{28,20},{1,9},{5... | collective-permute-start | bytes 393224 | tf_op jit(solution)/shard_map/ppermute | solution.py:480
  49.7 2.0 %shard_map.291 = (bf16[2080,256]{1,0:T(8,128)(2,1)S(1)}, bf16[512,256]{1,0:T(8,128)(2,1)S(1)}) custom-call(bf16[2048,128]{1,0:T(8,128)(2,1)S(1)} %get-tuple-element.118.dk0, bf16[2048,128]{1,0:T(8,128)(2,1)S(1)} %get-tuple-element.122.dk1, bf16[2048,128]{1,0:T(8,128)(2,1)S(1)} %get-tuple-element.125.dk2, bf16[2048,128]{1,0:T(8,128)(2,1)S(1)} %get-tuple-element.130.dk3, ...), custom_call_target="tpu_custom_call" | custom-call | flops 3000000000 | bytes 1048576 | tf_op jit(solution)/shard_map/pallas_call | solution.py:634
  53.1 2.0 %shard_map.294.refs_2_.refs_0_ = bf16[768,256]{1,0:T(8,128)(2,1)S(1)} custom-call(s32[2]{0:T(128)S(1)} %pad_add_fusion.me_ref, bf16[2048,128]{1,0:T(8,128)(2,1)S(1)} %get-tuple-element.118.dk0, bf16[2048,128]{1,0:T(8,128)(2,1)S(1)} %get-tuple-element.122.dk1, bf16[2048,128]{1,0:T(8,128)(2,1)S(1)} %get-tuple-element.125.dk2, ...), custom_call_target="tpu_custom_call" | custom-call | flops 3000000000 | bytes 1048576 | tf_op jit(solution)/shard_map/pallas_call | solution.py:647
  57.2 2.6 %collective-permute-start.14 = (bf16[256,256]{1,0:T(8,128)(2,1)S(1)}, bf16[256,256]{1,0:T(8,128)(2,1)S(1)}, u32[]{:S(2)}, u32[]{:S(2)}) collective-permute-start(bf16[256,256]{1,0:T(8,128)(2,1)S(1)} %shard_map.293.after.refs_0_), channel_id=1, source_target_pairs={{0,16},{4,20},{8,24},{12,28},{16,0},{20,4},{24,8},{28,12},{1,17},{... | collective-permute-start | bytes 393224 | tf_op jit(solution)/shard_map/ppermute | solution.py:480
  59.8 1.6 %collective-permute-start.10 = (bf16[512,256]{1,0:T(8,128)(2,1)S(1)}, bf16[512,256]{1,0:T(8,128)(2,1)S(1)}, u32[]{:S(2)}, u32[]{:S(2)}) collective-permute-start(bf16[512,256]{1,0:T(8,128)(2,1)S(1)} %get-tuple-element.151), channel_id=1, source_target_pairs={{0,2},{1,3},{2,0},{3,1},{4,6},{5,7},{6,4},{7,5},{8,10},{9,11},{10,... | collective-permute-start | bytes 786440 | tf_op jit(solution)/shard_map/ppermute | solution.py:480
  62.4 3.8 %collective-permute-done.14.refs_1_ = bf16[256,256]{1,0:T(8,128)(2,1)S(1)} collective-permute-done((bf16[256,256]{1,0:T(8,128)(2,1)S(1)}, bf16[256,256]{1,0:T(8,128)(2,1)S(1)}, u32[]{:S(2)}, u32[]{:S(2)}) %collective-permute-start.14) | collective-permute-done | bytes 131104 | tf_op jit(solution)/shard_map/ppermute | solution.py:480
  68.4 3.0 %collective-permute-done.16 = bf16[256,256]{1,0:T(8,128)(2,1)S(1)} collective-permute-done((bf16[256,256]{1,0:T(8,128)(2,1)S(1)}, bf16[256,256]{1,0:T(8,128)(2,1)S(1)}, u32[]{:S(2)}, u32[]{:S(2)}) %collective-permute-start.16) | collective-permute-done | bytes 131104 | tf_op jit(solution)/shard_map/ppermute | solution.py:480
  72.1 1.6 %collective-permute-start.19 = (bf16[256,256]{1,0:T(8,128)(2,1)S(1)}, bf16[256,256]{1,0:T(8,128)(2,1)S(1)}, u32[]{:S(2)}, u32[]{:S(2)}) collective-permute-start(bf16[256,256]{1,0:T(8,128)(2,1)S(1)} %shard_map.303.refs_3_.refs_0_), channel_id=1, source_target_pairs={{0,2},{1,3},{2,0},{3,1},{4,6},{5,7},{6,4},{7,5},{8,10},{9,11},{10,... | collective-permute-start | bytes 393224 | tf_op jit(solution)/shard_map/ppermute | solution.py:480
  73.7 3.3 %collective-permute-start.17 = (bf16[112,256]{1,0:T(8,128)(2,1)S(1)}, bf16[112,256]{1,0:T(8,128)(2,1)S(1)}, u32[]{:S(2)}, u32[]{:S(2)}) collective-permute-start(bf16[112,256]{1,0:T(8,128)(2,1)S(1)} %shard_map.304.after.refs_0_), channel_id=1, source_target_pairs={{0,16},{4,20},{8,24},{12,28},{16,0},{20,4},{24,8},{28,12},{1,17},{... | collective-permute-start | bytes 172040 | tf_op jit(solution)/shard_map/ppermute | solution.py:480
  78.8 1.6 %collective-permute-start.23 = (bf16[512,256]{1,0:T(8,128)(2,1)S(1)}, bf16[512,256]{1,0:T(8,128)(2,1)S(1)}, u32[]{:S(2)}, u32[]{:S(2)}) collective-permute-start(bf16[512,256]{1,0:T(8,128)(2,1)S(1)} %shard_map.307.refs_3_.refs_2_), channel_id=1, source_target_pairs={{0,4},{4,0},{8,12},{12,8},{16,20},{20,16},{24,28},{28,24},{1,5},{5... | collective-permute-start | bytes 786440 | tf_op jit(solution)/shard_map/ppermute | solution.py:480
  81.0 5.5 %collective-permute-done.20.refs_1_ = bf16[96,256]{1,0:T(8,128)(2,1)S(1)} collective-permute-done((bf16[96,256]{1,0:T(8,128)(2,1)S(1)}, bf16[96,256]{1,0:T(8,128)(2,1)S(1)}, u32[]{:S(2)}, u32[]{:S(2)}) %collective-permute-start.20) | collective-permute-done | bytes 49184 | tf_op jit(solution)/shard_map/ppermute | solution.py:480
  87.7 4.2 %collective-permute-done.21.refs_1_ = bf16[192,256]{1,0:T(8,128)(2,1)S(1)} collective-permute-done((bf16[192,256]{1,0:T(8,128)(2,1)S(1)}, bf16[192,256]{1,0:T(8,128)(2,1)S(1)}, u32[]{:S(2)}, u32[]{:S(2)}) %collective-permute-start.21) | collective-permute-done | bytes 98336 | tf_op jit(solution)/shard_map/ppermute | solution.py:480
  94.9 2.7 %shard_map.313 = (f32[256,256]{1,0:T(8,128)}, f32[256,256]{1,0:T(8,128)}, f32[256,256]{1,0:T(8,128)}, f32[1024,256]{1,0:T(8,128)}, f32[256,1024]{1,0:T(8,128)}, /*index=5*/f32[1280,256]{1,0:T(8,128)}) custom-call(s32[2]{0:T(128)S(1)} %pad_add_fusion.me_ref, bf16[2048,256]{1,0:T(8,128)(2,1)S(1)} %shard_map.310.refs_2_.mine, ...), custom_call_target="tpu_custom_call" | custom-call | flops 3000000000 | bytes 1048576 | tf_op jit(solution)/shard_map/pallas_call | solution.py:690
  (112 shorter events, 21.2 us)
Async XLA Ops:
  0.6 3.8 %collective-permute-start.1 = (bf16[512,256]{1,0:T(8,128)(2,1)}, bf16[512,256]{1,0:T(8,128)(2,1)S(1)}, u32[]{:S(2)}, u32[]{:S(2)}) collective-permute-start(bf16[512,256]{1,0:T(8,128)(2,1)} %tokens.5), channel_id=1, source_target_pairs={{0,1},{1,0},{2,3},{3,2},{4,5},{5,4},{6,7},{7,6},{8,9},{9,8},{10,11... | collective-permute-start | bytes 786440 | tf_op jit(solution)/shard_map/ppermute | solution.py:480
  1.2 9.7 %collective-permute-start = (bf16[512,256]{1,0:T(8,128)(2,1)}, bf16[512,256]{1,0:T(8,128)(2,1)S(1)}, u32[]{:S(2)}, u32[]{:S(2)}) collective-permute-start(bf16[512,256]{1,0:T(8,128)(2,1)} %tokens.5), channel_id=1, source_target_pairs={{0,2},{1,3},{2,0},{3,1},{4,6},{5,7},{6,4},{7,5},{8,10},{9,11},{10,... | collective-permute-start | bytes 786440 | tf_op jit(solution)/shard_map/ppermute | solution.py:480
  10.9 1.6 %collective-permute-start.2 = (bf16[528,256]{1,0:T(8,128)(2,1)S(1)}, bf16[528,256]{1,0:T(8,128)(2,1)S(1)}, u32[]{:S(2)}, u32[]{:S(2)}) collective-permute-start(bf16[528,256]{1,0:T(8,128)(2,1)S(1)} %pad_maximum_fusion), channel_id=1, source_target_pairs={{0,1},{1,0},{2,3},{3,2},{4,5},{5,4},{6,7},{7,6},{8,9},{9,8},{10,11... | collective-permute-start | bytes 811016 | tf_op jit(solution)/shard_map/ppermute | solution.py:480
  27.9 3.0 %collective-permute-start.3 = (bf16[2048,256]{1,0:T(8,128)(2,1)S(1)}, bf16[2048,256]{1,0:T(8,128)(2,1)S(1)}, u32[]{:S(2)}, u32[]{:S(2)}) collective-permute-start(bf16[2048,256]{1,0:T(8,128)(2,1)S(1)} %slice.49), channel_id=1, source_target_pairs={{0,1},{1,0},{2,3},{3,2},{4,5},{5,4},{6,7},{7,6},{8,9},{9,8},{10,11... | collective-permute-start | bytes 3145736 | tf_op jit(solution)/shard_map/ppermute | solution.py:480
  31.1 8.9 %collective-permute-start.4 = (bf16[512,256]{1,0:T(8,128)(2,1)S(1)}, bf16[512,256]{1,0:T(8,128)(2,1)S(1)}, u32[]{:S(2)}, u32[]{:S(2)}) collective-permute-start(bf16[512,256]{1,0:T(8,128)(2,1)S(1)} %get-tuple-element.126), channel_id=1, source_target_pairs={{0,2},{1,3},{2,0},{3,1},{4,6},{5,7},{6,4},{7,5},{8,10},{9,11},{10,... | collective-permute-start | bytes 786440 | tf_op jit(solution)/shard_map/ppermute | solution.py:480
  33.0 8.3 %collective-permute-start.5 = (bf16[512,256]{1,0:T(8,128)(2,1)S(1)}, bf16[512,256]{1,0:T(8,128)(2,1)S(1)}, u32[]{:S(2)}, u32[]{:S(2)}) collective-permute-start(bf16[512,256]{1,0:T(8,128)(2,1)S(1)} %get-tuple-element.127), channel_id=1, source_target_pairs={{0,4},{4,0},{8,12},{12,8},{16,20},{20,16},{24,28},{28,24},{1,5},{5... | collective-permute-start | bytes 786440 | tf_op jit(solution)/shard_map/ppermute | solution.py:480
  41.4 5.1 %collective-permute-start.6 = (bf16[256,256]{1,0:T(8,128)(2,1)S(1)}, bf16[256,256]{1,0:T(8,128)(2,1)S(1)}, u32[]{:S(2)}, u32[]{:S(2)}) collective-permute-start(bf16[256,256]{1,0:T(8,128)(2,1)S(1)} %get-tuple-element.136), channel_id=1, source_target_pairs={{0,4},{4,0},{8,12},{12,8},{16,20},{20,16},{24,28},{28,24},{1,5},{5... | collective-permute-start | bytes 393224 | tf_op jit(solution)/shard_map/ppermute | solution.py:480
  43.0 5.0 %collective-permute-start.7 = (bf16[256,256]{1,0:T(8,128)(2,1)S(1)}, bf16[256,256]{1,0:T(8,128)(2,1)S(1)}, u32[]{:S(2)}, u32[]{:S(2)}) collective-permute-start(bf16[256,256]{1,0:T(8,128)(2,1)S(1)} %get-tuple-element.138), channel_id=1, source_target_pairs={{0,2},{1,3},{2,0},{3,1},{4,6},{5,7},{6,4},{7,5},{8,10},{9,11},{10,... | collective-permute-start | bytes 393224 | tf_op jit(solution)/shard_map/ppermute | solution.py:480
  48.0 5.0 %collective-permute-start.9 = (bf16[256,256]{1,0:T(8,128)(2,1)S(1)}, bf16[256,256]{1,0:T(8,128)(2,1)S(1)}, u32[]{:S(2)}, u32[]{:S(2)}) collective-permute-start(bf16[256,256]{1,0:T(8,128)(2,1)S(1)} %shard_map.292), channel_id=1, source_target_pairs={{0,8},{4,12},{8,0},{12,4},{16,24},{20,28},{24,16},{28,20},{1,9},{5... | collective-permute-start | bytes 393224 | tf_op jit(solution)/shard_map/ppermute | solution.py:480
  51.7 3.4 %collective-permute-start.8 = (bf16[1040,256]{1,0:T(8,128)(2,1)S(1)}, bf16[1040,256]{1,0:T(8,128)(2,1)S(1)}, u32[]{:S(2)}, u32[]{:S(2)}) collective-permute-start(bf16[1040,256]{1,0:T(8,128)(2,1)S(1)} %slice.56), channel_id=1, source_target_pairs={{0,1},{1,0},{2,3},{3,2},{4,5},{5,4},{6,7},{7,6},{8,9},{9,8},{10,11... | collective-permute-start | bytes 1597448 | tf_op jit(solution)/shard_map/ppermute | solution.py:480
  56.6 5.1 %collective-permute-start.12 = (bf16[208,256]{1,0:T(8,128)(2,1)S(1)}, bf16[208,256]{1,0:T(8,128)(2,1)S(1)}, u32[]{:S(2)}, u32[]{:S(2)}) collective-permute-start(bf16[208,256]{1,0:T(8,128)(2,1)S(1)} %shard_map.298), channel_id=1, source_target_pairs={{0,2},{1,3},{2,0},{3,1},{4,6},{5,7},{6,4},{7,5},{8,10},{9,11},{10,... | collective-permute-start | bytes 319496 | tf_op jit(solution)/shard_map/ppermute | solution.py:480
  57.2 9.0 %collective-permute-start.14 = (bf16[256,256]{1,0:T(8,128)(2,1)S(1)}, bf16[256,256]{1,0:T(8,128)(2,1)S(1)}, u32[]{:S(2)}, u32[]{:S(2)}) collective-permute-start(bf16[256,256]{1,0:T(8,128)(2,1)S(1)} %shard_map.293.after.refs_0_), channel_id=1, source_target_pairs={{0,16},{4,20},{8,24},{12,28},{16,0},{20,4},{24,8},{28,12},{1,17},{... | collective-permute-start | bytes 393224 | tf_op jit(solution)/shard_map/ppermute | solution.py:480
  59.8 17.1 %collective-permute-start.10 = (bf16[512,256]{1,0:T(8,128)(2,1)S(1)}, bf16[512,256]{1,0:T(8,128)(2,1)S(1)}, u32[]{:S(2)}, u32[]{:S(2)}) collective-permute-start(bf16[512,256]{1,0:T(8,128)(2,1)S(1)} %get-tuple-element.151), channel_id=1, source_target_pairs={{0,2},{1,3},{2,0},{3,1},{4,6},{5,7},{6,4},{7,5},{8,10},{9,11},{10,... | collective-permute-start | bytes 786440 | tf_op jit(solution)/shard_map/ppermute | solution.py:480
  61.8 5.2 %collective-permute-start.13 = (bf16[112,256]{1,0:T(8,128)(2,1)S(1)}, bf16[112,256]{1,0:T(8,128)(2,1)S(1)}, u32[]{:S(2)}, u32[]{:S(2)}) collective-permute-start(bf16[112,256]{1,0:T(8,128)(2,1)S(1)} %get-tuple-element.157), channel_id=1, source_target_pairs={{0,4},{4,0},{8,12},{12,8},{16,20},{20,16},{24,28},{28,24},{1,5},{5... | collective-permute-start | bytes 172040 | tf_op jit(solution)/shard_map/ppermute | solution.py:480
  66.2 5.2 %collective-permute-start.16 = (bf16[256,256]{1,0:T(8,128)(2,1)S(1)}, bf16[256,256]{1,0:T(8,128)(2,1)S(1)}, u32[]{:S(2)}, u32[]{:S(2)}) collective-permute-start(bf16[256,256]{1,0:T(8,128)(2,1)S(1)} %shard_map.300.refs_2_), channel_id=1, source_target_pairs={{0,8},{4,12},{8,0},{12,4},{16,24},{20,28},{24,16},{28,20},{1,9},{5... | collective-permute-start | bytes 393224 | tf_op jit(solution)/shard_map/ppermute | solution.py:480
  67.0 6.6 %collective-permute-start.15 = (bf16[112,256]{1,0:T(8,128)(2,1)S(1)}, bf16[112,256]{1,0:T(8,128)(2,1)S(1)}, u32[]{:S(2)}, u32[]{:S(2)}) collective-permute-start(bf16[112,256]{1,0:T(8,128)(2,1)S(1)} %shard_map.301.refs_2_.refs_0_), channel_id=1, source_target_pairs={{0,8},{4,12},{8,0},{12,4},{16,24},{20,28},{24,16},{28,20},{1,9},{5... | collective-permute-start | bytes 172040 | tf_op jit(solution)/shard_map/ppermute | solution.py:480
  71.4 6.7 %collective-permute-start.18 = (bf16[256,256]{1,0:T(8,128)(2,1)S(1)}, bf16[256,256]{1,0:T(8,128)(2,1)S(1)}, u32[]{:S(2)}, u32[]{:S(2)}) collective-permute-start(bf16[256,256]{1,0:T(8,128)(2,1)S(1)} %shard_map.302.refs_2_.refs_0_), channel_id=1, source_target_pairs={{0,4},{4,0},{8,12},{12,8},{16,20},{20,16},{24,28},{28,24},{1,5},{5... | collective-permute-start | bytes 393224 | tf_op jit(solution)/shard_map/ppermute | solution.py:480
  72.1 6.7 %collective-permute-start.19 = (bf16[256,256]{1,0:T(8,128)(2,1)S(1)}, bf16[256,256]{1,0:T(8,128)(2,1)S(1)}, u32[]{:S(2)}, u32[]{:S(2)}) collective-permute-start(bf16[256,256]{1,0:T(8,128)(2,1)S(1)} %shard_map.303.refs_3_.refs_0_), channel_id=1, source_target_pairs={{0,2},{1,3},{2,0},{3,1},{4,6},{5,7},{6,4},{7,5},{8,10},{9,11},{10,... | collective-permute-start | bytes 393224 | tf_op jit(solution)/shard_map/ppermute | solution.py:480
  73.7 6.7 %collective-permute-start.17 = (bf16[112,256]{1,0:T(8,128)(2,1)S(1)}, bf16[112,256]{1,0:T(8,128)(2,1)S(1)}, u32[]{:S(2)}, u32[]{:S(2)}) collective-permute-start(bf16[112,256]{1,0:T(8,128)(2,1)S(1)} %shard_map.304.after.refs_0_), channel_id=1, source_target_pairs={{0,16},{4,20},{8,24},{12,28},{16,0},{20,4},{24,8},{28,12},{1,17},{... | collective-permute-start | bytes 172040 | tf_op jit(solution)/shard_map/ppermute | solution.py:480
  78.2 8.3 %collective-permute-start.22 = (bf16[512,256]{1,0:T(8,128)(2,1)S(1)}, bf16[512,256]{1,0:T(8,128)(2,1)S(1)}, u32[]{:S(2)}, u32[]{:S(2)}) collective-permute-start(bf16[512,256]{1,0:T(8,128)(2,1)S(1)} %shard_map.306.refs_2_.refs_0_), channel_id=1, source_target_pairs={{0,2},{1,3},{2,0},{3,1},{4,6},{5,7},{6,4},{7,5},{8,10},{9,11},{10,... | collective-permute-start | bytes 786440 | tf_op jit(solution)/shard_map/ppermute | solution.py:480
  78.8 7.7 %collective-permute-start.23 = (bf16[512,256]{1,0:T(8,128)(2,1)S(1)}, bf16[512,256]{1,0:T(8,128)(2,1)S(1)}, u32[]{:S(2)}, u32[]{:S(2)}) collective-permute-start(bf16[512,256]{1,0:T(8,128)(2,1)S(1)} %shard_map.307.refs_3_.refs_2_), channel_id=1, source_target_pairs={{0,4},{4,0},{8,12},{12,8},{16,20},{20,16},{24,28},{28,24},{1,5},{5... | collective-permute-start | bytes 786440 | tf_op jit(solution)/shard_map/ppermute | solution.py:480
  80.4 6.1 %collective-permute-start.20 = (bf16[96,256]{1,0:T(8,128)(2,1)S(1)}, bf16[96,256]{1,0:T(8,128)(2,1)S(1)}, u32[]{:S(2)}, u32[]{:S(2)}) collective-permute-start(bf16[96,256]{1,0:T(8,128)(2,1)S(1)} %slice.69.refs_0_), channel_id=1, source_target_pairs={{0,4},{4,0},{8,12},{12,8},{16,20},{20,16},{24,28},{28,24},{1,5},{5... | collective-permute-start | bytes 147464 | tf_op jit(solution)/shard_map/ppermute | solution.py:480
  86.6 8.3 %collective-permute-start.25 = (bf16[2048,256]{1,0:T(8,128)(2,1)S(1)}, bf16[2048,256]{1,0:T(8,128)(2,1)S(1)}, u32[]{:S(2)}, u32[]{:S(2)}) collective-permute-start(bf16[2048,256]{1,0:T(8,128)(2,1)S(1)} %shard_map.310.refs_2_.mine), channel_id=1, source_target_pairs={{0,1},{1,0},{2,3},{3,2},{4,5},{5,4},{6,7},{7,6},{8,9},{9,8},{10,11... | collective-permute-start | bytes 3145736 | tf_op jit(solution)/shard_map/ppermute | solution.py:480
  86.7 5.2 %collective-permute-start.21 = (bf16[192,256]{1,0:T(8,128)(2,1)S(1)}, bf16[192,256]{1,0:T(8,128)(2,1)S(1)}, u32[]{:S(2)}, u32[]{:S(2)}) collective-permute-start(bf16[192,256]{1,0:T(8,128)(2,1)S(1)} %shard_map.309.refs_4_.refs_0_), channel_id=1, source_target_pairs={{0,2},{1,3},{2,0},{3,1},{4,6},{5,7},{6,4},{7,5},{8,10},{9,11},{10,... | collective-permute-start | bytes 294920 | tf_op jit(solution)/shard_map/ppermute | solution.py:480
  (19 other events, 79.0 us)

commit v2 on v1

--- a/solution.py
+++ b/solution.py
@@ -15,6 +15,7 @@
 LANES = 128
 WIDE = HEADS * LANES
 HUGE = -1e30
+TALL = HEAD_DIM + 16
 BF = jnp.bfloat16
 F32 = jnp.float32
 MIB = 1024 * 1024
@@ -69,7 +70,7 @@
         scratch_shapes=list(scratch),
         compiler_params=pltpu.CompilerParams(vmem_limit_bytes=limit * MIB),
         cost_estimate=pl.CostEstimate(
-            flops=microseconds * 10**9, bytes_accessed=1 * MIB, transcendentals=0
+            flops=microseconds * 10**9, bytes_accessed=0, transcendentals=0
         ),
     )
 
@@ -120,8 +121,9 @@
     return low(jnp.where((lanes >> 7) == rows, 1.0, 0.0))
 
 
-def start_kernel(me_ref, token):
-    token[...] = jnp.zeros_like(token)
+def start_kernel(me_ref, spot):
+    rows = lax.broadcasted_iota(jnp.int32, spot.shape, 0)
+    spot[...] = jnp.where(rows == 0, me_ref[0], me_ref[1])
 
 
 def project(rows_in, gain, code, wk_pad, wv_pad, wk_t, wv_t, at, normed, normed_t, k_aug, v_pad, kt, vt):
@@ -133,30 +135,83 @@
     normed_t[:, at : at + count] = flipped
     wide = low(dot(value, wk_pad))
     k_aug[at : at + count, :] = wide + jnp.concatenate([code] * HEADS, axis=1)
-    v_pad[at : at + count, :] = low(dot(value, wv_pad))
+    v_lane = lax.broadcasted_iota(jnp.int32, (1, WIDE), 1) & (LANES - 1)
+    v_ones = jnp.where((v_lane >= HEAD_DIM) & (v_lane < HEAD_DIM + 3), 1.0, 0.0)
+    v_pad[at : at + count, :] = low(dot(value, wv_pad) + v_ones)
     kt[:, at : at + count] = low(dot(wk_t, flipped))
-    vt[:, at : at + count] = low(dot(wv_t, flipped))
+    turned = low(dot(wv_t, flipped))
+    for h in range(HEADS):
+        vt[h * TALL : h * TALL + HEAD_DIM, at : at + count] = turned[h * HEAD_DIM : (h + 1) * HEAD_DIM]
+        vt[h * TALL + HEAD_DIM : (h + 1) * TALL, at : at + count] = jnp.ones((16, count), BF)
+
+
+def raw_attention(q_aug, k_aug, vt, part):
+    for h in range(HEADS):
+        lanes = slice(h * LANES, (h + 1) * LANES)
+        tall = slice(h * TALL, (h + 1) * TALL)
+        p = low(jnp.exp(dot_nt(k_aug[:, lanes], q_aug[:, lanes])))
+        part[tall, :] = dot(vt[tall, :], p)
+
+
+def exact_attention(q_aug, halves, self_rows, vt_own, scores, o_t, lse_out):
+    for h in range(HEADS):
+        lanes = slice(h * LANES, (h + 1) * LANES)
+        q_h = q_aug[:, lanes]
+        top = self_h = self_rows[h : h + 1]
+        at = 0
+        for k_half, _ in halves:
+            count = k_half.shape[0]
+            scores[at : at + count, :] = dot_nt(k_half[:, lanes], q_h)
+            top = jnp.maximum(top, jnp.max(scores[at : at + count, :], axis=0, keepdims=True))
+            at += count
+        p_self = jnp.exp(self_h - top)
+        total = p_self
+        acc = high(low(p_self)) * high(vt_own[h * TALL : h * TALL + HEAD_DIM, :])
+        at = 0
+        for k_half, vt_half in halves:
+            count = k_half.shape[0]
+            p = jnp.exp(scores[at : at + count, :] - top)
+            total = total + jnp.sum(p, axis=0, keepdims=True)
+            acc = acc + dot(vt_half[h * TALL : h * TALL + HEAD_DIM, :], low(p))
+            at += count
+        o_t[h * LANES : h * LANES + HEAD_DIM, :] = acc / total
+        lse_out[h : h + 1, :] = top + jnp.log(total)
+
+
+def placed(rows16, first):
+    upper = low(rows16)
+    rest = rows16 - high(upper)
+    middle = low(rest)
+    parts = (upper, middle, low(rest - high(middle)))
+    rows = lax.broadcasted_iota(jnp.int32, (16, WIDE), 0)
+    lanes = lax.broadcasted_iota(jnp.int32, (16, WIDE), 1)
+    total = 0.0
+    for i, piece in enumerate(parts):
+        picked = ((lanes >> 7) == rows) & ((lanes & (LANES - 1)) == first + i)
+        total = total + dot_tn(piece, low(jnp.where(picked, 1.0, 0.0)))
+    return low(total)
 
 
 def lane_codes(rows_code):
     picked = lax.broadcasted_iota(jnp.int32, (16, LANES), 1) - HEAD_DIM
-    picked = (picked == lax.broadcasted_iota(jnp.int32, (16, LANES), 0)) & (picked <= SEGS)
+    picked = (picked == lax.broadcasted_iota(jnp.int32, (16, LANES), 0)) & (picked <= SEGS + 3)
     return low(dot_tn(low(rows_code), low(jnp.where(picked, 1.0, 0.0))))
 
 
 def first_kernel(
     own_rows,
-    me_ref, seg, token, core_rows, tokens, valid, gain_one, wq, wk, wv, wo,
+    spot, seg, core_rows, tokens, valid, gain_one, wq, wk, wv, wo,
     wq_pad, wk_pad, wv_pad, wo_pad, wk_t, wv_t, codes, real, counted,
-    normed, normed_t, q_aug, k_aug, v_pad, kt, vt,
+    normed, normed_t, q_aug, k_aug, v_pad, kt, vt, part,
 ):
-    me = me_ref[0]
+    me = jnp.max(spot[0:1, :])
     for step in range(4):
         at = pl.multiple_of((me ^ step) * own_rows, own_rows)
         spread, inside = segment_rows(seg, at, own_rows)
         ok = valid[:, pl.ds(at, own_rows)] > 0
         code = jnp.where(inside, HUGE, 0.0)
         code = jnp.where(spread == SEGS, jnp.where(ok, 0.0, HUGE), code)
+        code = jnp.where(spread > SEGS, 1.0, code)
         codes[step * own_rows : (step + 1) * own_rows, :] = lane_codes(code)
         real[:, step * own_rows : (step + 1) * own_rows] = jnp.where(ok, 1.0, 0.0)
         counted[:, step * own_rows : (step + 1) * own_rows] = low(jnp.where(inside & ok, 1.0, 0.0))
@@ -174,21 +229,22 @@
             normed, normed_t, k_aug, v_pad, kt, vt,
         )
     spread, inside = segment_rows(seg, pl.multiple_of(me * own_rows, own_rows), own_rows)
-    own_code = lane_codes(jnp.where(inside, 0.0, 1.0))
+    own_code = lane_codes(jnp.where(inside | (spread > SEGS), 0.0, 1.0))
     scaled = low(dot(normed[:own_rows, :], wq_pad[...]) * 0.125)
     q_aug[...] = scaled + jnp.concatenate([own_code] * HEADS, axis=1)
+    raw_attention(q_aug, k_aug, vt, part)
 
 
 def forward_kernel(
     own_rows,
-    me_ref, y_rows, far_rows, codes, real, counted, tokens, cot,
+    spot, y_rows, far_rows, codes, real, counted, tokens, cot,
     gain_one, wk_pad, wv_pad, wo_pad, wk_t, wv_t,
     w_cross, b_cross, w_mix, w_ens1, gain_two, w_up, b_up, w_ens2,
-    normed_a, normed_ta, q_aug, k_a, v_a, kt_a, vt_a,
+    normed_a, normed_ta, q_aug, k_a, v_a, kt_a, vt_a, part_a,
     out_rows, d_first_out, dn_own, payload, vectors,
     normed_b, normed_tb, k_b, v_b, kt_b,
-    grad_att, lse_out, delta_out, pself_out, dself_out, seg_grad_out,
-    vt_b, scores, o_t,
+    q_back, grad_att, pself_out, dself_out, seg_grad_out,
+    vt_b, part_b, scores, o_t, lse_out,
 ):
     gain = gain_one[...]
     for step, rows_in in enumerate((y_rows[...], far_rows[:own_rows, :])):
@@ -210,25 +266,26 @@
     o_t[...] = jnp.zeros_like(o_t)
     lse_out[...] = jnp.zeros_like(lse_out)
     half_keys = 2 * own_rows
+    raw_attention(q_aug, k_b, vt_b, part_b)
+    vt_own = vt_a[:, :own_rows]
+    smallest, largest = jnp.inf, -jnp.inf
     for h in range(HEADS):
-        lanes = slice(h * LANES, (h + 1) * LANES)
-        rows_h = slice(h * HEAD_DIM, (h + 1) * HEAD_DIM)
-        q_h = q_aug[:, lanes]
-        top = jnp.where(own_real, HUGE, self_scores[h : h + 1])
-        self_h = top
-        for c, k_half in enumerate((k_a, k_b)):
-            part = dot_nt(k_half[:, lanes], q_h)
-            scores[c * half_keys : (c + 1) * half_keys, :] = part
-            top = jnp.maximum(top, jnp.max(part, axis=0, keepdims=True))
-        p_self = jnp.exp(self_h - top)
-        total = p_self
-        acc = high(low(p_self)) * high(vt_a[rows_h, :own_rows])
-        for c, vt_half in enumerate((vt_a, vt_b)):
-            p = jnp.exp(scores[c * half_keys : (c + 1) * half_keys, :] - top)
-            total = total + jnp.sum(p, axis=0, keepdims=True)
-            acc = acc + dot(vt_half[rows_h, :], low(p))
+        p_self = jnp.where(own_real, 0.0, jnp.exp(self_scores[h : h + 1]))
+        both = part_a[h * TALL : (h + 1) * TALL, :] + part_b[h * TALL : (h + 1) * TALL, :]
+        total = both[HEAD_DIM : HEAD_DIM + 1] + p_self
+        acc = both[:HEAD_DIM] + high(low(p_self)) * high(vt_own[h * TALL : h * TALL + HEAD_DIM])
         o_t[h * LANES : h * LANES + HEAD_DIM, :] = acc / total
-        lse_out[h : h + 1, :] = top + jnp.log(total)
+        lse_out[h : h + 1, :] = jnp.log(total)
+        smallest = jnp.minimum(smallest, total)
+        largest = jnp.maximum(largest, total)
+    fits = (jnp.min(smallest) > 1e-25) & (jnp.max(largest) < 1e30)
+
+    @pl.when(jnp.logical_not(fits))
+    def _():
+        self_rows = jnp.where(own_real, HUGE, self_scores)
+        exact_attention(q_aug, ((k_a, vt_a), (k_b, vt_b)), self_rows, vt_own, scores, o_t, lse_out)
+
+    q_back[...] = q_aug[...] + placed(-lse_out[...], HEAD_DIM + SEGS + 1)
     att = o_t[...].T
     att_low = low(att)
 
@@ -260,8 +317,8 @@
     slope = cdf + inner * jnp.exp(-0.5 * inner * inner) * 0.3989422804014327
     out_rows[...] = first + (dot(active, w_ens2[:FF, :]) + dot(normed_two, w_ens2[FF:, :]))
 
-    core, y_bit, x_bit, z_bit = bits_of(me_ref)
-    orders = (y_bit * 4 + x_bit * 2 + z_bit, x_bit * 4 + y_bit * 2 + z_bit)
+    core, y_bit, x_bit, z_bit = bits_of(spot)
+    order = y_bit * 8 + x_bit * 4 + z_bit * 2
     block = payload.shape[0] // 32
     place = [0]
 
@@ -270,9 +327,9 @@
         for i in range(middle // block):
             n = place[0]
             place[0] = n + 1
-            spot = (n // 8) * 8 + ((n % 8) ^ orders[n // 8])
+            place_at = n ^ order
             for side in range(2):
-                start = pl.multiple_of(((side ^ core) * 16 + spot) * block, block)
+                start = pl.multiple_of(((side ^ core) * 16 + place_at) * block, block)
                 first = side * middle + i * block
                 payload[pl.ds(start, block), :] = low(grad[first : first + block])
 
@@ -314,7 +371,7 @@
 
     d_att = high(grad_att[...])
     delta = head_sums(heads16, d_att * att)
-    delta_out[...] = delta
+    grad_att[...] = grad_att[...] + placed(-delta, HEAD_DIM)
     p_self = jnp.where(own_real, 0.0, jnp.exp(self_scores - lse_out[...]))
     dp_self = head_sums(heads16, d_att * high(v_own))
     pself_out[...] = low(p_self)
@@ -323,7 +380,7 @@
 
 def head_kernel(
     own_rows, h,
-    q_aug, k_a, k_b, v_a, v_b, kt_a, kt_b, grad_att, lse, delta, pself, dself, after_one, after_two,
+    q_back, k_a, k_b, v_a, v_b, kt_a, kt_b, grad_att, pself, dself, after_one, after_two,
     dk_out, dv_out, dq_out,
 ):
     half_keys = 2 * own_rows
@@ -331,15 +388,13 @@
     spread = low(jnp.where(row16 == h, 1.0, 0.0))
     lanes = slice(h * LANES, (h + 1) * LANES)
     rows_h = slice(h * HEAD_DIM, (h + 1) * HEAD_DIM)
-    q_h = q_aug[:, lanes]
+    q_h = q_back[:, lanes]
     g_h = grad_att[:, lanes]
-    lse_h = lse[h : h + 1, :]
-    delta_h = delta[h : h + 1, :]
     acc = high(dself[h : h + 1, :]) * high(kt_a[rows_h, :own_rows])
     for c, (k_half, v_half, kt_half) in enumerate(((k_a, v_a, kt_a), (k_b, v_b, kt_b))):
         at = slice(c * half_keys, (c + 1) * half_keys)
-        p = jnp.exp(dot_nt(k_half[:, lanes], q_h) - lse_h)
-        ds = low(p * (dot_nt(v_half[:, lanes], g_h) - delta_h))
+        p = jnp.exp(dot_nt(k_half[:, lanes], q_h))
+        ds = low(p * dot_nt(v_half[:, lanes], g_h))
         dv = dot(low(p), g_h)
         dk = dot(ds, q_h)
         if c == 0:
@@ -396,7 +451,7 @@
 
 def weights_kernel(
     own_rows,
-    me_ref,
+    spot,
     dk0, dk1, dk2, dk3, dv0, dv1, dv2, dv3, dq_rows, normed_ta, normed_tb, after,
     out,
 ):
@@ -414,7 +469,7 @@
             )
         )
 
-    core, y_bit, x_bit, _ = bits_of(me_ref)
+    core, y_bit, x_bit, _ = bits_of(spot)
     order = core * 4 + y_bit * 2 + x_bit
     part = D // 8
     for i, grad in enumerate(
@@ -436,9 +491,9 @@
     done[...] = after[:16, :]
 
 
-def unpack_kernel(me_ref, mine, other, after, attn_out, cross, mix, ens1, up, ens2):
-    core, y_bit, x_bit, z_bit = bits_of(me_ref)
-    orders = (y_bit * 4 + x_bit * 2 + z_bit, x_bit * 4 + y_bit * 2 + z_bit)
+def unpack_kernel(spot, mine, other, attn_out, cross, mix, ens1, up, ens2, done):
+    core, y_bit, x_bit, z_bit = bits_of(spot)
+    order = y_bit * 8 + x_bit * 4 + z_bit * 2
     block = mine.shape[0] // 16
     every = slice(None)
     jobs = [(ens2, 0, FF, every), (ens2, FF, D, every)]
@@ -448,18 +503,19 @@
     n = 0
     for to, first, count, columns in jobs:
         for i in range(count // 2 // block):
-            spot = (n // 8) * 8 + ((n % 8) ^ orders[n // 8])
+            place_at = n ^ order
             n += 1
             for side, source in ((core, mine), (1 - core, other)):
                 at = pl.multiple_of(first + side * (count // 2) + i * block, block)
-                value = source[pl.ds(pl.multiple_of(spot * block, block), block), :]
+                value = source[pl.ds(pl.multiple_of(place_at * block, block), block), :]
                 to[pl.ds(at, block), columns] = high(value)
+    done[...] = mine[:16, :]
 
 
 def unpack_small_kernel(
-    me_ref, mine, other, vec, gain_one, query, key, value, b_cross, gain_two, b_up
+    spot, mine, other, vec, after, gain_one, query, key, value, b_cross, gain_two, b_up
 ):
-    core, y_bit, x_bit, _ = bits_of(me_ref)
+    core, y_bit, x_bit, _ = bits_of(spot)
     order = y_bit * 2 + x_bit
     part = D // 8
     for side, source in ((core, mine), (1 - core, other)):
@@ -480,23 +536,20 @@
     return lax.ppermute(value, axis, [(i, i ^ step) for i in range(count)])
 
 
-def bits_of(me_ref):
-    module, batch = me_ref[0], me_ref[1]
+def bits_of(spot):
+    module, batch = jnp.max(spot[0:1, :]), jnp.max(spot[1:2, :])
     return module & 1, (module >> 1) & 1, batch & 1, (batch >> 1) & 1
 
 
-def sum_kernel(jobs, afters, *refs):
-    inputs, outs = refs[: 2 * len(jobs)], refs[2 * len(jobs) + afters :]
-    o = 0
-    for j, cuts in enumerate(jobs):
-        mine, got = inputs[2 * j], inputs[2 * j + 1]
-        for spans in cuts:
-            to = 0
-            for first, count in spans:
-                here = slice(first, first + count)
-                outs[o][to : to + count, :] = added(mine[here, :], got[here, :])
-                to += count
-            o += 1
+def sum_kernel(counts, afters, *refs):
+    inputs, outs = refs[: len(refs) - afters - len(counts)], refs[len(refs) - len(counts) :]
+    at = 0
+    for count, out in zip(counts, outs):
+        total = high(inputs[0][at : at + count, :])
+        for other in inputs[1:]:
+            total = total + high(other[at : at + count, :])
+        out[...] = low(total)
+        at += count
 
 
 def join_kernel(jobs, afters, *refs):
@@ -554,80 +607,77 @@
     keys = 2 * own
     row = ((1, D), F32)
     gain_row, valid_row = gain_one.reshape(1, D), valid.reshape(1, rows)
-    (token,) = call(start_kernel, [((8, LANES), F32)], [], "s", 4, 20)(me)
+    (spot,) = call(start_kernel, [((8, LANES), jnp.int32)], [], "s", 4, 20)(me)
     (
         wq_pad, wk_pad, wv_pad, wo_pad, wk_t, wv_t, codes, real, counted,
-        normed_a, normed_ta, q_aug, k_a, v_a, kt_a, vt_a,
+        normed_a, normed_ta, q_aug, k_a, v_a, kt_a, vt_a, part_a,
     ) = call(
         functools.partial(first_kernel, own),
         [
             ((D, WIDE), BF), ((D, WIDE), BF), ((D, WIDE), BF), ((WIDE, D), BF), square, square,
             ((rows, LANES), BF), ((1, rows), F32), ((16, rows), BF),
             ((keys, D), BF), ((D, keys), BF), ((own, WIDE), BF), ((keys, WIDE), BF), ((keys, WIDE), BF),
-            ((D, keys), BF), ((D, keys), BF),
+            ((D, keys), BF), ((HEADS * TALL, keys), BF), ((HEADS * TALL, own), F32),
         ],
-        [], "ss" + "v" * 9, 16, 5,
+        [], "vs" + "v" * 8, 16, 5,
     )(
-        me, seg_lengths, token, from_core, tokens, valid_row, gain_row, w_query, w_key, w_value, w_attn_out
+        spot, seg_lengths, from_core, tokens, valid_row, gain_row, w_query, w_key, w_value, w_attn_out
     )
     from_far = by_core(jnp.concatenate([from_y, normed_a[:16]], axis=0))
     (
         out_rows, d_first, dn_own, payload, vectors, normed_b, normed_tb, k_b, v_b, kt_b,
-        grad_att, lse, delta, pself, dself, seg_grad,
+        q_back, grad_att, pself, dself, seg_grad,
     ) = call(
         functools.partial(forward_kernel, own),
         [
             ((own, D), F32), ((own, D), F32), ((own, D), F32), ((16 * D, D), BF), ((16, D), F32),
             ((keys, D), BF), ((D, keys), BF), ((keys, WIDE), BF), ((keys, WIDE), BF), ((D, keys), BF),
-            ((own, WIDE), BF), ((16, own), F32), ((16, own), F32), ((16, own), BF), ((16, own), BF), ((16, D), F32),
+            ((own, WIDE), BF), ((own, WIDE), BF), ((16, own), BF), ((16, own), BF), ((16, D), F32),
         ],
-        [pltpu.VMEM((D, keys), BF), pltpu.VMEM((rows, own), F32), pltpu.VMEM((WIDE, own), F32)],
-        "s" + "v" * 28, 32, 18,
+        [
+            pltpu.VMEM((HEADS * TALL, keys), BF), pltpu.VMEM((HEADS * TALL, own), F32), pltpu.VMEM((rows, own), F32),
+            pltpu.VMEM((WIDE, own), F32), pltpu.VMEM((16, own), F32),
+        ],
+        "v" * 30, 32, 10,
     )(
-        me, from_y, from_far, codes, real, counted, tokens, cotangent, gain_row, wk_pad, wv_pad, wo_pad, wk_t, wv_t,
+        spot, from_y, from_far, codes, real, counted, tokens, cotangent, gain_row, wk_pad, wv_pad, wo_pad, wk_t, wv_t,
         w_cross, b_cross.reshape(1, D), w_mix, w_ens1, gain_two.reshape(1, D), w_up, b_up.reshape(1, FF), w_ens2,
-        normed_a, normed_ta, q_aug, k_a, v_a, kt_a, vt_a,
+        normed_a, normed_ta, q_aug, k_a, v_a, kt_a, vt_a, part_a,
     )
 
     def head(index, after_one, after_two):
         return call(
             functools.partial(head_kernel, own, index),
             [((rows, LANES), BF), ((rows, LANES), BF), ((HEAD_DIM, own), BF)],
-            [], "v" * 14, 16, 3,
+            [], "v" * 12, 16, 2,
         )(
-            q_aug, k_a, k_b, v_a, v_b, kt_a, kt_b, grad_att, lse, delta, pself, dself, after_one[:16], after_two[:16]
+            q_back, k_a, k_b, v_a, v_b, kt_a, kt_b, grad_att, pself, dself, after_one[:16], after_two[:16]
         )
 
-    def sums(jobs, pairs, *after):
-        outs = [((sum(count for _, count in spans), D), BF) for cuts in jobs for spans in cuts]
-        args = [value for pair in pairs for value in pair] + list(after)
-        body = functools.partial(sum_kernel, jobs, len(after))
-        return call(body, outs, [], "v" * len(args), 8, 1)(*args)
-
-    def joined(parts, *after):
+    def summed(counts, parts, *after, cost=0):
+        outs = [((count, D), BF) for count in counts]
+        args = list(parts) + list(after)
+        body = functools.partial(sum_kernel, counts, len(after))
+        return call(body, outs, [], "v" * len(args), 8, cost)(*args)
+
+    def joined(parts, *after, cost=0):
         count = sum(part.shape[0] for part in parts)
         body = functools.partial(join_kernel, len(parts), len(after))
         args = list(parts) + list(after)
-        return call(body, [((count, D), BF)], [], "v" * len(args), 8, 1)(*args)[0]
+        return call(body, [((count, D), BF)], [], "v" * len(args), 8, cost)(*args)[0]
+
+    def by_both(value):
+        pairs = [(i, i ^ (n_module + 2)) for i in range(n_batch * n_module)]
+        return lax.ppermute(value, ("batch", "module"), pairs)
 
     size = payload.shape[0] // 8
-    got = by_core(payload[4 * size :])
-    dk0, dv0, dq0 = head(0, lse, lse)
-    quarters = [[(i * size, size)] for i in range(4)]
-    a, a_send, b, b_send = sums([quarters], [(payload, got)])
-    dk1, dv1, dq1 = head(1, a, dq0)
-    dk2, dv2, dq2 = head(2, b, dq1)
-    a_got, b_got = by_y(a_send), by_batch(b_send, 1)
-    halves = [[(0, size // 2)], [(size // 2, size // 2)]]
-    a, a_send, b, b_send = sums([halves] * 2, [(a, a_got), (b, b_got)])
-    dk3, dv3, dq3 = head(3, a, dq2)
-    a_got, b_got = by_batch(a_send, 1), by_y(b_send)
-    eighth = size // 4
-    eighths = [[(0, eighth)], [(eighth, eighth)]]
-    a, a_send, b, b_send = sums([eighths] * 2, [(a, a_got), (b, b_got)])
-    ab, ab_send = joined([a, b]), joined([a_send, b_send])
-    ab_got = by_batch(ab_send, 2)
-
+    big_got = by_core(payload[4 * size :])
+    dk0, dv0, dq0 = head(0, pself, pself)
+    mine, to_x, to_y, to_both = summed([size] * 4, [payload, big_got])
+    got = (by_batch(to_x, 1), by_y(to_y), by_both(to_both))
+    dk1, dv1, dq1 = head(1, mine, dq0)
+    dk2, dv2, dq2 = head(2, to_x, dq1)
+    dk3, dv3, dq3 = head(3, to_y, dq2)
     steps = [1 << place for place in range(1, n_batch.bit_length() - 1)]
     part = D // 8
     count = 2 * own + 16
@@ -637,64 +687,56 @@
         [pltpu.VMEM((rows, D), F32)],
         "v" * 23, 16, 3,
     )(
-        dk0, dk1, dk2, dk3, dv0, dv1, dv2, dv3, dq0, dq1, dq2, dq3, ab, normed_a, normed_b, counted, seg_grad, dn_own,
+        dk0, dk1, dk2, dk3, dv0, dv1, dv2, dv3, dq0, dq1, dq2, dq3, mine, normed_a, normed_b, counted, seg_grad, dn_own,
         gain_row, w_query, wk_pad, wv_pad, vectors,
     )
     shared_got = by_core(shared[count:])
-    every = [[[(0, 2 * eighth)]]]
-    (ab,) = sums(every, [(ab, ab_got)], shared)
-    ab_got = by_batch(ab, steps[1]) if len(steps) > 1 else ab
-    (q,) = call(functools.partial(weights_kernel, own), [((24 * part, D), BF)], [], "s" + "v" * 12, 16, 3)(
-        me, dk0, dk1, dk2, dk3, dv0, dv1, dv2, dv3, dq_rows, normed_ta, normed_tb, ab
+    half = size // 2
+    ab, ab_send = summed([half] * 2, [mine, *got], shared)
+    ab_got = by_batch(ab_send, steps[0])
+    (q,) = call(functools.partial(weights_kernel, own), [((24 * part, D), BF)], [], "v" * 13, 16, 3)(
+        spot, dk0, dk1, dk2, dk3, dv0, dv1, dv2, dv3, dq_rows, normed_ta, normed_tb, ab
     )
     q_got = by_core(q[12 * part :])
-    dn, dn_send, vec = sums([[[(0, own)], [(own, own)], [(2 * own, 16)]]], [(shared, shared_got)], q)
-    q, q_send = sums([[[(0, 6 * part)], [(6 * part, 6 * part)]]], [(q, q_got)], vec)
-    q_got = by_y(joined([q_send, vec]))
+    (ab,) = summed([half], [ab, ab_got], q, cost=1)
+    ab_got = by_batch(ab, steps[1]) if len(steps) > 1 else ab
+    dn, dn_send, vec = summed([own, own, 16], [shared, shared_got], q)
     dn_got = by_y(dn_send)
-    six = 6 * part
-    q, q_send = sums(
-        [[[(0, 3 * part), (six, 16)], [(3 * part, 3 * part + 16)]]], [(joined([q, vec]), q_got)]
-    )
-    q_got = by_batch(q_send, 1)
+    grad_tokens, done = call(
+        finish_kernel, [((own, D), F32), ((16, D), BF)], [], "v" * 6, 16, 6
+    )(dn, dn_got, tokens, d_first, gain_row, ab)
+    blocks = summed([3 * part] * 4, [q, q_got], ab)
+    q, *sends = [joined([block, vec]) for block in blocks]
+    q_got = (by_batch(sends[0], 1), by_y(sends[1]), by_both(sends[2]))
     for i in range(1, len(steps)):
-        (ab,) = sums(every, [(ab, ab_got)], q)
+        (ab,) = summed([half], [ab, ab_got], sends[2], done, cost=4)
         if i + 1 < len(steps):
             ab_got = by_batch(ab, steps[i + 1])
     ab_got = by_batch(ab, steps[0])
-    whole = [[[(0, 3 * part + 16)]]]
-    (q,) = sums(whole, [(q, q_got)], ab)
+    rows_q = 3 * part + 16
+    (q,) = summed([rows_q], [q, *q_got], ab, cost=3)
     q_got = by_batch(q, steps[0])
-    a = joined([ab[:eighth], ab_got[:eighth]], q)
-    b = joined([ab[eighth:], ab_got[eighth:]], q)
-    a_got, b_got = by_batch(a, 1), by_y(b)
+    mine = joined([ab, ab_got], q, cost=2)
+    got = (by_batch(mine, 1), by_y(mine), by_both(mine))
+    (q,) = summed([rows_q], [q, q_got], mine, cost=3)
     for step in steps[1:]:
-        (q,) = sums(whole, [(q, q_got)], a, b)
         q_got = by_batch(q, step)
-    grad_tokens, done = call(
-        finish_kernel, [((own, D), F32), ((16, D), BF)], [], "v" * 6, 16, 2
-    )(dn, dn_got, tokens, d_first, gain_row, q)
-    a = joined([a, a_got], done)
-    b = joined([b, b_got], done)
-    a_got, b_got = by_y(a), by_batch(b, 1)
-    (q,) = sums(whole, [(q, q_got)], a, b)
+        (q,) = summed([rows_q], [q, q_got], cost=4)
     q, vec = q[: 3 * part], q[3 * part :]
-    q_got = by_batch(q, 1)
-    q = joined([q, q_got])
-    q_got = by_y(q)
-    big = joined([a, a_got, b, b_got], q)
+    q_got = (by_batch(q, 1), by_y(q), by_both(q))
+    big = joined([mine, *got], cost=5)
     big_got = by_core(big)
-    q = joined([q, q_got], big)
+    q = joined([q, *q_got], cost=8)
     q_got = by_core(q)
     wide = ((D, D), F32)
-    attn_out, cross, mix, ens1, up, ens2 = call(
+    attn_out, cross, mix, ens1, up, ens2, done = call(
         unpack_kernel,
-        [wide, wide, wide, ((4 * D, D), F32), ((D, FF), F32), ((FF + D, D), F32)],
-        [], "svvv", 16, 3,
-    )(me, big, big_got, q)
+        [wide, wide, wide, ((4 * D, D), F32), ((D, FF), F32), ((FF + D, D), F32), ((16, D), BF)],
+        [], "vvv", 16, 3,
+    )(spot, big, big_got)
     gain_one_g, query, key, value, b_cross_g, gain_two_g, b_up_g = call(
-        unpack_small_kernel, [row, wide, wide, wide, row, row, ((1, FF), F32)], [], "svvv", 16, 1
-    )(me, q, q_got, vec)
+        unpack_small_kernel, [row, wide, wide, wide, row, row, ((1, FF), F32)], [], "vvvvv", 16, 2
+    )(spot, q, q_got, vec, done)
     return (
         out_rows, grad_tokens, gain_one_g.reshape(D), query, key, value, attn_out, cross, b_cross_g.reshape(D), mix,
         ens1, gain_two_g.reshape(D), up, b_up_g.reshape(FF), ens2,

time: 97.8 us -> 87.7 us (0.90)
  waiting for transfers between devices: 27.6 us -> 18.2 us
  Pallas kernels: 40.5 us -> 37.5 us
  starting transfers between devices: 27.4 us -> 29.7 us
    ppermute x26 -> x22, waiting for transfers between devices: 27.6 us -> 12.8 us  [swap(): return lax.ppermute(value, axis, [(i, i ^ step) for i in range(count)])]
    ppermute x0 -> x4, starting transfers between devices: none -> 6.13 us  [by_both(): return lax.ppermute(value, ('batch', 'module'), pairs)]
    ppermute x0 -> x4, waiting for transfers between devices: none -> 5.41 us  [by_both(): return lax.ppermute(value, ('batch', 'module'), pairs)]
    ppermute x26 -> x22, starting transfers between devices: 27.4 us -> 23.6 us  [swap(): return lax.ppermute(value, axis, [(i, i ^ step) for i in range(count)])]
    pallas_call x1, Pallas kernels: 15.2 us -> 12 us  [shards(): call(functools.partial(forward_kernel, own), [((own, D), F32), ((own, D),...]
    pallas_call x1, Pallas kernels: 3.15 us -> 4.68 us  [shards(): call(functools.partial(first_kernel, own), [((D, WIDE), BF), ((D, WIDE),...]
    pallas_call x24 -> x18, Pallas kernels: 2.72 us -> 2.6 us  [the longest x1 1.25 us: shards(): call(finish_kernel, [((own, D), F32), ((16, D), BF)], [], 'v' * 6, 16, 6)]
  transfers between devices with their start and end apart: 26 -> 26, of which waited for: 12 -> 13; matrix products, arithmetic and copies ran while one was open for 0% -> 0% of each run, Pallas kernels for 23% -> 27%
where the time goes in v2:
time: 87.7 us; the launch traced here: 87.4 us
  Pallas kernels  37.5 us (43%)
  starting transfers between devices  29.7 us (34%)
  waiting for transfers between devices  18.2 us (21%)
  between operations  1.12 us (1%)
    ppermute x22, starting transfers between devices, swap(): return lax.ppermute(value, axis, [(i, i ^ step) for i in range(count)])  23.6 us
    ppermute x22, waiting for transfers between devices, swap(): return lax.ppermute(value, axis, [(i, i ^ step) for i in range(count)])  12.8 us
    pallas_call x1, Pallas kernels, shards(): call(functools.partial(forward_kernel, own), [((own, D), F32), ((own, D),...  12 us
    pallas_call x4, Pallas kernels, head(): call(functools.partial(head_kernel, own, index), [((rows, LANES), BF), ((...  11.4 us
    ppermute x4, starting transfers between devices, by_both(): return lax.ppermute(value, ('batch', 'module'), pairs)  6.13 us
    ppermute x4, waiting for transfers between devices, by_both(): return lax.ppermute(value, ('batch', 'module'), pairs)  5.41 us
    pallas_call x1, Pallas kernels, shards(): call(functools.partial(first_kernel, own), [((D, WIDE), BF), ((D, WIDE),...  4.68 us
    pallas_call x1, Pallas kernels, shards(): call(unpack_kernel, [wide, wide, wide, ((4 * D, D), F32), ((D, FF), F32),...  2.22 us
  transfers between devices with their start and end apart: 26, of which 13 were waited for; matrix products, arithmetic and copies ran while one was open for 0% of the time, Pallas kernels for 27%

profile of v2, /device:TPU:0, one launch (start us, length us, event | category | flops | bytes accessed | tf_op | source)
XLA Modules:
  0.0 87.4 jit_solution(3517328920167249169)
XLA Ops:
  1.2 2.6 %collective-permute-start = (bf16[512,256]{1,0:T(8,128)(2,1)}, bf16[512,256]{1,0:T(8,128)(2,1)S(1)}, u32[]{:S(2)}, u32[]{:S(2)}) collective-permute-start(bf16[512,256]{1,0:T(8,128)(2,1)} %tokens.5), channel_id=1, source_target_pairs={{0,2},{1,3},{2,0},{3,1},{4,6},{5,7},{6,4},{7,5},{8,10},{9,11},{10,... | collective-permute-start | bytes 786440 | tf_op jit(solution)/shard_map/ppermute | solution.py:536
  5.1 4.7 %shard_map.281 = (bf16[256,512]{1,0:T(8,128)(2,1)}, bf16[256,512]{1,0:T(8,128)(2,1)S(1)}, bf16[256,512]{1,0:T(8,128)(2,1)S(1)}, bf16[512,256]{1,0:T(8,128)(2,1)S...) custom-call(s32[8,128]{1,0:T(8,128)S(1)} %shard_map.280.spot, ...), custom_call_target="tpu_custom_call" | custom-call | flops 5000000000 | tf_op jit(solution)/shard_map/pallas_call | solution.py:614
  12.6 12.0 %shard_map.282 = (f32[512,256]{1,0:T(8,128)}, f32[512,256]{1,0:T(8,128)S(1)}, f32[512,256]{1,0:T(8,128)S(1)}, bf16[4096,256]{1,0:T(8,128)(2,1)S(1)}, f32[16,256]...) custom-call(s32[8,128]{1,0:T(8,128)S(1)} %shard_map.280.spot, ...), custom_call_target="tpu_custom_call" | custom-call | flops 10000000000 | tf_op jit(solution)/shard_map/pallas_call | solution.py:630
  24.9 2.8 %shard_map.283 = (bf16[2048,128]{1,0:T(8,128)(2,1)S(1)}, bf16[2048,128]{1,0:T(8,128)(2,1)S(1)}, bf16[64,512]{1,0:T(8,128)(2,1)S(1)}) custom-call(bf16[512,512]{1,0:T(8,128)(2,1)S(1)} %get-tuple-element.106.q_back, bf16[1024,512]{1,0:T(8,128)(2,1)S(1)} %get-tuple-element.100.k_a, bf16[1024,512]{1,0:T(8,128)(2,1)S(1)} %get-tuple-element.107.k_b, ...), custom_call_target="tpu_custom_call" | custom-call | flops 2000000000 | tf_op jit(solution)/shard_map/pallas_call | solution.py:649
  27.9 1.8 %collective-permute-start.5 = (bf16[512,256]{1,0:T(8,128)(2,1)S(1)}, bf16[512,256]{1,0:T(8,128)(2,1)S(1)}, u32[]{:S(2)}, u32[]{:S(2)}) collective-permute-start(bf16[512,256]{1,0:T(8,128)(2,1)S(1)} %get-tuple-element.118), channel_id=1, source_target_pairs={{0,4},{4,0},{8,12},{12,8},{16,20},{20,16},{24,28},{28,24},{1,5},{5... | collective-permute-start | bytes 786440 | tf_op jit(solution)/shard_map/ppermute | solution.py:536
  31.5 2.8 %shard_map.285 = (bf16[2048,128]{1,0:T(8,128)(2,1)S(1)}, bf16[2048,128]{1,0:T(8,128)(2,1)S(1)}, bf16[64,512]{1,0:T(8,128)(2,1)S(1)}) custom-call(bf16[512,512]{1,0:T(8,128)(2,1)S(1)} %get-tuple-element.106.q_back, bf16[1024,512]{1,0:T(8,128)(2,1)S(1)} %get-tuple-element.100.k_a, bf16[1024,512]{1,0:T(8,128)(2,1)S(1)} %get-tuple-element.107.k_b, ...), custom_call_target="tpu_custom_call" | custom-call | flops 2000000000 | tf_op jit(solution)/shard_map/pallas_call | solution.py:649
  34.3 3.1 %shard_map.286 = (bf16[2048,128]{1,0:T(8,128)(2,1)S(1)}, bf16[2048,128]{1,0:T(8,128)(2,1)S(1)}, bf16[64,512]{1,0:T(8,128)(2,1)S(1)}) custom-call(bf16[512,512]{1,0:T(8,128)(2,1)S(1)} %get-tuple-element.106.q_back, bf16[1024,512]{1,0:T(8,128)(2,1)S(1)} %get-tuple-element.100.k_a, bf16[1024,512]{1,0:T(8,128)(2,1)S(1)} %get-tuple-element.107.k_b, ...), custom_call_target="tpu_custom_call" | custom-call | flops 2000000000 | tf_op jit(solution)/shard_map/pallas_call | solution.py:649
  37.4 2.8 %shard_map.287 = (bf16[2048,128]{1,0:T(8,128)(2,1)S(1)}, bf16[2048,128]{1,0:T(8,128)(2,1)S(1)}, bf16[64,512]{1,0:T(8,128)(2,1)S(1)}) custom-call(bf16[512,512]{1,0:T(8,128)(2,1)S(1)} %get-tuple-element.106.q_back, bf16[1024,512]{1,0:T(8,128)(2,1)S(1)} %get-tuple-element.100.k_a, bf16[1024,512]{1,0:T(8,128)(2,1)S(1)} %get-tuple-element.107.k_b, ...), custom_call_target="tpu_custom_call" | custom-call | flops 2000000000 | tf_op jit(solution)/shard_map/pallas_call | solution.py:649
  40.2 2.0 %shard_map.288 = (bf16[2080,256]{1,0:T(8,128)(2,1)S(1)}, bf16[512,256]{1,0:T(8,128)(2,1)S(1)}) custom-call(bf16[2048,128]{1,0:T(8,128)(2,1)S(1)} %get-tuple-element.113.dk0, bf16[2048,128]{1,0:T(8,128)(2,1)S(1)} %get-tuple-element.117.dk1, bf16[2048,128]{1,0:T(8,128)(2,1)S(1)} %get-tuple-element.120.dk2, bf16[2048,128]{1,0:T(8,128)(2,1)S(1)} %get-tuple-element.123.dk3, ...), custom_call_target="tpu_custom_call" | custom-call | flops 3000000000 | tf_op jit(solution)/shard_map/pallas_call | solution.py:684
  45.4 1.6 %collective-permute-start.8 = (bf16[512,256]{1,0:T(8,128)(2,1)S(1)}, bf16[512,256]{1,0:T(8,128)(2,1)S(1)}, u32[]{:S(2)}, u32[]{:S(2)}) collective-permute-start(bf16[512,256]{1,0:T(8,128)(2,1)S(1)} %get-tuple-element.139), channel_id=1, source_target_pairs={{0,2},{1,3},{2,0},{3,1},{4,6},{5,7},{6,4},{7,5},{8,10},{9,11},{10,... | collective-permute-start | bytes 786440 | tf_op jit(solution)/shard_map/ppermute | solution.py:536
  47.0 1.6 %collective-permute-start.9 = (bf16[256,256]{1,0:T(8,128)(2,1)S(1)}, bf16[256,256]{1,0:T(8,128)(2,1)S(1)}, u32[]{:S(2)}, u32[]{:S(2)}) collective-permute-start(bf16[256,256]{1,0:T(8,128)(2,1)S(1)} %get-tuple-element.141), channel_id=1, source_target_pairs={{0,8},{4,12},{8,0},{12,4},{16,24},{20,28},{24,16},{28,20},{1,9},{5... | collective-permute-start | bytes 393224 | tf_op jit(solution)/shard_map/ppermute | solution.py:536
  48.6 3.3 %collective-permute-done.9.refs_1_ = bf16[256,256]{1,0:T(8,128)(2,1)S(1)} collective-permute-done((bf16[256,256]{1,0:T(8,128)(2,1)S(1)}, bf16[256,256]{1,0:T(8,128)(2,1)S(1)}, u32[]{:S(2)}, u32[]{:S(2)}) %collective-permute-start.9) | collective-permute-done | bytes 131104 | tf_op jit(solution)/shard_map/ppermute | solution.py:536
  52.0 2.7 %collective-permute-start.14 = (bf16[256,256]{1,0:T(8,128)(2,1)S(1)}, bf16[256,256]{1,0:T(8,128)(2,1)S(1)}, u32[]{:S(2)}, u32[]{:S(2)}) collective-permute-start(bf16[256,256]{1,0:T(8,128)(2,1)S(1)} %shard_map.292.after.refs_2_.refs_0_), channel_id=1, source_target_pairs={{0,16},{4,20},{8,24},{12,28},{16,0},{20,4},{24,8},{28,12},{1,17},{... | collective-permute-start | bytes 393224 | tf_op jit(solution)/shard_map/ppermute | solution.py:536
  56.5 1.7 %collective-permute-start.13 = (bf16[112,256]{1,0:T(8,128)(2,1)S(1)}, bf16[112,256]{1,0:T(8,128)(2,1)S(1)}, u32[]{:S(2)}, u32[]{:S(2)}) collective-permute-start(bf16[112,256]{1,0:T(8,128)(2,1)S(1)} %shard_map.298.refs_2_), channel_id=1, source_target_pairs={{0,6},{1,7},{2,4},{3,5},{4,2},{5,3},{6,0},{7,1},{8,14},{9,15},{10,... | collective-permute-start | bytes 172040 | tf_op jit(solution)/shard_map/ppermute | solution.py:671
  59.6 1.6 %collective-permute-start.16 = (bf16[256,256]{1,0:T(8,128)(2,1)S(1)}, bf16[256,256]{1,0:T(8,128)(2,1)S(1)}, u32[]{:S(2)}, u32[]{:S(2)}) collective-permute-start(bf16[256,256]{1,0:T(8,128)(2,1)S(1)} %shard_map.299.refs_4_.refs_0_), channel_id=1, source_target_pairs={{0,8},{4,12},{8,0},{12,4},{16,24},{20,28},{24,16},{28,20},{1,9},{5... | collective-permute-start | bytes 393224 | tf_op jit(solution)/shard_map/ppermute | solution.py:536
  61.7 1.6 %collective-permute-start.15 = (bf16[112,256]{1,0:T(8,128)(2,1)S(1)}, bf16[112,256]{1,0:T(8,128)(2,1)S(1)}, u32[]{:S(2)}, u32[]{:S(2)}) collective-permute-start(bf16[112,256]{1,0:T(8,128)(2,1)S(1)} %shard_map.300.refs_2_.refs_0_), channel_id=1, source_target_pairs={{0,8},{4,12},{8,0},{12,4},{16,24},{20,28},{24,16},{28,20},{1,9},{5... | collective-permute-start | bytes 172040 | tf_op jit(solution)/shard_map/ppermute | solution.py:536
  66.0 1.9 %collective-permute-start.23 = (bf16[512,256]{1,0:T(8,128)(2,1)S(1)}, bf16[512,256]{1,0:T(8,128)(2,1)S(1)}, u32[]{:S(2)}, u32[]{:S(2)}) collective-permute-start(bf16[512,256]{1,0:T(8,128)(2,1)S(1)} %shard_map.301.refs_2_.refs_0_), channel_id=1, source_target_pairs={{0,2},{1,3},{2,0},{3,1},{4,6},{5,7},{6,4},{7,5},{8,10},{9,11},{10,... | collective-permute-start | bytes 786440 | tf_op jit(solution)/shard_map/ppermute | solution.py:536
  68.2 2.7 %collective-permute-start.17 = (bf16[112,256]{1,0:T(8,128)(2,1)S(1)}, bf16[112,256]{1,0:T(8,128)(2,1)S(1)}, u32[]{:S(2)}, u32[]{:S(2)}) collective-permute-start(bf16[112,256]{1,0:T(8,128)(2,1)S(1)} %shard_map.302.refs_0_), channel_id=1, source_target_pairs={{0,16},{4,20},{8,24},{12,28},{16,0},{20,4},{24,8},{28,12},{1,17},{... | collective-permute-start | bytes 172040 | tf_op jit(solution)/shard_map/ppermute | solution.py:536
  70.9 2.3 %collective-permute-done.24.refs_3_ = bf16[512,256]{1,0:T(8,128)(2,1)S(1)} collective-permute-done((bf16[512,256]{1,0:T(8,128)(2,1)S(1)}, bf16[512,256]{1,0:T(8,128)(2,1)S(1)}, u32[]{:S(2)}, u32[]{:S(2)}) %collective-permute-start.24) | collective-permute-done | bytes 262176 | tf_op jit(solution)/shard_map/ppermute | solution.py:671
  73.2 2.5 %collective-permute-done.23.refs_2_ = bf16[512,256]{1,0:T(8,128)(2,1)S(1)} collective-permute-done((bf16[512,256]{1,0:T(8,128)(2,1)S(1)}, bf16[512,256]{1,0:T(8,128)(2,1)S(1)}, u32[]{:S(2)}, u32[]{:S(2)}) %collective-permute-start.23) | collective-permute-done | bytes 262176 | tf_op jit(solution)/shard_map/ppermute | solution.py:536
  76.5 2.7 %collective-permute-start.20 = (bf16[96,256]{1,0:T(8,128)(2,1)S(1)}, bf16[96,256]{1,0:T(8,128)(2,1)S(1)}, u32[]{:S(2)}, u32[]{:S(2)}) collective-permute-start(bf16[96,256]{1,0:T(8,128)(2,1)S(1)} %slice.49.refs_0_), channel_id=1, source_target_pairs={{0,6},{1,7},{2,4},{3,5},{4,2},{5,3},{6,0},{7,1},{8,14},{9,15},{10,... | collective-permute-start | bytes 147464 | tf_op jit(solution)/shard_map/ppermute | solution.py:671
  80.1 1.6 %collective-permute-done.20.refs_3_ = bf16[96,256]{1,0:T(8,128)(2,1)S(1)} collective-permute-done((bf16[96,256]{1,0:T(8,128)(2,1)S(1)}, bf16[96,256]{1,0:T(8,128)(2,1)S(1)}, u32[]{:S(2)}, u32[]{:S(2)}) %collective-permute-start.20) | collective-permute-done | bytes 49184 | tf_op jit(solution)/shard_map/ppermute | solution.py:671
  81.7 1.7 %collective-permute-done.19.refs_2_ = bf16[96,256]{1,0:T(8,128)(2,1)S(1)} collective-permute-done((bf16[96,256]{1,0:T(8,128)(2,1)S(1)}, bf16[96,256]{1,0:T(8,128)(2,1)S(1)}, u32[]{:S(2)}, u32[]{:S(2)}) %collective-permute-start.19) | collective-permute-done | bytes 49184 | tf_op jit(solution)/shard_map/ppermute | solution.py:536
  84.1 2.2 %shard_map.306 = (f32[256,256]{1,0:T(8,128)}, f32[256,256]{1,0:T(8,128)}, f32[256,256]{1,0:T(8,128)}, f32[1024,256]{1,0:T(8,128)}, f32[256,1024]{1,0:T(8,128)}, ...) custom-call(s32[8,128]{1,0:T(8,128)S(1)} %shard_map.280.spot, bf16[2048,256]{1,0:T(8,128)(2,1)S(1)} %shard_map.305.mine, ...), custom_call_target="tpu_custom_call" | custom-call | flops 3000000000 | tf_op jit(solution)/shard_map/pallas_call | solution.py:732
  (104 shorter events, 20.1 us)
Async XLA Ops:
  0.6 3.8 %collective-permute-start.1 = (bf16[512,256]{1,0:T(8,128)(2,1)}, bf16[512,256]{1,0:T(8,128)(2,1)S(1)}, u32[]{:S(2)}, u32[]{:S(2)}) collective-permute-start(bf16[512,256]{1,0:T(8,128)(2,1)} %tokens.5), channel_id=1, source_target_pairs={{0,1},{1,0},{2,3},{3,2},{4,5},{5,4},{6,7},{7,6},{8,9},{9,8},{10,11... | collective-permute-start | bytes 786440 | tf_op jit(solution)/shard_map/ppermute | solution.py:536
  1.2 9.7 %collective-permute-start = (bf16[512,256]{1,0:T(8,128)(2,1)}, bf16[512,256]{1,0:T(8,128)(2,1)S(1)}, u32[]{:S(2)}, u32[]{:S(2)}) collective-permute-start(bf16[512,256]{1,0:T(8,128)(2,1)} %tokens.5), channel_id=1, source_target_pairs={{0,2},{1,3},{2,0},{3,1},{4,6},{5,7},{6,4},{7,5},{8,10},{9,11},{10,... | collective-permute-start | bytes 786440 | tf_op jit(solution)/shard_map/ppermute | solution.py:536
  24.7 3.0 %collective-permute-start.3 = (bf16[2048,256]{1,0:T(8,128)(2,1)S(1)}, bf16[2048,256]{1,0:T(8,128)(2,1)S(1)}, u32[]{:S(2)}, u32[]{:S(2)}) collective-permute-start(bf16[2048,256]{1,0:T(8,128)(2,1)S(1)} %slice.37), channel_id=1, source_target_pairs={{0,1},{1,0},{2,3},{3,2},{4,5},{5,4},{6,7},{7,6},{8,9},{9,8},{10,11... | collective-permute-start | bytes 3145736 | tf_op jit(solution)/shard_map/ppermute | solution.py:536
  27.9 15.6 %collective-permute-start.5 = (bf16[512,256]{1,0:T(8,128)(2,1)S(1)}, bf16[512,256]{1,0:T(8,128)(2,1)S(1)}, u32[]{:S(2)}, u32[]{:S(2)}) collective-permute-start(bf16[512,256]{1,0:T(8,128)(2,1)S(1)} %get-tuple-element.118), channel_id=1, source_target_pairs={{0,4},{4,0},{8,12},{12,8},{16,20},{20,16},{24,28},{28,24},{1,5},{5... | collective-permute-start | bytes 786440 | tf_op jit(solution)/shard_map/ppermute | solution.py:536
  29.7 13.9 %collective-permute-start.6 = (bf16[512,256]{1,0:T(8,128)(2,1)S(1)}, bf16[512,256]{1,0:T(8,128)(2,1)S(1)}, u32[]{:S(2)}, u32[]{:S(2)}) collective-permute-start(bf16[512,256]{1,0:T(8,128)(2,1)S(1)} %get-tuple-element.121), channel_id=1, source_target_pairs={{0,2},{1,3},{2,0},{3,1},{4,6},{5,7},{6,4},{7,5},{8,10},{9,11},{10,... | collective-permute-start | bytes 786440 | tf_op jit(solution)/shard_map/ppermute | solution.py:536
  31.3 12.2 %collective-permute-start.7 = (bf16[512,256]{1,0:T(8,128)(2,1)S(1)}, bf16[512,256]{1,0:T(8,128)(2,1)S(1)}, u32[]{:S(2)}, u32[]{:S(2)}) collective-permute-start(bf16[512,256]{1,0:T(8,128)(2,1)S(1)} %get-tuple-element.136), channel_id=1, source_target_pairs={{0,6},{1,7},{2,4},{3,5},{4,2},{5,3},{6,0},{7,1},{8,14},{9,15},{10,... | collective-permute-start | bytes 786440 | tf_op jit(solution)/shard_map/ppermute | solution.py:671
  42.2 3.0 %collective-permute-start.4 = (bf16[1040,256]{1,0:T(8,128)(2,1)S(1)}, bf16[1040,256]{1,0:T(8,128)(2,1)S(1)}, u32[]{:S(2)}, u32[]{:S(2)}) collective-permute-start(bf16[1040,256]{1,0:T(8,128)(2,1)S(1)} %slice.44), channel_id=1, source_target_pairs={{0,1},{1,0},{2,3},{3,2},{4,5},{5,4},{6,7},{7,6},{8,9},{9,8},{10,11... | collective-permute-start | bytes 1597448 | tf_op jit(solution)/shard_map/ppermute | solution.py:536
  45.4 12.9 %collective-permute-start.8 = (bf16[512,256]{1,0:T(8,128)(2,1)S(1)}, bf16[512,256]{1,0:T(8,128)(2,1)S(1)}, u32[]{:S(2)}, u32[]{:S(2)}) collective-permute-start(bf16[512,256]{1,0:T(8,128)(2,1)S(1)} %get-tuple-element.139), channel_id=1, source_target_pairs={{0,2},{1,3},{2,0},{3,1},{4,6},{5,7},{6,4},{7,5},{8,10},{9,11},{10,... | collective-permute-start | bytes 786440 | tf_op jit(solution)/shard_map/ppermute | solution.py:536
  47.0 5.0 %collective-permute-start.9 = (bf16[256,256]{1,0:T(8,128)(2,1)S(1)}, bf16[256,256]{1,0:T(8,128)(2,1)S(1)}, u32[]{:S(2)}, u32[]{:S(2)}) collective-permute-start(bf16[256,256]{1,0:T(8,128)(2,1)S(1)} %get-tuple-element.141), channel_id=1, source_target_pairs={{0,8},{4,12},{8,0},{12,4},{16,24},{20,28},{24,16},{28,20},{1,9},{5... | collective-permute-start | bytes 393224 | tf_op jit(solution)/shard_map/ppermute | solution.py:536
  48.6 6.1 %collective-permute-start.10 = (bf16[384,256]{1,0:T(8,128)(2,1)S(1)}, bf16[384,256]{1,0:T(8,128)(2,1)S(1)}, u32[]{:S(2)}, u32[]{:S(2)}) collective-permute-start(bf16[384,256]{1,0:T(8,128)(2,1)S(1)} %slice.48), channel_id=1, source_target_pairs={{0,1},{1,0},{2,3},{3,2},{4,5},{5,4},{6,7},{7,6},{8,9},{9,8},{10,11... | collective-permute-start | bytes 589832 | tf_op jit(solution)/shard_map/ppermute | solution.py:536
  52.0 7.6 %collective-permute-start.14 = (bf16[256,256]{1,0:T(8,128)(2,1)S(1)}, bf16[256,256]{1,0:T(8,128)(2,1)S(1)}, u32[]{:S(2)}, u32[]{:S(2)}) collective-permute-start(bf16[256,256]{1,0:T(8,128)(2,1)S(1)} %shard_map.292.after.refs_2_.refs_0_), channel_id=1, source_target_pairs={{0,16},{4,20},{8,24},{12,28},{16,0},{20,4},{24,8},{28,12},{1,17},{... | collective-permute-start | bytes 393224 | tf_op jit(solution)/shard_map/ppermute | solution.py:536
  54.7 6.5 %collective-permute-start.11 = (bf16[112,256]{1,0:T(8,128)(2,1)S(1)}, bf16[112,256]{1,0:T(8,128)(2,1)S(1)}, u32[]{:S(2)}, u32[]{:S(2)}) collective-permute-start(bf16[112,256]{1,0:T(8,128)(2,1)S(1)} %shard_map.296), channel_id=1, source_target_pairs={{0,4},{4,0},{8,12},{12,8},{16,20},{20,16},{24,28},{28,24},{1,5},{5... | collective-permute-start | bytes 172040 | tf_op jit(solution)/shard_map/ppermute | solution.py:536
  55.9 5.4 %collective-permute-start.12 = (bf16[112,256]{1,0:T(8,128)(2,1)S(1)}, bf16[112,256]{1,0:T(8,128)(2,1)S(1)}, u32[]{:S(2)}, u32[]{:S(2)}) collective-permute-start(bf16[112,256]{1,0:T(8,128)(2,1)S(1)} %shard_map.297), channel_id=1, source_target_pairs={{0,2},{1,3},{2,0},{3,1},{4,6},{5,7},{6,4},{7,5},{8,10},{9,11},{10,... | collective-permute-start | bytes 172040 | tf_op jit(solution)/shard_map/ppermute | solution.py:536
  56.5 5.1 %collective-permute-start.13 = (bf16[112,256]{1,0:T(8,128)(2,1)S(1)}, bf16[112,256]{1,0:T(8,128)(2,1)S(1)}, u32[]{:S(2)}, u32[]{:S(2)}) collective-permute-start(bf16[112,256]{1,0:T(8,128)(2,1)S(1)} %shard_map.298.refs_2_), channel_id=1, source_target_pairs={{0,6},{1,7},{2,4},{3,5},{4,2},{5,3},{6,0},{7,1},{8,14},{9,15},{10,... | collective-permute-start | bytes 172040 | tf_op jit(solution)/shard_map/ppermute | solution.py:671
  59.6 5.0 %collective-permute-start.16 = (bf16[256,256]{1,0:T(8,128)(2,1)S(1)}, bf16[256,256]{1,0:T(8,128)(2,1)S(1)}, u32[]{:S(2)}, u32[]{:S(2)}) collective-permute-start(bf16[256,256]{1,0:T(8,128)(2,1)S(1)} %shard_map.299.refs_4_.refs_0_), channel_id=1, source_target_pairs={{0,8},{4,12},{8,0},{12,4},{16,24},{20,28},{24,16},{28,20},{1,9},{5... | collective-permute-start | bytes 393224 | tf_op jit(solution)/shard_map/ppermute | solution.py:536
  61.7 6.5 %collective-permute-start.15 = (bf16[112,256]{1,0:T(8,128)(2,1)S(1)}, bf16[112,256]{1,0:T(8,128)(2,1)S(1)}, u32[]{:S(2)}, u32[]{:S(2)}) collective-permute-start(bf16[112,256]{1,0:T(8,128)(2,1)S(1)} %shard_map.300.refs_2_.refs_0_), channel_id=1, source_target_pairs={{0,8},{4,12},{8,0},{12,4},{16,24},{20,28},{24,16},{28,20},{1,9},{5... | collective-permute-start | bytes 172040 | tf_op jit(solution)/shard_map/ppermute | solution.py:536
  64.6 8.5 %collective-permute-start.24 = (bf16[512,256]{1,0:T(8,128)(2,1)S(1)}, bf16[512,256]{1,0:T(8,128)(2,1)S(1)}, u32[]{:S(2)}, u32[]{:S(2)}) collective-permute-start(bf16[512,256]{1,0:T(8,128)(2,1)S(1)} %shard_map.301.refs_2_.refs_0_), channel_id=1, source_target_pairs={{0,6},{1,7},{2,4},{3,5},{4,2},{5,3},{6,0},{7,1},{8,14},{9,15},{10,... | collective-permute-start | bytes 786440 | tf_op jit(solution)/shard_map/ppermute | solution.py:671
  66.0 9.6 %collective-permute-start.23 = (bf16[512,256]{1,0:T(8,128)(2,1)S(1)}, bf16[512,256]{1,0:T(8,128)(2,1)S(1)}, u32[]{:S(2)}, u32[]{:S(2)}) collective-permute-start(bf16[512,256]{1,0:T(8,128)(2,1)S(1)} %shard_map.301.refs_2_.refs_0_), channel_id=1, source_target_pairs={{0,2},{1,3},{2,0},{3,1},{4,6},{5,7},{6,4},{7,5},{8,10},{9,11},{10,... | collective-permute-start | bytes 786440 | tf_op jit(solution)/shard_map/ppermute | solution.py:536
  67.9 8.4 %collective-permute-start.22 = (bf16[512,256]{1,0:T(8,128)(2,1)S(1)}, bf16[512,256]{1,0:T(8,128)(2,1)S(1)}, u32[]{:S(2)}, u32[]{:S(2)}) collective-permute-start(bf16[512,256]{1,0:T(8,128)(2,1)S(1)} %shard_map.301.refs_2_.refs_0_), channel_id=1, source_target_pairs={{0,4},{4,0},{8,12},{12,8},{16,20},{20,16},{24,28},{28,24},{1,5},{5... | collective-permute-start | bytes 786440 | tf_op jit(solution)/shard_map/ppermute | solution.py:536
  68.2 8.3 %collective-permute-start.17 = (bf16[112,256]{1,0:T(8,128)(2,1)S(1)}, bf16[112,256]{1,0:T(8,128)(2,1)S(1)}, u32[]{:S(2)}, u32[]{:S(2)}) collective-permute-start(bf16[112,256]{1,0:T(8,128)(2,1)S(1)} %shard_map.302.refs_0_), channel_id=1, source_target_pairs={{0,16},{4,20},{8,24},{12,28},{16,0},{20,4},{24,8},{28,12},{1,17},{... | collective-permute-start | bytes 172040 | tf_op jit(solution)/shard_map/ppermute | solution.py:536
  76.4 7.7 %collective-permute-start.25 = (bf16[2048,256]{1,0:T(8,128)(2,1)S(1)}, bf16[2048,256]{1,0:T(8,128)(2,1)S(1)}, u32[]{:S(2)}, u32[]{:S(2)}) collective-permute-start(bf16[2048,256]{1,0:T(8,128)(2,1)S(1)} %shard_map.305.mine), channel_id=1, source_target_pairs={{0,1},{1,0},{2,3},{3,2},{4,5},{5,4},{6,7},{7,6},{8,9},{9,8},{10,11... | collective-permute-start | bytes 3145736 | tf_op jit(solution)/shard_map/ppermute | solution.py:536
  76.5 5.1 %collective-permute-start.20 = (bf16[96,256]{1,0:T(8,128)(2,1)S(1)}, bf16[96,256]{1,0:T(8,128)(2,1)S(1)}, u32[]{:S(2)}, u32[]{:S(2)}) collective-permute-start(bf16[96,256]{1,0:T(8,128)(2,1)S(1)} %slice.49.refs_0_), channel_id=1, source_target_pairs={{0,6},{1,7},{2,4},{3,5},{4,2},{5,3},{6,0},{7,1},{8,14},{9,15},{10,... | collective-permute-start | bytes 147464 | tf_op jit(solution)/shard_map/ppermute | solution.py:671
  79.3 4.1 %collective-permute-start.19 = (bf16[96,256]{1,0:T(8,128)(2,1)S(1)}, bf16[96,256]{1,0:T(8,128)(2,1)S(1)}, u32[]{:S(2)}, u32[]{:S(2)}) collective-permute-start(bf16[96,256]{1,0:T(8,128)(2,1)S(1)} %slice.49.refs_0_), channel_id=1, source_target_pairs={{0,2},{1,3},{2,0},{3,1},{4,6},{5,7},{6,4},{7,5},{8,10},{9,11},{10,... | collective-permute-start | bytes 147464 | tf_op jit(solution)/shard_map/ppermute | solution.py:536
  79.9 4.1 %collective-permute-start.18 = (bf16[96,256]{1,0:T(8,128)(2,1)S(1)}, bf16[96,256]{1,0:T(8,128)(2,1)S(1)}, u32[]{:S(2)}, u32[]{:S(2)}) collective-permute-start(bf16[96,256]{1,0:T(8,128)(2,1)S(1)} %slice.49.refs_0_), channel_id=1, source_target_pairs={{0,4},{4,0},{8,12},{12,8},{16,20},{20,16},{24,28},{28,24},{1,5},{5... | collective-permute-start | bytes 147464 | tf_op jit(solution)/shard_map/ppermute | solution.py:536
  (19 other events, 79.9 us)

commit v3 on v2

--- a/solution.py
+++ b/solution.py
@@ -126,7 +126,7 @@
     spot[...] = jnp.where(rows == 0, me_ref[0], me_ref[1])
 
 
-def project(rows_in, gain, code, wk_pad, wv_pad, wk_t, wv_t, at, normed, normed_t, k_aug, v_pad, kt, vt):
+def project(rows_in, gain, code, wk_pad, wv_t, at, normed, normed_t, k_aug, vt):
     count = rows_in.shape[0]
     unit, _ = unit_rows(high(rows_in))
     value = low(unit * gain)
@@ -135,47 +135,61 @@
     normed_t[:, at : at + count] = flipped
     wide = low(dot(value, wk_pad))
     k_aug[at : at + count, :] = wide + jnp.concatenate([code] * HEADS, axis=1)
-    v_lane = lax.broadcasted_iota(jnp.int32, (1, WIDE), 1) & (LANES - 1)
-    v_ones = jnp.where((v_lane >= HEAD_DIM) & (v_lane < HEAD_DIM + 3), 1.0, 0.0)
-    v_pad[at : at + count, :] = low(dot(value, wv_pad) + v_ones)
-    kt[:, at : at + count] = low(dot(wk_t, flipped))
     turned = low(dot(wv_t, flipped))
     for h in range(HEADS):
         vt[h * TALL : h * TALL + HEAD_DIM, at : at + count] = turned[h * HEAD_DIM : (h + 1) * HEAD_DIM]
         vt[h * TALL + HEAD_DIM : (h + 1) * TALL, at : at + count] = jnp.ones((16, count), BF)
 
 
-def raw_attention(q_aug, k_aug, vt, part):
+def raw_attention(q_aug, k_aug, vt, before, part):
     for h in range(HEADS):
         lanes = slice(h * LANES, (h + 1) * LANES)
         tall = slice(h * TALL, (h + 1) * TALL)
         p = low(jnp.exp(dot_nt(k_aug[:, lanes], q_aug[:, lanes])))
-        part[tall, :] = dot(vt[tall, :], p)
-
-
-def exact_attention(q_aug, halves, self_rows, vt_own, scores, o_t, lse_out):
-    for h in range(HEADS):
-        lanes = slice(h * LANES, (h + 1) * LANES)
+        got = dot(vt[tall, :], p)
+        part[tall, :] = got if before is None else got + before[tall, :]
+
+
+def exact_attention(q_aug, parts, self_rows, vt_own, scores, o_t, lse_out):
+    step = 256
+
+    def one_head(h, _):
+        lanes = pl.ds(pl.multiple_of(h * LANES, LANES), LANES)
+        tall = pl.ds(pl.multiple_of(h * TALL, 16), HEAD_DIM)
         q_h = q_aug[:, lanes]
-        top = self_h = self_rows[h : h + 1]
-        at = 0
-        for k_half, _ in halves:
-            count = k_half.shape[0]
-            scores[at : at + count, :] = dot_nt(k_half[:, lanes], q_h)
-            top = jnp.maximum(top, jnp.max(scores[at : at + count, :], axis=0, keepdims=True))
-            at += count
+        self_h = self_rows[pl.ds(h, 1), :]
+        top = self_h
+        first = 0
+        for k_part, _ in parts:
+
+            def score(c, top, k_part=k_part, first=first):
+                at = pl.multiple_of(c * step, step)
+                part = dot_nt(k_part[pl.ds(at, step), lanes], q_h)
+                scores[pl.ds(first + at, step), :] = part
+                return jnp.maximum(top, jnp.max(part, axis=0, keepdims=True))
+
+            top = lax.fori_loop(0, k_part.shape[0] // step, score, top)
+            first += k_part.shape[0]
         p_self = jnp.exp(self_h - top)
         total = p_self
-        acc = high(low(p_self)) * high(vt_own[h * TALL : h * TALL + HEAD_DIM, :])
-        at = 0
-        for k_half, vt_half in halves:
-            count = k_half.shape[0]
-            p = jnp.exp(scores[at : at + count, :] - top)
-            total = total + jnp.sum(p, axis=0, keepdims=True)
-            acc = acc + dot(vt_half[h * TALL : h * TALL + HEAD_DIM, :], low(p))
-            at += count
-        o_t[h * LANES : h * LANES + HEAD_DIM, :] = acc / total
-        lse_out[h : h + 1, :] = top + jnp.log(total)
+        acc = high(low(p_self)) * high(vt_own[tall, :])
+        first = 0
+        for _, vt_part in parts:
+
+            def weigh(c, carry, vt_part=vt_part, first=first):
+                total, acc = carry
+                at = pl.multiple_of(c * step, step)
+                p = jnp.exp(scores[pl.ds(first + at, step), :] - top)
+                total = total + jnp.sum(p, axis=0, keepdims=True)
+                return total, acc + dot(vt_part[tall, pl.ds(at, step)], low(p))
+
+            total, acc = lax.fori_loop(0, vt_part.shape[1] // step, weigh, (total, acc))
+            first += vt_part.shape[1]
+        o_t[pl.ds(pl.multiple_of(h * LANES, LANES), HEAD_DIM), :] = acc / total
+        lse_out[pl.ds(h, 1), :] = top + jnp.log(total)
+        return 0
+
+    lax.fori_loop(0, HEADS, one_head, 0)
 
 
 def placed(rows16, first):
@@ -200,9 +214,9 @@
 
 def first_kernel(
     own_rows,
-    spot, seg, core_rows, tokens, valid, gain_one, wq, wk, wv, wo,
+    spot, seg, core_rows, tokens, valid, gain_one, wq, wk, wv, wo, w_cross, b_cross,
     wq_pad, wk_pad, wv_pad, wo_pad, wk_t, wv_t, codes, real, counted,
-    normed, normed_t, q_aug, k_aug, v_pad, kt, vt, part,
+    normed, normed_t, q_aug, k_aug, vt, part, self_scores, crossed,
 ):
     me = jnp.max(spot[0:1, :])
     for step in range(4):
@@ -225,53 +239,56 @@
     for step, rows_in in enumerate((tokens, core_rows)):
         at = step * own_rows
         project(
-            rows_in[...], gain, codes[at : at + own_rows, :], wk_pad[...], wv_pad[...], wk_t[...], wv_t[...], at,
-            normed, normed_t, k_aug, v_pad, kt, vt,
+            rows_in[...], gain, codes[at : at + own_rows, :], wk_pad[...], wv_t[...], at,
+            normed, normed_t, k_aug, vt,
         )
     spread, inside = segment_rows(seg, pl.multiple_of(me * own_rows, own_rows), own_rows)
     own_code = lane_codes(jnp.where(inside | (spread > SEGS), 0.0, 1.0))
     scaled = low(dot(normed[:own_rows, :], wq_pad[...]) * 0.125)
     q_aug[...] = scaled + jnp.concatenate([own_code] * HEADS, axis=1)
-    raw_attention(q_aug, k_aug, vt, part)
+    raw_attention(q_aug, k_aug, vt, None, part)
+    lanes_own = lax.broadcasted_iota(jnp.int32, (own_rows, WIDE), 1) & (LANES - 1)
+    product = high(q_aug[...]) * high(k_aug[:own_rows, :])
+    self_scores[...] = head_sums(head_selector(), jnp.where(lanes_own < HEAD_DIM, product, 0.0))
+    crossed[...] = dot(normed[:own_rows, :], w_cross[...]) + b_cross[...]
+
+
+def middle_kernel(
+    own_rows,
+    y_rows, gain_one, codes, wk_pad, wv_t, q_aug, part_a,
+    normed, normed_t, k_aug, vt, part,
+):
+    project(
+        y_rows[...], gain_one[...], codes[2 * own_rows : 3 * own_rows, :], wk_pad[...], wv_t[...], 0,
+        normed, normed_t, k_aug, vt,
+    )
+    raw_attention(q_aug, k_aug, vt, part_a, part)
 
 
 def forward_kernel(
     own_rows,
-    spot, y_rows, far_rows, codes, real, counted, tokens, cot,
-    gain_one, wk_pad, wv_pad, wo_pad, wk_t, wv_t,
-    w_cross, b_cross, w_mix, w_ens1, gain_two, w_up, b_up, w_ens2,
-    normed_a, normed_ta, q_aug, k_a, v_a, kt_a, vt_a, part_a,
-    out_rows, d_first_out, dn_own, payload, vectors,
-    normed_b, normed_tb, k_b, v_b, kt_b,
-    q_back, grad_att, pself_out, dself_out, seg_grad_out,
-    vt_b, part_b, scores, o_t, lse_out,
+    spot, far_rows, codes, real, counted, tokens, cot,
+    gain_one, wk_pad, wo_pad, wv_t,
+    w_mix, w_ens1, gain_two, w_up, b_up, w_ens2,
+    normed_a, normed_y, q_aug, k_a, k_y, vt_a, vt_y, part_y, self_scores, crossed,
+    payload, d_first_out, vectors, normed_f, normed_tf, k_f,
+    first_out, active_out, normed_two_out, d_modules_out, att_out, lse_out, member_out, counts_out,
+    vt_f, part_f, scores, o_t, self_rows,
 ):
-    gain = gain_one[...]
-    for step, rows_in in enumerate((y_rows[...], far_rows[:own_rows, :])):
-        at = step * own_rows
-        project(
-            rows_in, gain, codes[at + 2 * own_rows : at + 3 * own_rows, :],
-            wk_pad[...], wv_pad[...], wk_t[...], wv_t[...], at,
-            normed_b, normed_tb, k_b, v_b, kt_b, vt_b,
-        )
+    project(
+        far_rows[:own_rows, :], gain_one[...], codes[3 * own_rows :, :], wk_pad[...], wv_t[...], 0,
+        normed_f, normed_tf, k_f, vt_f,
+    )
     normed_own = normed_a[:own_rows, :]
-    heads16 = head_selector()
-    lanes_own = lax.broadcasted_iota(jnp.int32, (own_rows, WIDE), 1) & (LANES - 1)
-    v_own = v_a[:own_rows, :]
-    self_product = jnp.where(
-        lanes_own < HEAD_DIM, high(q_aug[...]) * high(k_a[:own_rows, :]), 0.0
-    )
-    self_scores = head_sums(heads16, self_product)
     own_real = real[:, :own_rows] > 0
     o_t[...] = jnp.zeros_like(o_t)
     lse_out[...] = jnp.zeros_like(lse_out)
-    half_keys = 2 * own_rows
-    raw_attention(q_aug, k_b, vt_b, part_b)
+    raw_attention(q_aug, k_f, vt_f, part_y, part_f)
     vt_own = vt_a[:, :own_rows]
     smallest, largest = jnp.inf, -jnp.inf
     for h in range(HEADS):
-        p_self = jnp.where(own_real, 0.0, jnp.exp(self_scores[h : h + 1]))
-        both = part_a[h * TALL : (h + 1) * TALL, :] + part_b[h * TALL : (h + 1) * TALL, :]
+        p_self = jnp.where(own_real, 0.0, jnp.exp(self_scores[h : h + 1, :]))
+        both = part_f[h * TALL : (h + 1) * TALL, :]
         total = both[HEAD_DIM : HEAD_DIM + 1] + p_self
         acc = both[:HEAD_DIM] + high(low(p_self)) * high(vt_own[h * TALL : h * TALL + HEAD_DIM])
         o_t[h * LANES : h * LANES + HEAD_DIM, :] = acc / total
@@ -282,40 +299,46 @@
 
     @pl.when(jnp.logical_not(fits))
     def _():
-        self_rows = jnp.where(own_real, HUGE, self_scores)
-        exact_attention(q_aug, ((k_a, vt_a), (k_b, vt_b)), self_rows, vt_own, scores, o_t, lse_out)
-
-    q_back[...] = q_aug[...] + placed(-lse_out[...], HEAD_DIM + SEGS + 1)
+        self_rows[...] = jnp.where(own_real, HUGE, self_scores[...])
+        parts = ((k_a, vt_a), (k_y, vt_y), (k_f, vt_f))
+        exact_attention(q_aug, parts, self_rows, vt_a.at[:, :own_rows], scores, o_t, lse_out)
+
     att = o_t[...].T
+    att_out[...] = att
     att_low = low(att)
 
     modules = []
     for g in range(2):
         lanes = slice(g * 256, (g + 1) * 256)
         modules.append(low(dot(att_low[:, lanes], wo_pad[lanes, :])))
-    crossed = dot(normed_own, w_cross[...]) + b_cross[...]
-    modules.append(low(high(normed_own) * crossed))
+    modules.append(low(high(normed_own) * crossed[...]))
     counts = jnp.sum(high(counted[...]), axis=1, keepdims=True)
     counts = jnp.maximum(counts, 1.0)
-    seg_sums = dot(counted[:, :half_keys], normed_a[...]) + dot(counted[:, half_keys:], normed_b[...])
+    counts_out[...] = jnp.broadcast_to(counts, counts_out.shape)
+    seg_sums = dot(counted[:, : 2 * own_rows], normed_a[...])
+    seg_sums = seg_sums + dot(counted[:, 2 * own_rows : 3 * own_rows], normed_y[...])
+    seg_sums = seg_sums + dot(counted[:, 3 * own_rows :], normed_f[...])
     seg_mean = low(seg_sums / counts)
     picked = lax.broadcasted_iota(jnp.int32, (LANES, 16), 0) - HEAD_DIM
     picked = (picked == lax.broadcasted_iota(jnp.int32, (LANES, 16), 1)) & (picked < SEGS)
     own_member = 1.0 - dot(q_aug[:, :LANES], low(jnp.where(picked, 1.0, 0.0)))
     own_lane = lax.broadcasted_iota(jnp.int32, (own_rows, 16), 1)
     own_member = low(jnp.where(own_lane < SEGS, own_member, 0.0))
+    member_out[...] = own_member
     mixed = low(dot(own_member, seg_mean))
     modules.append(low(dot(mixed, w_mix[...])))
     first = high(tokens[...])
     for i in range(4):
         first = first + dot(modules[i], w_ens1[i * D : (i + 1) * D, :])
+    first_out[...] = first
     unit_two, scale_two = unit_rows(first)
     normed_two = low(unit_two * gain_two[...])
     inner = dot(normed_two, w_up[...]) + b_up[...]
     cdf = 0.5 * (1.0 + lax.erf(inner * 0.7071067811865476))
     active = low(inner * cdf)
     slope = cdf + inner * jnp.exp(-0.5 * inner * inner) * 0.3989422804014327
-    out_rows[...] = first + (dot(active, w_ens2[:FF, :]) + dot(normed_two, w_ens2[FF:, :]))
+    active_out[...] = active
+    normed_two_out[...] = normed_two
 
     core, y_bit, x_bit, z_bit = bits_of(spot)
     order = y_bit * 8 + x_bit * 4 + z_bit * 2
@@ -349,75 +372,105 @@
     for i in range(4):
         put(dot_tn(modules[i], e1))
         d_modules.append(low(dot_nt(e1, w_ens1[i * D : (i + 1) * D, :])))
+        d_modules_out[:, i * D : (i + 1) * D] = d_modules[i]
     out_grads = []
     for g in range(2):
         lanes = slice(g * 256, (g + 1) * 256)
         out_grads.append(dot_tn(att_low[:, lanes], d_modules[g]))
-        grad_att[:, lanes] = low(dot_nt(d_modules[g], wo_pad[lanes, :]))
     put(narrow_rows(jnp.concatenate(out_grads, axis=0)))
-    d_cross = low(high(d_modules[2]) * high(normed_own))
-    put(dot_tn(normed_own, d_cross))
+    put(dot_tn(normed_own, low(high(d_modules[2]) * high(normed_own))))
     put(dot_tn(mixed, d_modules[3]))
-    dn_own[...] = high(d_modules[2]) * crossed + dot_nt(d_cross, w_cross[...])
-    d_mixed = dot_nt(d_modules[3], w_mix[...])
-    mixed_up = low(d_mixed)
-    mixed_down = low(d_mixed - high(mixed_up))
-    seg_grad_out[...] = (dot_tn(own_member, mixed_up) + dot_tn(own_member, mixed_down)) / counts
     vectors[...] = jnp.zeros_like(vectors)
     for i in range(FF // D):
         vectors[i : i + 1, :] = b_up_grad[:, i * D : (i + 1) * D]
-    vectors[4:5, :] = jnp.sum(high(d_cross), axis=0, keepdims=True)
     vectors[5:6, :] = jnp.sum(d_norm2 * unit_two, axis=0, keepdims=True)
 
-    d_att = high(grad_att[...])
-    delta = head_sums(heads16, d_att * att)
-    grad_att[...] = grad_att[...] + placed(-delta, HEAD_DIM)
-    p_self = jnp.where(own_real, 0.0, jnp.exp(self_scores - lse_out[...]))
-    dp_self = head_sums(heads16, d_att * high(v_own))
+
+def side_kernel(
+    own_rows,
+    first, active, normed_two, w_ens2, d_modules, att, lse, own_member, counts, vectors_in,
+    normed_a, normed_y, normed_f, normed_ta, normed_ty, normed_tf, q_aug, self_scores, crossed, real,
+    wv_pad, wk_t, wo_pad, w_cross, w_mix,
+    out_rows, dn_own, vectors, v_all, kt_all, q_back, grad_att, pself_out, dself_out, seg_grad_out,
+):
+    v_lane = lax.broadcasted_iota(jnp.int32, (1, WIDE), 1) & (LANES - 1)
+    v_ones = jnp.where((v_lane >= HEAD_DIM) & (v_lane < HEAD_DIM + 3), 1.0, 0.0)
+    at = 0
+    for normed, flipped in ((normed_a, normed_ta), (normed_y, normed_ty), (normed_f, normed_tf)):
+        count = normed.shape[0]
+        v_all[at : at + count, :] = low(dot(normed[...], wv_pad[...]) + v_ones)
+        kt_all[:, at : at + count] = low(dot(wk_t[...], flipped[...]))
+        at += count
+    out_rows[...] = first[...] + (dot(active[...], w_ens2[:FF, :]) + dot(normed_two[...], w_ens2[FF:, :]))
+    d_att = []
+    for g in range(2):
+        lanes = slice(g * 256, (g + 1) * 256)
+        d_att.append(low(dot_nt(d_modules[:, g * D : (g + 1) * D], wo_pad[lanes, :])))
+    d_att = jnp.concatenate(d_att, axis=1)
+    heads16 = head_selector()
+    delta = head_sums(heads16, high(d_att) * att[...])
+    grad_att[...] = d_att + placed(-delta, HEAD_DIM)
+    q_back[...] = q_aug[...] + placed(-lse[...], HEAD_DIM + SEGS + 1)
+    p_self = jnp.where(real[:, :own_rows] > 0, 0.0, jnp.exp(self_scores[...] - lse[...]))
+    dp_self = head_sums(heads16, high(d_att) * high(v_all[:own_rows, :]))
     pself_out[...] = low(p_self)
     dself_out[...] = low(p_self * (dp_self - delta))
+    d_two = high(d_modules[:, 2 * D : 3 * D])
+    d_cross = low(d_two * high(normed_a[:own_rows, :]))
+    dn_own[...] = d_two * crossed[...] + dot_nt(d_cross, w_cross[...])
+    d_mixed = dot_nt(d_modules[:, 3 * D :], w_mix[...])
+    mixed_up = low(d_mixed)
+    mixed_down = low(d_mixed - high(mixed_up))
+    seg_grad = dot_tn(own_member[...], mixed_up) + dot_tn(own_member[...], mixed_down)
+    seg_grad_out[...] = seg_grad / counts[:, :1]
+    tail = lax.broadcasted_iota(jnp.int32, (16, D), 0)
+    b_cross_grad = jnp.sum(high(d_cross), axis=0, keepdims=True)
+    vectors[...] = jnp.where(tail == 4, b_cross_grad, vectors_in[...])
 
 
 def head_kernel(
     own_rows, h,
-    q_back, k_a, k_b, v_a, v_b, kt_a, kt_b, grad_att, pself, dself, after_one, after_two,
-    dk_out, dv_out, dq_out,
+    q_back, k_a, k_y, k_f, v_all, kt_all, grad_att, pself, dself,
+    *rest,
 ):
-    half_keys = 2 * own_rows
+    dk_out, dv_out, dq_out = rest[-3:]
     row16 = lax.broadcasted_iota(jnp.int32, (16, LANES), 0)
     spread = low(jnp.where(row16 == h, 1.0, 0.0))
     lanes = slice(h * LANES, (h + 1) * LANES)
     rows_h = slice(h * HEAD_DIM, (h + 1) * HEAD_DIM)
     q_h = q_back[:, lanes]
     g_h = grad_att[:, lanes]
-    acc = high(dself[h : h + 1, :]) * high(kt_a[rows_h, :own_rows])
-    for c, (k_half, v_half, kt_half) in enumerate(((k_a, v_a, kt_a), (k_b, v_b, kt_b))):
-        at = slice(c * half_keys, (c + 1) * half_keys)
-        p = jnp.exp(dot_nt(k_half[:, lanes], q_h))
-        ds = low(p * dot_nt(v_half[:, lanes], g_h))
+    acc = high(dself[h : h + 1, :]) * high(kt_all[rows_h, :own_rows])
+    first = 0
+    for k_part in (k_a, k_y, k_f):
+        count = k_part.shape[0]
+        at = slice(first, first + count)
+        p = jnp.exp(dot_nt(k_part[:, lanes], q_h))
+        ds = low(p * dot_nt(v_all[at, lanes], g_h))
         dv = dot(low(p), g_h)
         dk = dot(ds, q_h)
-        if c == 0:
+        if first == 0:
             dk_self = dot_tn(dself[...], spread) * high(q_h)
             dv_self = dot_tn(pself[...], spread) * high(g_h)
             dk_out[:own_rows, :] = low(dk[:own_rows] + dk_self)
             dv_out[:own_rows, :] = low(dv[:own_rows] + dv_self)
-            dk_out[own_rows:half_keys, :] = low(dk[own_rows:])
-            dv_out[own_rows:half_keys, :] = low(dv[own_rows:])
+            dk_out[own_rows:count, :] = low(dk[own_rows:])
+            dv_out[own_rows:count, :] = low(dv[own_rows:])
         else:
             dk_out[at, :] = low(dk)
             dv_out[at, :] = low(dv)
-        acc = acc + dot(kt_half[rows_h, :], ds)
+        acc = acc + dot(kt_all[rows_h, at], ds)
+        first += count
     dq_out[...] = low(acc * 0.125)
 
 
 def rows_kernel(
     own_rows,
-    dk0, dk1, dk2, dk3, dv0, dv1, dv2, dv3, dq0, dq1, dq2, dq3, after, normed_a, normed_b, counted, seg_grad, dn_own,
+    dk0, dk1, dk2, dk3, dv0, dv1, dv2, dv3, dq0, dq1, dq2, dq3, normed_a, normed_y, normed_f, counted, seg_grad, dn_own,
     gain_one, wq, wk_pad, wv_pad, vectors,
-    out, dq_out,
-    dn,
+    *rest,
 ):
+    out, dq_out, dn = rest[-3:]
     half_keys = 2 * own_rows
     dq = jnp.concatenate([high(part[...]) for part in (dq0, dq1, dq2, dq3)], axis=0)
     dq_rows = low(dq.T)
@@ -437,7 +490,9 @@
         )
     dn[:own_rows, :] = dn[:own_rows, :] + (dot_nt(dq_rows, wq[...]) + dn_own[...])
     gain_grad = jnp.sum(dn[:half_keys, :] * high(normed_a[...]), axis=0, keepdims=True)
-    gain_grad += jnp.sum(dn[half_keys:, :] * high(normed_b[...]), axis=0, keepdims=True)
+    for i, normed in enumerate((normed_y, normed_f)):
+        here = dn[(2 + i) * own_rows : (3 + i) * own_rows, :]
+        gain_grad = gain_grad + jnp.sum(here * high(normed[...]), axis=0, keepdims=True)
     gain_grad = gain_grad / gain_one[...]
     count = out.shape[0] // 2
     for step in range(4):
@@ -452,17 +507,21 @@
 def weights_kernel(
     own_rows,
     spot,
-    dk0, dk1, dk2, dk3, dv0, dv1, dv2, dv3, dq_rows, normed_ta, normed_tb, after,
-    out,
+    dk0, dk1, dk2, dk3, dv0, dv1, dv2, dv3, dq_rows, normed_ta, normed_ty, normed_tf,
+    *rest,
 ):
-    half_keys = 2 * own_rows
+    out = rest[-1]
+    flips = ((normed_ta, 0), (normed_ty, 2), (normed_tf, 3))
 
     def key_grad(parts):
         pairs = [jnp.concatenate([parts[i][...], parts[i + 1][...]], axis=1) for i in (0, 2)]
         return narrow(
             jnp.concatenate(
                 [
-                    dot(normed_ta[...], pair[:half_keys]) + dot(normed_tb[...], pair[half_keys:])
+                    sum(
+                        dot(flip[...], pair[at * own_rows : at * own_rows + flip.shape[1]])
+                        for flip, at in flips
+                    )
                     for pair in pairs
                 ],
                 axis=1,
@@ -484,14 +543,16 @@
             out[pl.ds(pl.multiple_of(at, part), part), :] = low(grad[n * part : (n + 1) * part])
 
 
-def finish_kernel(mine, other, tokens, d_first, gain_one, after, grad_tokens, done):
+def finish_kernel(mine, other, tokens, d_first, gain_one, *rest):
+    grad_tokens, done = rest[-2:]
     unit, scale = unit_rows(high(tokens[...]))
     total = high(mine[...]) + high(other[...])
     grad_tokens[...] = d_first[...] + norm_back(total, unit, scale, gain_one[...])
-    done[...] = after[:16, :]
-
-
-def unpack_kernel(spot, mine, other, attn_out, cross, mix, ens1, up, ens2, done):
+    done[...] = mine[:16, :]
+
+
+def unpack_kernel(spot, mine, other, *rest):
+    attn_out, cross, mix, ens1, up, ens2, done = rest[-7:]
     core, y_bit, x_bit, z_bit = bits_of(spot)
     order = y_bit * 8 + x_bit * 4 + z_bit * 2
     block = mine.shape[0] // 16
@@ -512,9 +573,8 @@
     done[...] = mine[:16, :]
 
 
-def unpack_small_kernel(
-    spot, mine, other, vec, after, gain_one, query, key, value, b_cross, gain_two, b_up
-):
+def unpack_small_kernel(spot, mine, other, vec, *rest):
+    gain_one, query, key, value, b_cross, gain_two, b_up, done = rest[-8:]
     core, y_bit, x_bit, _ = bits_of(spot)
     order = y_bit * 2 + x_bit
     part = D // 8
@@ -530,6 +590,7 @@
     b_cross[...] = wide[4:5]
     gain_two[...] = wide[5:6]
     gain_one[...] = wide[6:7]
+    done[...] = mine[:16, :]
 
 
 def swap(value, axis, count, step):
@@ -610,49 +671,67 @@
     (spot,) = call(start_kernel, [((8, LANES), jnp.int32)], [], "s", 4, 20)(me)
     (
         wq_pad, wk_pad, wv_pad, wo_pad, wk_t, wv_t, codes, real, counted,
-        normed_a, normed_ta, q_aug, k_a, v_a, kt_a, vt_a, part_a,
+        normed_a, normed_ta, q_aug, k_a, vt_a, part_a, self_scores, crossed,
     ) = call(
         functools.partial(first_kernel, own),
         [
             ((D, WIDE), BF), ((D, WIDE), BF), ((D, WIDE), BF), ((WIDE, D), BF), square, square,
             ((rows, LANES), BF), ((1, rows), F32), ((16, rows), BF),
-            ((keys, D), BF), ((D, keys), BF), ((own, WIDE), BF), ((keys, WIDE), BF), ((keys, WIDE), BF),
-            ((D, keys), BF), ((HEADS * TALL, keys), BF), ((HEADS * TALL, own), F32),
+            ((keys, D), BF), ((D, keys), BF), ((own, WIDE), BF), ((keys, WIDE), BF),
+            ((HEADS * TALL, keys), BF), ((HEADS * TALL, own), F32), ((16, own), F32), ((own, D), F32),
         ],
-        [], "vs" + "v" * 8, 16, 5,
+        [], "vs" + "v" * 10, 16, 5,
     )(
-        spot, seg_lengths, from_core, tokens, valid_row, gain_row, w_query, w_key, w_value, w_attn_out
+        spot, seg_lengths, from_core, tokens, valid_row, gain_row, w_query, w_key, w_value, w_attn_out,
+        w_cross, b_cross.reshape(1, D),
     )
     from_far = by_core(jnp.concatenate([from_y, normed_a[:16]], axis=0))
+    normed_y, normed_ty, k_y, vt_y, part_y = call(
+        functools.partial(middle_kernel, own),
+        [((own, D), BF), ((D, own), BF), ((own, WIDE), BF), ((HEADS * TALL, own), BF), ((HEADS * TALL, own), F32)],
+        [], "v" * 7, 16, 2,
+    )(from_y, gain_row, codes, wk_pad, wv_t, q_aug, part_a)
     (
-        out_rows, d_first, dn_own, payload, vectors, normed_b, normed_tb, k_b, v_b, kt_b,
-        q_back, grad_att, pself, dself, seg_grad,
+        payload, d_first, vectors, normed_f, normed_tf, k_f,
+        first, active, normed_two, d_modules, att, lse, own_member, counts,
     ) = call(
         functools.partial(forward_kernel, own),
         [
-            ((own, D), F32), ((own, D), F32), ((own, D), F32), ((16 * D, D), BF), ((16, D), F32),
-            ((keys, D), BF), ((D, keys), BF), ((keys, WIDE), BF), ((keys, WIDE), BF), ((D, keys), BF),
+            ((16 * D, D), BF), ((own, D), F32), ((16, D), F32), ((own, D), BF), ((D, own), BF), ((own, WIDE), BF),
+            ((own, D), F32), ((own, FF), BF), ((own, D), BF), ((own, 4 * D), BF), ((own, WIDE), F32), ((16, own), F32),
+            ((own, 16), BF), ((16, LANES), F32),
+        ],
+        [
+            pltpu.VMEM((HEADS * TALL, own), BF), pltpu.VMEM((HEADS * TALL, own), F32), pltpu.VMEM((rows, own), F32),
+            pltpu.VMEM((WIDE, own), F32), pltpu.VMEM((16, own), F32),
+        ],
+        "v" * 27, 32, 8,
+    )(
+        spot, from_far, codes, real, counted, tokens, cotangent, gain_row, wk_pad, wo_pad, wv_t,
+        w_mix, w_ens1, gain_two.reshape(1, D), w_up, b_up.reshape(1, FF), w_ens2,
+        normed_a, normed_y, q_aug, k_a, k_y, vt_a, vt_y, part_y, self_scores, crossed,
+    )
+    big_got = by_core(payload[payload.shape[0] // 2 :])
+    out_rows, dn_own, vectors, v_all, kt_all, q_back, grad_att, pself, dself, seg_grad = call(
+        functools.partial(side_kernel, own),
+        [
+            ((own, D), F32), ((own, D), F32), ((16, D), F32), ((rows, WIDE), BF), ((D, rows), BF),
             ((own, WIDE), BF), ((own, WIDE), BF), ((16, own), BF), ((16, own), BF), ((16, D), F32),
         ],
-        [
-            pltpu.VMEM((HEADS * TALL, keys), BF), pltpu.VMEM((HEADS * TALL, own), F32), pltpu.VMEM((rows, own), F32),
-            pltpu.VMEM((WIDE, own), F32), pltpu.VMEM((16, own), F32),
-        ],
-        "v" * 30, 32, 10,
+        [], "v" * 25, 16, 3,
     )(
-        spot, from_y, from_far, codes, real, counted, tokens, cotangent, gain_row, wk_pad, wv_pad, wo_pad, wk_t, wv_t,
-        w_cross, b_cross.reshape(1, D), w_mix, w_ens1, gain_two.reshape(1, D), w_up, b_up.reshape(1, FF), w_ens2,
-        normed_a, normed_ta, q_aug, k_a, v_a, kt_a, vt_a, part_a,
+        first, active, normed_two, w_ens2, d_modules, att, lse, own_member, counts, vectors,
+        normed_a, normed_y, normed_f, normed_ta, normed_ty, normed_tf, q_aug, self_scores, crossed, real,
+        wv_pad, wk_t, wo_pad, w_cross, w_mix,
     )
 
-    def head(index, after_one, after_two):
+    def head(index, *after, cost=0):
+        args = [q_back, k_a, k_y, k_f, v_all, kt_all, grad_att, pself, dself, *after]
         return call(
             functools.partial(head_kernel, own, index),
             [((rows, LANES), BF), ((rows, LANES), BF), ((HEAD_DIM, own), BF)],
-            [], "v" * 12, 16, 2,
-        )(
-            q_back, k_a, k_b, v_a, v_b, kt_a, kt_b, grad_att, pself, dself, after_one[:16], after_two[:16]
-        )
+            [], "v" * len(args), 16, cost,
+        )(*args)
 
     def summed(counts, parts, *after, cost=0):
         outs = [((count, D), BF) for count in counts]
@@ -670,73 +749,87 @@
         pairs = [(i, i ^ (n_module + 2)) for i in range(n_batch * n_module)]
         return lax.ppermute(value, ("batch", "module"), pairs)
 
+    def around(values):
+        return by_batch(values[0], 1), by_y(values[1]), by_both(values[2])
+
+    steps = [1 << place for place in range(1, n_batch.bit_length() - 1)]
+
+    def through(value, got, *after, cost=0):
+        for step in steps[2:] + [0]:
+            (value,) = summed([value.shape[0]], [value, got], *after, cost=cost)
+            got = by_batch(value, step) if step else None
+        return value
+
     size = payload.shape[0] // 8
-    big_got = by_core(payload[4 * size :])
-    dk0, dv0, dq0 = head(0, pself, pself)
-    mine, to_x, to_y, to_both = summed([size] * 4, [payload, big_got])
-    got = (by_batch(to_x, 1), by_y(to_y), by_both(to_both))
-    dk1, dv1, dq1 = head(1, mine, dq0)
-    dk2, dv2, dq2 = head(2, to_x, dq1)
-    dk3, dv3, dq3 = head(3, to_y, dq2)
-    steps = [1 << place for place in range(1, n_batch.bit_length() - 1)]
+    half = size // 2
     part = D // 8
     count = 2 * own + 16
+    rows_q = 3 * part + 16
+    wide = ((D, D), F32)
+    mine, *outward = summed([size] * 4, [payload, big_got], pself, cost=0)
+    xy_got = around(outward)
+    dk0, dv0, dq0 = head(0, mine, cost=2)
+    dk1, dv1, dq1 = head(1, dq0, cost=2)
+    dk2, dv2, dq2 = head(2, dq1, cost=2)
+    dk3, dv3, dq3 = head(3, dq2, cost=2)
+    args = [
+        dk0, dk1, dk2, dk3, dv0, dv1, dv2, dv3, dq0, dq1, dq2, dq3, normed_a, normed_y, normed_f, counted, seg_grad,
+        dn_own, gain_row, w_query, wk_pad, wv_pad, vectors,
+    ]
     shared, dq_rows = call(
         functools.partial(rows_kernel, own),
         [((2 * count, D), BF), ((own, D), BF)],
         [pltpu.VMEM((rows, D), F32)],
-        "v" * 23, 16, 3,
-    )(
-        dk0, dk1, dk2, dk3, dv0, dv1, dv2, dv3, dq0, dq1, dq2, dq3, mine, normed_a, normed_b, counted, seg_grad, dn_own,
-        gain_row, w_query, wk_pad, wv_pad, vectors,
-    )
+        "v" * len(args), 16, 3,
+    )(*args)
+    ab, ab_send = summed([half] * 2, [mine, *xy_got], dq_rows, cost=0)
+    z1_got = by_batch(ab_send, steps[0])
     shared_got = by_core(shared[count:])
-    half = size // 2
-    ab, ab_send = summed([half] * 2, [mine, *got], shared)
-    ab_got = by_batch(ab_send, steps[0])
-    (q,) = call(functools.partial(weights_kernel, own), [((24 * part, D), BF)], [], "v" * 13, 16, 3)(
-        spot, dk0, dk1, dk2, dk3, dv0, dv1, dv2, dv3, dq_rows, normed_ta, normed_tb, ab
-    )
-    q_got = by_core(q[12 * part :])
-    (ab,) = summed([half], [ab, ab_got], q, cost=1)
-    ab_got = by_batch(ab, steps[1]) if len(steps) > 1 else ab
-    dn, dn_send, vec = summed([own, own, 16], [shared, shared_got], q)
+    args = [
+        spot, dk0, dk1, dk2, dk3, dv0, dv1, dv2, dv3, dq_rows, normed_ta, normed_ty, normed_tf, ab,
+    ]
+    (q,) = call(
+        functools.partial(weights_kernel, own), [((24 * part, D), BF)], [], "v" * len(args), 16, 3
+    )(*args)
+    (ab1,) = summed([half], [ab, z1_got], q, cost=0)
+    z2_got = by_batch(ab1, steps[1])
+    q_out = joined([q[12 * part :]], ab1, cost=0)
+    q_core = by_core(q_out)
+    dn, dn_send, vec = summed([own, own, 16], [shared, shared_got], q, cost=0)
     dn_got = by_y(dn_send)
+    args = [dn, dn_got, tokens, d_first, gain_row, ab1]
     grad_tokens, done = call(
-        finish_kernel, [((own, D), F32), ((16, D), BF)], [], "v" * 6, 16, 6
-    )(dn, dn_got, tokens, d_first, gain_row, ab)
-    blocks = summed([3 * part] * 4, [q, q_got], ab)
-    q, *sends = [joined([block, vec]) for block in blocks]
-    q_got = (by_batch(sends[0], 1), by_y(sends[1]), by_both(sends[2]))
-    for i in range(1, len(steps)):
-        (ab,) = summed([half], [ab, ab_got], sends[2], done, cost=4)
-        if i + 1 < len(steps):
-            ab_got = by_batch(ab, steps[i + 1])
-    ab_got = by_batch(ab, steps[0])
-    rows_q = 3 * part + 16
-    (q,) = summed([rows_q], [q, *q_got], ab, cost=3)
-    q_got = by_batch(q, steps[0])
-    mine = joined([ab, ab_got], q, cost=2)
-    got = (by_batch(mine, 1), by_y(mine), by_both(mine))
-    (q,) = summed([rows_q], [q, q_got], mine, cost=3)
-    for step in steps[1:]:
-        q_got = by_batch(q, step)
-        (q,) = summed([rows_q], [q, q_got], cost=4)
-    q, vec = q[: 3 * part], q[3 * part :]
-    q_got = (by_batch(q, 1), by_y(q), by_both(q))
-    big = joined([mine, *got], cost=5)
+        finish_kernel, [((own, D), F32), ((16, D), BF)], [], "v" * len(args), 16, 6
+    )(*args)
+    blocks = summed([3 * part] * 4, [q, q_core], ab1, cost=0)
+    q0, *sends = [joined([block, vec]) for block in blocks]
+    q_xy = around(sends)
+    ab2 = through(ab1, z2_got, sends[2], done, cost=4)
+    back_got = by_batch(ab2, steps[0])
+    (q1,) = summed([rows_q], [q0, *q_xy], ab2, cost=3)
+    q_z1 = by_batch(q1, steps[0])
+    mine2 = joined([ab2, back_got], q1, cost=2)
+    xy_back = around([mine2] * 3)
+    (q2,) = summed([rows_q], [q1, q_z1], mine2, cost=3)
+    q_z2 = by_batch(q2, steps[1])
+    q3 = through(q2, q_z2, cost=0)
+    q4 = q3[: 3 * part]
+    q_back_got = around([q4] * 3)
+    big = joined([mine2, *xy_back], q3, cost=0)
     big_got = by_core(big)
-    q = joined([q, *q_got], cost=8)
-    q_got = by_core(q)
-    wide = ((D, D), F32)
-    attn_out, cross, mix, ens1, up, ens2, done = call(
+    args = [spot, big, big_got]
+    attn_out, cross, mix, ens1, up, ens2, done_big = call(
         unpack_kernel,
         [wide, wide, wide, ((4 * D, D), F32), ((D, FF), F32), ((FF + D, D), F32), ((16, D), BF)],
-        [], "vvv", 16, 3,
-    )(spot, big, big_got)
-    gain_one_g, query, key, value, b_cross_g, gain_two_g, b_up_g = call(
-        unpack_small_kernel, [row, wide, wide, wide, row, row, ((1, FF), F32)], [], "vvvvv", 16, 2
-    )(spot, q, q_got, vec, done)
+        [], "v" * len(args), 16, 3,
+    )(*args)
+    q5 = joined([q4, *q_back_got], done_big, cost=0)
+    q_last = by_core(q5)
+    args = [spot, q5, q_last, q3[3 * part :], done_big]
+    gain_one_g, query, key, value, b_cross_g, gain_two_g, b_up_g, done_small = call(
+        unpack_small_kernel, [row, wide, wide, wide, row, row, ((1, FF), F32), ((16, D), BF)],
+        [], "v" * len(args), 16, 2,
+    )(*args)
     return (
         out_rows, grad_tokens, gain_one_g.reshape(D), query, key, value, attn_out, cross, b_cross_g.reshape(D), mix,
         ens1, gain_two_g.reshape(D), up, b_up_g.reshape(FF), ens2,

time: 87.7 us -> 86.8 us (0.990)
  waiting for transfers between devices: 18.2 us -> 16.3 us
  Pallas kernels: 37.5 us -> 38.8 us
    ppermute x4, waiting for transfers between devices: 5.41 us -> 1.99 us  [by_both(): return lax.ppermute(value, ('batch', 'module'), pairs)]
    ppermute x22, waiting for transfers between devices: 12.8 us -> 14.3 us  [swap(): return lax.ppermute(value, axis, [(i, i ^ step) for i in range(count)])]
    ppermute x4, starting transfers between devices: 6.13 us -> 5 us  [by_both(): return lax.ppermute(value, ('batch', 'module'), pairs)]
    ppermute x22, starting transfers between devices: 23.6 us -> 24.6 us  [swap(): return lax.ppermute(value, axis, [(i, i ^ step) for i in range(count)])]
    pallas_call x2 -> x4, Pallas kernels: 13.3 us -> 13.9 us  [the longest x1 7.43 us: shards(): call(functools.partial(forward_kernel, own), [((16 * D, D), BF), ((own, D...]
  transfers between devices with their start and end apart: 26 -> 26, of which waited for: 13 -> 11; matrix products, arithmetic and copies ran while one was open for 0% -> 0% of each run, Pallas kernels for 27% -> 35%
where the time goes in v3:
time: 86.8 us; the launch traced here: 86.7 us
  Pallas kernels  38.8 us (45%)
  starting transfers between devices  29.6 us (34%)
  waiting for transfers between devices  16.3 us (19%)
  between operations  1.12 us (1%)
    ppermute x22, starting transfers between devices, swap(): return lax.ppermute(value, axis, [(i, i ^ step) for i in range(count)])  24.6 us
    ppermute x22, waiting for transfers between devices, swap(): return lax.ppermute(value, axis, [(i, i ^ step) for i in range(count)])  14.3 us
    pallas_call x4, Pallas kernels, head(): call(functools.partial(head_kernel, own, index), [((rows, LANES), BF), ((...  11.4 us
    pallas_call x1, Pallas kernels, shards(): call(functools.partial(forward_kernel, own), [((16 * D, D), BF), ((own, D...  7.43 us
    pallas_call x1, Pallas kernels, shards(): call(functools.partial(first_kernel, own), [((D, WIDE), BF), ((D, WIDE),...  5.35 us
    ppermute x4, starting transfers between devices, by_both(): return lax.ppermute(value, ('batch', 'module'), pairs)  5 us
    pallas_call x1, Pallas kernels, shards(): call(functools.partial(side_kernel, own), [((own, D), F32), ((own, D), F3...  3.48 us
    pallas_call x1, Pallas kernels, shards(): call(unpack_kernel, [wide, wide, wide, ((4 * D, D), F32), ((D, FF), F32),...  2.22 us
  transfers between devices with their start and end apart: 26, of which 11 were waited for; matrix products, arithmetic and copies ran while one was open for 0% of the time, Pallas kernels for 35%

profile of v3, /device:TPU:0, one launch (start us, length us, event | category | flops | bytes accessed | tf_op | source)
XLA Modules:
  0.0 86.7 jit_solution(1537869557057759460)
XLA Ops:
  1.2 2.6 %collective-permute-start = (bf16[512,256]{1,0:T(8,128)(2,1)}, bf16[512,256]{1,0:T(8,128)(2,1)S(1)}, u32[]{:S(2)}, u32[]{:S(2)}) collective-permute-start(bf16[512,256]{1,0:T(8,128)(2,1)} %tokens.5), channel_id=1, source_target_pairs={{0,2},{1,3},{2,0},{3,1},{4,6},{5,7},{6,4},{7,5},{8,10},{9,11},{10,... | collective-permute-start | bytes 786440 | tf_op jit(solution)/shard_map/ppermute | solution.py:597
  5.0 5.4 %shard_map.281 = (bf16[256,512]{1,0:T(8,128)(2,1)}, bf16[256,512]{1,0:T(8,128)(2,1)S(1)}, bf16[256,512]{1,0:T(8,128)(2,1)S(1)}, bf16[512,256]{1,0:T(8,128)(2,1)S...) custom-call(s32[8,128]{1,0:T(8,128)S(1)} %shard_map.280.spot, ...), custom_call_target="tpu_custom_call" | custom-call | flops 5000000000 | tf_op jit(solution)/shard_map/pallas_call | solution.py:675
  11.1 1.8 %shard_map.282 = (bf16[512,256]{1,0:T(8,128)(2,1)S(1)}, bf16[256,512]{1,0:T(8,128)(2,1)S(1)}, bf16[512,512]{1,0:T(8,128)(2,1)S(1)}, bf16[320,512]{1,0:T(8,128)(2,1)S(1)}, f32[320,512]{1,0:T(8,128)S(1)}) custom-call(bf16[512,256]{1,0:T(8,128)(2,1)S(1)} %collective-permute-done.y_rows, f32[1,256]{1,0:T(1,128)S(1)} %bitcast.16, ...), custom_call_target="tpu_custom_call" | custom-call | flops 2000000000 | tf_op jit(solution)/shard_map/pallas_call | solution.py:689
  13.0 7.4 %shard_map.283 = (bf16[4096,256]{1,0:T(8,128)(2,1)S(1)}, f32[512,256]{1,0:T(8,128)S(1)}, f32[16,256]{1,0:T(8,128)S(1)}, bf16[512,256]{1,0:T(8,128)(2,1)S(1)}, bf...) custom-call(s32[8,128]{1,0:T(8,128)S(1)} %shard_map.280.spot, ...), custom_call_target="tpu_custom_call" | custom-call | flops 8000000000 | tf_op jit(solution)/shard_map/pallas_call | solution.py:697
  21.0 3.5 %shard_map.284 = (f32[512,256]{1,0:T(8,128)}, f32[512,256]{1,0:T(8,128)S(1)}, f32[16,256]{1,0:T(8,128)S(1)}, bf16[2048,512]{1,0:T(8,128)(2,1)S(1)}, bf16[256,204...) custom-call(f32[512,256]{1,0:T(8,128)S(1)} %get-tuple-element.120.fi, ...), custom_call_target="tpu_custom_call" | custom-call | flops 3000000000 | tf_op jit(solution)/shard_map/pallas_call | solution.py:715
  24.7 1.8 %collective-permute-start.5 = (bf16[512,256]{1,0:T(8,128)(2,1)S(1)}, bf16[512,256]{1,0:T(8,128)(2,1)S(1)}, u32[]{:S(2)}, u32[]{:S(2)}) collective-permute-start(bf16[512,256]{1,0:T(8,128)(2,1)S(1)} %get-tuple-element.162), channel_id=1, source_target_pairs={{0,4},{4,0},{8,12},{12,8},{16,20},{20,16},{24,28},{28,24},{1,5},{5... | collective-permute-start | bytes 786440 | tf_op jit(solution)/shard_map/ppermute | solution.py:597
  28.3 2.8 %shard_map.286 = (bf16[2048,128]{1,0:T(8,128)(2,1)S(1)}, bf16[2048,128]{1,0:T(8,128)(2,1)S(1)}, bf16[64,512]{1,0:T(8,128)(2,1)S(1)}) custom-call(bf16[512,512]{1,0:T(8,128)(2,1)S(1)} %get-tuple-element.136.q_back, bf16[1024,512]{1,0:T(8,128)(2,1)S(1)} %get-tuple-element.113.k_a, bf16[512,512]{1,0:T(8,128)(2,1)S(1)} %get-tuple-element.114.k_y, ...), custom_call_target="tpu_custom_call" | custom-call | flops 2000000000 | tf_op jit(solution)/shard_map/pallas_call | solution.py:730
  31.1 3.0 %shard_map.287 = (bf16[2048,128]{1,0:T(8,128)(2,1)S(1)}, bf16[2048,128]{1,0:T(8,128)(2,1)S(1)}, bf16[64,512]{1,0:T(8,128)(2,1)S(1)}) custom-call(bf16[512,512]{1,0:T(8,128)(2,1)S(1)} %get-tuple-element.136.q_back, bf16[1024,512]{1,0:T(8,128)(2,1)S(1)} %get-tuple-element.113.k_a, bf16[512,512]{1,0:T(8,128)(2,1)S(1)} %get-tuple-element.114.k_y, ...), custom_call_target="tpu_custom_call" | custom-call | flops 2000000000 | tf_op jit(solution)/shard_map/pallas_call | solution.py:730
  34.1 2.8 %shard_map.288 = (bf16[2048,128]{1,0:T(8,128)(2,1)S(1)}, bf16[2048,128]{1,0:T(8,128)(2,1)S(1)}, bf16[64,512]{1,0:T(8,128)(2,1)S(1)}) custom-call(bf16[512,512]{1,0:T(8,128)(2,1)S(1)} %get-tuple-element.136.q_back, bf16[1024,512]{1,0:T(8,128)(2,1)S(1)} %get-tuple-element.113.k_a, bf16[512,512]{1,0:T(8,128)(2,1)S(1)} %get-tuple-element.114.k_y, ...), custom_call_target="tpu_custom_call" | custom-call | flops 2000000000 | tf_op jit(solution)/shard_map/pallas_call | solution.py:730
  36.9 2.8 %shard_map.289 = (bf16[2048,128]{1,0:T(8,128)(2,1)S(1)}, bf16[2048,128]{1,0:T(8,128)(2,1)S(1)}, bf16[64,512]{1,0:T(8,128)(2,1)S(1)}) custom-call(bf16[512,512]{1,0:T(8,128)(2,1)S(1)} %get-tuple-element.136.q_back, bf16[1024,512]{1,0:T(8,128)(2,1)S(1)} %get-tuple-element.113.k_a, bf16[512,512]{1,0:T(8,128)(2,1)S(1)} %get-tuple-element.114.k_y, ...), custom_call_target="tpu_custom_call" | custom-call | flops 2000000000 | tf_op jit(solution)/shard_map/pallas_call | solution.py:730
  39.7 2.0 %shard_map.290 = (bf16[2080,256]{1,0:T(8,128)(2,1)S(1)}, bf16[512,256]{1,0:T(8,128)(2,1)S(1)}) custom-call(bf16[2048,128]{1,0:T(8,128)(2,1)S(1)} %get-tuple-element.145.dk0, bf16[2048,128]{1,0:T(8,128)(2,1)S(1)} %get-tuple-element.147.dk1, bf16[2048,128]{1,0:T(8,128)(2,1)S(1)} %get-tuple-element.149.dk2, bf16[2048,128]{1,0:T(8,128)(2,1)S(1)} %get-tuple-element.151.dk3, ...), custom_call_target="tpu_custom_call" | custom-call | flops 3000000000 | tf_op jit(solution)/shard_map/pallas_call | solution.py:779
  42.0 1.9 %collective-permute-start.9 = (bf16[256,256]{1,0:T(8,128)(2,1)S(1)}, bf16[256,256]{1,0:T(8,128)(2,1)S(1)}, u32[]{:S(2)}, u32[]{:S(2)}) collective-permute-start(bf16[256,256]{1,0:T(8,128)(2,1)S(1)} %get-tuple-element.169), channel_id=1, source_target_pairs={{0,8},{4,12},{8,0},{12,4},{16,24},{20,28},{24,16},{28,20},{1,9},{5... | collective-permute-start | bytes 393224 | tf_op jit(solution)/shard_map/ppermute | solution.py:597
  45.4 1.6 %collective-permute-start.8 = (bf16[512,256]{1,0:T(8,128)(2,1)S(1)}, bf16[512,256]{1,0:T(8,128)(2,1)S(1)}, u32[]{:S(2)}, u32[]{:S(2)}) collective-permute-start(bf16[512,256]{1,0:T(8,128)(2,1)S(1)} %get-tuple-element.167), channel_id=1, source_target_pairs={{0,2},{1,3},{2,0},{3,1},{4,6},{5,7},{6,4},{7,5},{8,10},{9,11},{10,... | collective-permute-start | bytes 786440 | tf_op jit(solution)/shard_map/ppermute | solution.py:597
  48.1 2.8 %collective-permute-start.14 = (bf16[256,256]{1,0:T(8,128)(2,1)S(1)}, bf16[256,256]{1,0:T(8,128)(2,1)S(1)}, u32[]{:S(2)}, u32[]{:S(2)}) collective-permute-start(bf16[256,256]{1,0:T(8,128)(2,1)S(1)} %shard_map.294.rest_0_.refs_1_.refs_2_.refs_0_), channel_id=1, source_target_pairs={{0,16},{4,20},{8,24},{12,28},{16,0},{20,4},{24,8},{28,12},{1,17},{... | collective-permute-start | bytes 393224 | tf_op jit(solution)/shard_map/ppermute | solution.py:597
  51.0 1.6 %collective-permute-start.11 = (bf16[112,256]{1,0:T(8,128)(2,1)S(1)}, bf16[112,256]{1,0:T(8,128)(2,1)S(1)}, u32[]{:S(2)}, u32[]{:S(2)}) collective-permute-start(bf16[112,256]{1,0:T(8,128)(2,1)S(1)} %shard_map.299), channel_id=1, source_target_pairs={{0,4},{4,0},{8,12},{12,8},{16,20},{20,16},{24,28},{28,24},{1,5},{5... | collective-permute-start | bytes 172040 | tf_op jit(solution)/shard_map/ppermute | solution.py:597
  55.8 2.0 %collective-permute-done.14.refs_1_ = bf16[256,256]{1,0:T(8,128)(2,1)S(1)} collective-permute-done((bf16[256,256]{1,0:T(8,128)(2,1)S(1)}, bf16[256,256]{1,0:T(8,128)(2,1)S(1)}, u32[]{:S(2)}, u32[]{:S(2)}) %collective-permute-start.14) | collective-permute-done | bytes 131104 | tf_op jit(solution)/shard_map/ppermute | solution.py:597
  59.2 1.6 %collective-permute-start.15 = (bf16[112,256]{1,0:T(8,128)(2,1)S(1)}, bf16[112,256]{1,0:T(8,128)(2,1)S(1)}, u32[]{:S(2)}, u32[]{:S(2)}) collective-permute-start(bf16[112,256]{1,0:T(8,128)(2,1)S(1)} %shard_map.303.refs_2_.refs_0_), channel_id=1, source_target_pairs={{0,8},{4,12},{8,0},{12,4},{16,24},{20,28},{24,16},{28,20},{1,9},{5... | collective-permute-start | bytes 172040 | tf_op jit(solution)/shard_map/ppermute | solution.py:597
  60.9 2.8 %collective-permute-done.16.refs_1_ = bf16[256,256]{1,0:T(8,128)(2,1)S(1)} collective-permute-done((bf16[256,256]{1,0:T(8,128)(2,1)S(1)}, bf16[256,256]{1,0:T(8,128)(2,1)S(1)}, u32[]{:S(2)}, u32[]{:S(2)}) %collective-permute-start.16) | collective-permute-done | bytes 131104 | tf_op jit(solution)/shard_map/ppermute | solution.py:597
  63.7 2.5 %collective-permute-start.23 = (bf16[512,256]{1,0:T(8,128)(2,1)S(1)}, bf16[512,256]{1,0:T(8,128)(2,1)S(1)}, u32[]{:S(2)}, u32[]{:S(2)}) collective-permute-start(bf16[512,256]{1,0:T(8,128)(2,1)S(1)} %shard_map.304.refs_2_.refs_0_), channel_id=1, source_target_pairs={{0,6},{1,7},{2,4},{3,5},{4,2},{5,3},{6,0},{7,1},{8,14},{9,15},{10,... | collective-permute-start | bytes 786440 | tf_op jit(solution)/shard_map/ppermute | solution.py:750
  67.3 2.7 %collective-permute-start.17 = (bf16[112,256]{1,0:T(8,128)(2,1)S(1)}, bf16[112,256]{1,0:T(8,128)(2,1)S(1)}, u32[]{:S(2)}, u32[]{:S(2)}) collective-permute-start(bf16[112,256]{1,0:T(8,128)(2,1)S(1)} %shard_map.305.refs_0_), channel_id=1, source_target_pairs={{0,16},{4,20},{8,24},{12,28},{16,0},{20,4},{24,8},{28,12},{1,17},{... | collective-permute-start | bytes 172040 | tf_op jit(solution)/shard_map/ppermute | solution.py:597
  70.0 2.5 %collective-permute-done.17.refs_1_ = bf16[112,256]{1,0:T(8,128)(2,1)S(1)} collective-permute-done((bf16[112,256]{1,0:T(8,128)(2,1)S(1)}, bf16[112,256]{1,0:T(8,128)(2,1)S(1)}, u32[]{:S(2)}, u32[]{:S(2)}) %collective-permute-start.17) | collective-permute-done | bytes 57376 | tf_op jit(solution)/shard_map/ppermute | solution.py:597
  74.0 2.8 %collective-permute-done.22.refs_2_ = bf16[512,256]{1,0:T(8,128)(2,1)S(1)} collective-permute-done((bf16[512,256]{1,0:T(8,128)(2,1)S(1)}, bf16[512,256]{1,0:T(8,128)(2,1)S(1)}, u32[]{:S(2)}, u32[]{:S(2)}) %collective-permute-start.22) | collective-permute-done | bytes 262176 | tf_op jit(solution)/shard_map/ppermute | solution.py:597
  77.0 1.8 %collective-permute-start.20 = (bf16[96,256]{1,0:T(8,128)(2,1)S(1)}, bf16[96,256]{1,0:T(8,128)(2,1)S(1)}, u32[]{:S(2)}, u32[]{:S(2)}) collective-permute-start(bf16[96,256]{1,0:T(8,128)(2,1)S(1)} %slice.25.refs_0_), channel_id=1, source_target_pairs={{0,6},{1,7},{2,4},{3,5},{4,2},{5,3},{6,0},{7,1},{8,14},{9,15},{10,... | collective-permute-start | bytes 147464 | tf_op jit(solution)/shard_map/ppermute | solution.py:750
  80.5 2.2 %shard_map.308 = (f32[256,256]{1,0:T(8,128)}, f32[256,256]{1,0:T(8,128)}, f32[256,256]{1,0:T(8,128)}, f32[1024,256]{1,0:T(8,128)}, f32[256,1024]{1,0:T(8,128)}, ...) custom-call(s32[8,128]{1,0:T(8,128)S(1)} %shard_map.280.spot, bf16[2048,256]{1,0:T(8,128)(2,1)S(1)} %shard_map.307.mine, ...), custom_call_target="tpu_custom_call" | custom-call | flops 3000000000 | tf_op jit(solution)/shard_map/pallas_call | solution.py:821
  (101 shorter events, 20.9 us)
Async XLA Ops:
  0.6 3.8 %collective-permute-start.1 = (bf16[512,256]{1,0:T(8,128)(2,1)}, bf16[512,256]{1,0:T(8,128)(2,1)S(1)}, u32[]{:S(2)}, u32[]{:S(2)}) collective-permute-start(bf16[512,256]{1,0:T(8,128)(2,1)} %tokens.5), channel_id=1, source_target_pairs={{0,1},{1,0},{2,3},{3,2},{4,5},{5,4},{6,7},{7,6},{8,9},{9,8},{10,11... | collective-permute-start | bytes 786440 | tf_op jit(solution)/shard_map/ppermute | solution.py:597
  1.2 9.7 %collective-permute-start = (bf16[512,256]{1,0:T(8,128)(2,1)}, bf16[512,256]{1,0:T(8,128)(2,1)S(1)}, u32[]{:S(2)}, u32[]{:S(2)}) collective-permute-start(bf16[512,256]{1,0:T(8,128)(2,1)} %tokens.5), channel_id=1, source_target_pairs={{0,2},{1,3},{2,0},{3,1},{4,6},{5,7},{6,4},{7,5},{8,10},{9,11},{10,... | collective-permute-start | bytes 786440 | tf_op jit(solution)/shard_map/ppermute | solution.py:597
  20.5 4.0 %collective-permute-start.3 = (bf16[2048,256]{1,0:T(8,128)(2,1)S(1)}, bf16[2048,256]{1,0:T(8,128)(2,1)S(1)}, u32[]{:S(2)}, u32[]{:S(2)}) collective-permute-start(bf16[2048,256]{1,0:T(8,128)(2,1)S(1)} %slice.19), channel_id=1, source_target_pairs={{0,1},{1,0},{2,3},{3,2},{4,5},{5,4},{6,7},{7,6},{8,9},{9,8},{10,11... | collective-permute-start | bytes 3145736 | tf_op jit(solution)/shard_map/ppermute | solution.py:597
  24.7 17.1 %collective-permute-start.5 = (bf16[512,256]{1,0:T(8,128)(2,1)S(1)}, bf16[512,256]{1,0:T(8,128)(2,1)S(1)}, u32[]{:S(2)}, u32[]{:S(2)}) collective-permute-start(bf16[512,256]{1,0:T(8,128)(2,1)S(1)} %get-tuple-element.162), channel_id=1, source_target_pairs={{0,4},{4,0},{8,12},{12,8},{16,20},{20,16},{24,28},{28,24},{1,5},{5... | collective-permute-start | bytes 786440 | tf_op jit(solution)/shard_map/ppermute | solution.py:597
  26.5 15.3 %collective-permute-start.6 = (bf16[512,256]{1,0:T(8,128)(2,1)S(1)}, bf16[512,256]{1,0:T(8,128)(2,1)S(1)}, u32[]{:S(2)}, u32[]{:S(2)}) collective-permute-start(bf16[512,256]{1,0:T(8,128)(2,1)S(1)} %get-tuple-element.163), channel_id=1, source_target_pairs={{0,2},{1,3},{2,0},{3,1},{4,6},{5,7},{6,4},{7,5},{8,10},{9,11},{10,... | collective-permute-start | bytes 786440 | tf_op jit(solution)/shard_map/ppermute | solution.py:597
  28.0 13.8 %collective-permute-start.7 = (bf16[512,256]{1,0:T(8,128)(2,1)S(1)}, bf16[512,256]{1,0:T(8,128)(2,1)S(1)}, u32[]{:S(2)}, u32[]{:S(2)}) collective-permute-start(bf16[512,256]{1,0:T(8,128)(2,1)S(1)} %get-tuple-element.164), channel_id=1, source_target_pairs={{0,6},{1,7},{2,4},{3,5},{4,2},{5,3},{6,0},{7,1},{8,14},{9,15},{10,... | collective-permute-start | bytes 786440 | tf_op jit(solution)/shard_map/ppermute | solution.py:750
  41.7 3.6 %collective-permute-start.4 = (bf16[1040,256]{1,0:T(8,128)(2,1)S(1)}, bf16[1040,256]{1,0:T(8,128)(2,1)S(1)}, u32[]{:S(2)}, u32[]{:S(2)}) collective-permute-start(bf16[1040,256]{1,0:T(8,128)(2,1)S(1)} %slice.20), channel_id=1, source_target_pairs={{0,1},{1,0},{2,3},{3,2},{4,5},{5,4},{6,7},{7,6},{8,9},{9,8},{10,11... | collective-permute-start | bytes 1597448 | tf_op jit(solution)/shard_map/ppermute | solution.py:597
  42.0 6.0 %collective-permute-start.9 = (bf16[256,256]{1,0:T(8,128)(2,1)S(1)}, bf16[256,256]{1,0:T(8,128)(2,1)S(1)}, u32[]{:S(2)}, u32[]{:S(2)}) collective-permute-start(bf16[256,256]{1,0:T(8,128)(2,1)S(1)} %get-tuple-element.169), channel_id=1, source_target_pairs={{0,8},{4,12},{8,0},{12,4},{16,24},{20,28},{24,16},{28,20},{1,9},{5... | collective-permute-start | bytes 393224 | tf_op jit(solution)/shard_map/ppermute | solution.py:597
  45.4 9.2 %collective-permute-start.8 = (bf16[512,256]{1,0:T(8,128)(2,1)S(1)}, bf16[512,256]{1,0:T(8,128)(2,1)S(1)}, u32[]{:S(2)}, u32[]{:S(2)}) collective-permute-start(bf16[512,256]{1,0:T(8,128)(2,1)S(1)} %get-tuple-element.167), channel_id=1, source_target_pairs={{0,2},{1,3},{2,0},{3,1},{4,6},{5,7},{6,4},{7,5},{8,10},{9,11},{10,... | collective-permute-start | bytes 786440 | tf_op jit(solution)/shard_map/ppermute | solution.py:597
  48.0 2.9 %collective-permute-start.10 = (bf16[384,256]{1,0:T(8,128)(2,1)S(1)}, bf16[384,256]{1,0:T(8,128)(2,1)S(1)}, u32[]{:S(2)}, u32[]{:S(2)}) collective-permute-start(bf16[384,256]{1,0:T(8,128)(2,1)S(1)} %shard_map.296), channel_id=1, source_target_pairs={{0,1},{1,0},{2,3},{3,2},{4,5},{5,4},{6,7},{7,6},{8,9},{9,8},{10,11... | collective-permute-start | bytes 589832 | tf_op jit(solution)/shard_map/ppermute | solution.py:597
  48.1 9.7 %collective-permute-start.14 = (bf16[256,256]{1,0:T(8,128)(2,1)S(1)}, bf16[256,256]{1,0:T(8,128)(2,1)S(1)}, u32[]{:S(2)}, u32[]{:S(2)}) collective-permute-start(bf16[256,256]{1,0:T(8,128)(2,1)S(1)} %shard_map.294.rest_0_.refs_1_.refs_2_.refs_0_), channel_id=1, source_target_pairs={{0,16},{4,20},{8,24},{12,28},{16,0},{20,4},{24,8},{28,12},{1,17},{... | collective-permute-start | bytes 393224 | tf_op jit(solution)/shard_map/ppermute | solution.py:597
  51.0 7.6 %collective-permute-start.11 = (bf16[112,256]{1,0:T(8,128)(2,1)S(1)}, bf16[112,256]{1,0:T(8,128)(2,1)S(1)}, u32[]{:S(2)}, u32[]{:S(2)}) collective-permute-start(bf16[112,256]{1,0:T(8,128)(2,1)S(1)} %shard_map.299), channel_id=1, source_target_pairs={{0,4},{4,0},{8,12},{12,8},{16,20},{20,16},{24,28},{28,24},{1,5},{5... | collective-permute-start | bytes 172040 | tf_op jit(solution)/shard_map/ppermute | solution.py:597
  52.6 6.1 %collective-permute-start.12 = (bf16[112,256]{1,0:T(8,128)(2,1)S(1)}, bf16[112,256]{1,0:T(8,128)(2,1)S(1)}, u32[]{:S(2)}, u32[]{:S(2)}) collective-permute-start(bf16[112,256]{1,0:T(8,128)(2,1)S(1)} %shard_map.300), channel_id=1, source_target_pairs={{0,2},{1,3},{2,0},{3,1},{4,6},{5,7},{6,4},{7,5},{8,10},{9,11},{10,... | collective-permute-start | bytes 172040 | tf_op jit(solution)/shard_map/ppermute | solution.py:597
  54.1 5.1 %collective-permute-start.13 = (bf16[112,256]{1,0:T(8,128)(2,1)S(1)}, bf16[112,256]{1,0:T(8,128)(2,1)S(1)}, u32[]{:S(2)}, u32[]{:S(2)}) collective-permute-start(bf16[112,256]{1,0:T(8,128)(2,1)S(1)} %shard_map.301.refs_2_), channel_id=1, source_target_pairs={{0,6},{1,7},{2,4},{3,5},{4,2},{5,3},{6,0},{7,1},{8,14},{9,15},{10,... | collective-permute-start | bytes 172040 | tf_op jit(solution)/shard_map/ppermute | solution.py:750
  57.9 5.9 %collective-permute-start.16 = (bf16[256,256]{1,0:T(8,128)(2,1)S(1)}, bf16[256,256]{1,0:T(8,128)(2,1)S(1)}, u32[]{:S(2)}, u32[]{:S(2)}) collective-permute-start(bf16[256,256]{1,0:T(8,128)(2,1)S(1)} %shard_map.302.refs_4_.refs_0_), channel_id=1, source_target_pairs={{0,8},{4,12},{8,0},{12,4},{16,24},{20,28},{24,16},{28,20},{1,9},{5... | collective-permute-start | bytes 393224 | tf_op jit(solution)/shard_map/ppermute | solution.py:597
  59.2 8.1 %collective-permute-start.15 = (bf16[112,256]{1,0:T(8,128)(2,1)S(1)}, bf16[112,256]{1,0:T(8,128)(2,1)S(1)}, u32[]{:S(2)}, u32[]{:S(2)}) collective-permute-start(bf16[112,256]{1,0:T(8,128)(2,1)S(1)} %shard_map.303.refs_2_.refs_0_), channel_id=1, source_target_pairs={{0,8},{4,12},{8,0},{12,4},{16,24},{20,28},{24,16},{28,20},{1,9},{5... | collective-permute-start | bytes 172040 | tf_op jit(solution)/shard_map/ppermute | solution.py:597
  63.7 10.2 %collective-permute-start.23 = (bf16[512,256]{1,0:T(8,128)(2,1)S(1)}, bf16[512,256]{1,0:T(8,128)(2,1)S(1)}, u32[]{:S(2)}, u32[]{:S(2)}) collective-permute-start(bf16[512,256]{1,0:T(8,128)(2,1)S(1)} %shard_map.304.refs_2_.refs_0_), channel_id=1, source_target_pairs={{0,6},{1,7},{2,4},{3,5},{4,2},{5,3},{6,0},{7,1},{8,14},{9,15},{10,... | collective-permute-start | bytes 786440 | tf_op jit(solution)/shard_map/ppermute | solution.py:750
  66.2 10.6 %collective-permute-start.22 = (bf16[512,256]{1,0:T(8,128)(2,1)S(1)}, bf16[512,256]{1,0:T(8,128)(2,1)S(1)}, u32[]{:S(2)}, u32[]{:S(2)}) collective-permute-start(bf16[512,256]{1,0:T(8,128)(2,1)S(1)} %shard_map.304.refs_2_.refs_0_), channel_id=1, source_target_pairs={{0,2},{1,3},{2,0},{3,1},{4,6},{5,7},{6,4},{7,5},{8,10},{9,11},{10,... | collective-permute-start | bytes 786440 | tf_op jit(solution)/shard_map/ppermute | solution.py:597
  66.7 10.1 %collective-permute-start.21 = (bf16[512,256]{1,0:T(8,128)(2,1)S(1)}, bf16[512,256]{1,0:T(8,128)(2,1)S(1)}, u32[]{:S(2)}, u32[]{:S(2)}) collective-permute-start(bf16[512,256]{1,0:T(8,128)(2,1)S(1)} %shard_map.304.refs_2_.refs_0_), channel_id=1, source_target_pairs={{0,4},{4,0},{8,12},{12,8},{16,20},{20,16},{24,28},{28,24},{1,5},{5... | collective-permute-start | bytes 786440 | tf_op jit(solution)/shard_map/ppermute | solution.py:597
  67.3 5.1 %collective-permute-start.17 = (bf16[112,256]{1,0:T(8,128)(2,1)S(1)}, bf16[112,256]{1,0:T(8,128)(2,1)S(1)}, u32[]{:S(2)}, u32[]{:S(2)}) collective-permute-start(bf16[112,256]{1,0:T(8,128)(2,1)S(1)} %shard_map.305.refs_0_), channel_id=1, source_target_pairs={{0,16},{4,20},{8,24},{12,28},{16,0},{20,4},{24,8},{28,12},{1,17},{... | collective-permute-start | bytes 172040 | tf_op jit(solution)/shard_map/ppermute | solution.py:597
  76.9 3.6 %collective-permute-start.24 = (bf16[2048,256]{1,0:T(8,128)(2,1)S(1)}, bf16[2048,256]{1,0:T(8,128)(2,1)S(1)}, u32[]{:S(2)}, u32[]{:S(2)}) collective-permute-start(bf16[2048,256]{1,0:T(8,128)(2,1)S(1)} %shard_map.307.mine), channel_id=1, source_target_pairs={{0,1},{1,0},{2,3},{3,2},{4,5},{5,4},{6,7},{7,6},{8,9},{9,8},{10,11... | collective-permute-start | bytes 3145736 | tf_op jit(solution)/shard_map/ppermute | solution.py:597
  77.0 5.8 %collective-permute-start.20 = (bf16[96,256]{1,0:T(8,128)(2,1)S(1)}, bf16[96,256]{1,0:T(8,128)(2,1)S(1)}, u32[]{:S(2)}, u32[]{:S(2)}) collective-permute-start(bf16[96,256]{1,0:T(8,128)(2,1)S(1)} %slice.25.refs_0_), channel_id=1, source_target_pairs={{0,6},{1,7},{2,4},{3,5},{4,2},{5,3},{6,0},{7,1},{8,14},{9,15},{10,... | collective-permute-start | bytes 147464 | tf_op jit(solution)/shard_map/ppermute | solution.py:750
  78.8 4.3 %collective-permute-start.19 = (bf16[96,256]{1,0:T(8,128)(2,1)S(1)}, bf16[96,256]{1,0:T(8,128)(2,1)S(1)}, u32[]{:S(2)}, u32[]{:S(2)}) collective-permute-start(bf16[96,256]{1,0:T(8,128)(2,1)S(1)} %slice.25.refs_0_), channel_id=1, source_target_pairs={{0,2},{1,3},{2,0},{3,1},{4,6},{5,7},{6,4},{7,5},{8,10},{9,11},{10,... | collective-permute-start | bytes 147464 | tf_op jit(solution)/shard_map/ppermute | solution.py:597
  79.9 4.1 %collective-permute-start.18 = (bf16[96,256]{1,0:T(8,128)(2,1)S(1)}, bf16[96,256]{1,0:T(8,128)(2,1)S(1)}, u32[]{:S(2)}, u32[]{:S(2)}) collective-permute-start(bf16[96,256]{1,0:T(8,128)(2,1)S(1)} %slice.25.refs_0_), channel_id=1, source_target_pairs={{0,4},{4,0},{8,12},{12,8},{16,20},{20,16},{24,28},{28,24},{1,5},{5... | collective-permute-start | bytes 147464 | tf_op jit(solution)/shard_map/ppermute | solution.py:597
  (19 other events, 27.8 us)

commit v4 on v3

--- a/solution.py
+++ b/solution.py
@@ -214,9 +214,9 @@
 
 def first_kernel(
     own_rows,
-    spot, seg, core_rows, tokens, valid, gain_one, wq, wk, wv, wo, w_cross, b_cross,
+    spot, seg, core_rows, tokens, valid, gain_one, wq, wk, wv, wo, w_cross, b_cross, cot, w_ens2,
     wq_pad, wk_pad, wv_pad, wo_pad, wk_t, wv_t, codes, real, counted,
-    normed, normed_t, q_aug, k_aug, vt, part, self_scores, crossed,
+    normed, normed_t, q_aug, k_aug, vt, part, self_scores, crossed, d_joint,
 ):
     me = jnp.max(spot[0:1, :])
     for step in range(4):
@@ -251,6 +251,7 @@
     product = high(q_aug[...]) * high(k_aug[:own_rows, :])
     self_scores[...] = head_sums(head_selector(), jnp.where(lanes_own < HEAD_DIM, product, 0.0))
     crossed[...] = dot(normed[:own_rows, :], w_cross[...]) + b_cross[...]
+    d_joint[...] = dot_nt(cot[...], w_ens2[...])
 
 
 def middle_kernel(
@@ -269,7 +270,7 @@
     own_rows,
     spot, far_rows, codes, real, counted, tokens, cot,
     gain_one, wk_pad, wo_pad, wv_t,
-    w_mix, w_ens1, gain_two, w_up, b_up, w_ens2,
+    w_mix, w_ens1, gain_two, w_up, b_up, d_joint,
     normed_a, normed_y, q_aug, k_a, k_y, vt_a, vt_y, part_y, self_scores, crossed,
     payload, d_first_out, vectors, normed_f, normed_tf, k_f,
     first_out, active_out, normed_two_out, d_modules_out, att_out, lse_out, member_out, counts_out,
@@ -359,12 +360,12 @@
     e2 = cot[...]
     put(dot_tn(active, e2))
     put(dot_tn(normed_two, e2))
-    d_inner = low(dot_nt(e2, w_ens2[:FF, :]) * slope)
+    d_inner = low(d_joint[:, :FF] * slope)
     b_up_grad = jnp.sum(high(d_inner), axis=0, keepdims=True)
     grad_up = dot_tn(normed_two, d_inner)
     for i in range(FF // D):
         put(grad_up[:, i * D : (i + 1) * D])
-    d_norm2 = dot_nt(e2, w_ens2[FF:, :]) + dot_nt(d_inner, w_up[...])
+    d_norm2 = d_joint[:, FF:] + dot_nt(d_inner, w_up[...])
     d_first = high(e2) + norm_back(d_norm2, unit_two, scale_two, gain_two[...])
     d_first_out[...] = d_first
     e1 = low(d_first)
@@ -388,10 +389,10 @@
 
 def side_kernel(
     own_rows,
-    first, active, normed_two, w_ens2, d_modules, att, lse, own_member, counts, vectors_in,
-    normed_a, normed_y, normed_f, normed_ta, normed_ty, normed_tf, q_aug, self_scores, crossed, real,
-    wv_pad, wk_t, wo_pad, w_cross, w_mix,
-    out_rows, dn_own, vectors, v_all, kt_all, q_back, grad_att, pself_out, dself_out, seg_grad_out,
+    d_modules, att, lse,
+    normed_a, normed_y, normed_f, normed_ta, normed_ty, normed_tf, q_aug, self_scores, real,
+    wv_pad, wk_t, wo_pad,
+    v_all, kt_all, q_back, grad_att, pself_out, dself_out,
 ):
     v_lane = lax.broadcasted_iota(jnp.int32, (1, WIDE), 1) & (LANES - 1)
     v_ones = jnp.where((v_lane >= HEAD_DIM) & (v_lane < HEAD_DIM + 3), 1.0, 0.0)
@@ -401,7 +402,6 @@
         v_all[at : at + count, :] = low(dot(normed[...], wv_pad[...]) + v_ones)
         kt_all[:, at : at + count] = low(dot(wk_t[...], flipped[...]))
         at += count
-    out_rows[...] = first[...] + (dot(active[...], w_ens2[:FF, :]) + dot(normed_two[...], w_ens2[FF:, :]))
     d_att = []
     for g in range(2):
         lanes = slice(g * 256, (g + 1) * 256)
@@ -415,17 +415,6 @@
     dp_self = head_sums(heads16, high(d_att) * high(v_all[:own_rows, :]))
     pself_out[...] = low(p_self)
     dself_out[...] = low(p_self * (dp_self - delta))
-    d_two = high(d_modules[:, 2 * D : 3 * D])
-    d_cross = low(d_two * high(normed_a[:own_rows, :]))
-    dn_own[...] = d_two * crossed[...] + dot_nt(d_cross, w_cross[...])
-    d_mixed = dot_nt(d_modules[:, 3 * D :], w_mix[...])
-    mixed_up = low(d_mixed)
-    mixed_down = low(d_mixed - high(mixed_up))
-    seg_grad = dot_tn(own_member[...], mixed_up) + dot_tn(own_member[...], mixed_down)
-    seg_grad_out[...] = seg_grad / counts[:, :1]
-    tail = lax.broadcasted_iota(jnp.int32, (16, D), 0)
-    b_cross_grad = jnp.sum(high(d_cross), axis=0, keepdims=True)
-    vectors[...] = jnp.where(tail == 4, b_cross_grad, vectors_in[...])
 
 
 def head_kernel(
@@ -466,19 +455,28 @@
 
 def rows_kernel(
     own_rows,
-    dk0, dk1, dk2, dk3, dv0, dv1, dv2, dv3, dq0, dq1, dq2, dq3, normed_a, normed_y, normed_f, counted, seg_grad, dn_own,
-    gain_one, wq, wk_pad, wv_pad, vectors,
+    dk0, dk1, dk2, dk3, dv0, dv1, dv2, dv3, dq0, dq1, dq2, dq3, normed_a, normed_y, normed_f, counted, d_modules, crossed,
+    w_cross, w_mix, own_member, counts, gain_one, wq, wk_pad, wv_pad, vectors,
     *rest,
 ):
     out, dq_out, dn = rest[-3:]
+    d_two = high(d_modules[:, 2 * D : 3 * D])
+    d_cross = low(d_two * high(normed_a[:own_rows, :]))
+    dn_own = d_two * crossed[...] + dot_nt(d_cross, w_cross[...])
+    b_cross_grad = jnp.sum(high(d_cross), axis=0, keepdims=True)
+    d_mixed = dot_nt(d_modules[:, 3 * D :], w_mix[...])
+    mixed_up = low(d_mixed)
+    mixed_down = low(d_mixed - high(mixed_up))
+    seg_grad = dot_tn(own_member[...], mixed_up) + dot_tn(own_member[...], mixed_down)
+    seg_grad = seg_grad / counts[:, :1]
     half_keys = 2 * own_rows
     dq = jnp.concatenate([high(part[...]) for part in (dq0, dq1, dq2, dq3)], axis=0)
     dq_rows = low(dq.T)
     dq_out[...] = dq_rows
     dk_pairs = [jnp.concatenate([dk0[...], dk1[...]], axis=1), jnp.concatenate([dk2[...], dk3[...]], axis=1)]
     dv_pairs = [jnp.concatenate([dv0[...], dv1[...]], axis=1), jnp.concatenate([dv2[...], dv3[...]], axis=1)]
-    up = low(seg_grad[...])
-    down = low(seg_grad[...] - high(up))
+    up = low(seg_grad)
+    down = low(seg_grad - high(up))
     for c in range(2):
         at = slice(c * half_keys, (c + 1) * half_keys)
         mixing = dot_tn(counted[:, at], up) + dot_tn(counted[:, at], down)
@@ -488,7 +486,7 @@
             + dot_nt(dv_pairs[0][at, :], wv_pad[:, :256])
             + dot_nt(dv_pairs[1][at, :], wv_pad[:, 256:])
         )
-    dn[:own_rows, :] = dn[:own_rows, :] + (dot_nt(dq_rows, wq[...]) + dn_own[...])
+    dn[:own_rows, :] = dn[:own_rows, :] + (dot_nt(dq_rows, wq[...]) + dn_own)
     gain_grad = jnp.sum(dn[:half_keys, :] * high(normed_a[...]), axis=0, keepdims=True)
     for i, normed in enumerate((normed_y, normed_f)):
         here = dn[(2 + i) * own_rows : (3 + i) * own_rows, :]
@@ -499,7 +497,7 @@
         at = (step % 2) * count + (step // 2) * own_rows
         out[at : at + own_rows, :] = low(dn[step * own_rows : (step + 1) * own_rows, :])
     tail = lax.broadcasted_iota(jnp.int32, (16, D), 0)
-    row = jnp.where(tail == 6, gain_grad, vectors[...])
+    row = jnp.where(tail == 6, gain_grad, jnp.where(tail == 4, b_cross_grad, vectors[...]))
     out[count - 16 : count, :] = low(row)
     out[2 * count - 16 :, :] = low(row)
 
@@ -543,8 +541,11 @@
             out[pl.ds(pl.multiple_of(at, part), part), :] = low(grad[n * part : (n + 1) * part])
 
 
-def finish_kernel(mine, other, tokens, d_first, gain_one, *rest):
-    grad_tokens, done = rest[-2:]
+def finish_kernel(
+    mine, other, tokens, d_first, gain_one, first, active, normed_two, w_ens2, *rest
+):
+    grad_tokens, out_rows, done = rest[-3:]
+    out_rows[...] = first[...] + (dot(active[...], w_ens2[:FF, :]) + dot(normed_two[...], w_ens2[FF:, :]))
     unit, scale = unit_rows(high(tokens[...]))
     total = high(mine[...]) + high(other[...])
     grad_tokens[...] = d_first[...] + norm_back(total, unit, scale, gain_one[...])
@@ -671,7 +672,7 @@
     (spot,) = call(start_kernel, [((8, LANES), jnp.int32)], [], "s", 4, 20)(me)
     (
         wq_pad, wk_pad, wv_pad, wo_pad, wk_t, wv_t, codes, real, counted,
-        normed_a, normed_ta, q_aug, k_a, vt_a, part_a, self_scores, crossed,
+        normed_a, normed_ta, q_aug, k_a, vt_a, part_a, self_scores, crossed, d_joint,
     ) = call(
         functools.partial(first_kernel, own),
         [
@@ -679,11 +680,12 @@
             ((rows, LANES), BF), ((1, rows), F32), ((16, rows), BF),
             ((keys, D), BF), ((D, keys), BF), ((own, WIDE), BF), ((keys, WIDE), BF),
             ((HEADS * TALL, keys), BF), ((HEADS * TALL, own), F32), ((16, own), F32), ((own, D), F32),
+            ((own, FF + D), F32),
         ],
-        [], "vs" + "v" * 10, 16, 5,
+        [], "vs" + "v" * 12, 16, 5,
     )(
         spot, seg_lengths, from_core, tokens, valid_row, gain_row, w_query, w_key, w_value, w_attn_out,
-        w_cross, b_cross.reshape(1, D),
+        w_cross, b_cross.reshape(1, D), cotangent, w_ens2,
     )
     from_far = by_core(jnp.concatenate([from_y, normed_a[:16]], axis=0))
     normed_y, normed_ty, k_y, vt_y, part_y = call(
@@ -708,21 +710,19 @@
         "v" * 27, 32, 8,
     )(
         spot, from_far, codes, real, counted, tokens, cotangent, gain_row, wk_pad, wo_pad, wv_t,
-        w_mix, w_ens1, gain_two.reshape(1, D), w_up, b_up.reshape(1, FF), w_ens2,
+        w_mix, w_ens1, gain_two.reshape(1, D), w_up, b_up.reshape(1, FF), d_joint,
         normed_a, normed_y, q_aug, k_a, k_y, vt_a, vt_y, part_y, self_scores, crossed,
     )
     big_got = by_core(payload[payload.shape[0] // 2 :])
-    out_rows, dn_own, vectors, v_all, kt_all, q_back, grad_att, pself, dself, seg_grad = call(
+    v_all, kt_all, q_back, grad_att, pself, dself = call(
         functools.partial(side_kernel, own),
         [
-            ((own, D), F32), ((own, D), F32), ((16, D), F32), ((rows, WIDE), BF), ((D, rows), BF),
-            ((own, WIDE), BF), ((own, WIDE), BF), ((16, own), BF), ((16, own), BF), ((16, D), F32),
+            ((rows, WIDE), BF), ((D, rows), BF), ((own, WIDE), BF), ((own, WIDE), BF), ((16, own), BF), ((16, own), BF),
         ],
-        [], "v" * 25, 16, 3,
+        [], "v" * 15, 16, 3,
     )(
-        first, active, normed_two, w_ens2, d_modules, att, lse, own_member, counts, vectors,
-        normed_a, normed_y, normed_f, normed_ta, normed_ty, normed_tf, q_aug, self_scores, crossed, real,
-        wv_pad, wk_t, wo_pad, w_cross, w_mix,
+        d_modules, att, lse, normed_a, normed_y, normed_f, normed_ta, normed_ty, normed_tf, q_aug, self_scores, real,
+        wv_pad, wk_t, wo_pad,
     )
 
     def head(index, *after, cost=0):
@@ -773,8 +773,8 @@
     dk2, dv2, dq2 = head(2, dq1, cost=2)
     dk3, dv3, dq3 = head(3, dq2, cost=2)
     args = [
-        dk0, dk1, dk2, dk3, dv0, dv1, dv2, dv3, dq0, dq1, dq2, dq3, normed_a, normed_y, normed_f, counted, seg_grad,
-        dn_own, gain_row, w_query, wk_pad, wv_pad, vectors,
+        dk0, dk1, dk2, dk3, dv0, dv1, dv2, dv3, dq0, dq1, dq2, dq3, normed_a, normed_y, normed_f, counted,
+        d_modules, crossed, w_cross, w_mix, own_member, counts, gain_row, w_query, wk_pad, wv_pad, vectors,
     ]
     shared, dq_rows = call(
         functools.partial(rows_kernel, own),
@@ -797,9 +797,9 @@
     q_core = by_core(q_out)
     dn, dn_send, vec = summed([own, own, 16], [shared, shared_got], q, cost=0)
     dn_got = by_y(dn_send)
-    args = [dn, dn_got, tokens, d_first, gain_row, ab1]
-    grad_tokens, done = call(
-        finish_kernel, [((own, D), F32), ((16, D), BF)], [], "v" * len(args), 16, 6
+    args = [dn, dn_got, tokens, d_first, gain_row, first, active, normed_two, w_ens2, ab1]
+    grad_tokens, out_rows, done = call(
+        finish_kernel, [((own, D), F32), ((own, D), F32), ((16, D), BF)], [], "v" * len(args), 16, 6
     )(*args)
     blocks = summed([3 * part] * 4, [q, q_core], ab1, cost=0)
     q0, *sends = [joined([block, vec]) for block in blocks]

time: 86.8 us -> 86.1 us (level)
  waiting for transfers between devices: 16.3 us -> 15.4 us
where the time goes in v4:
time: 86.1 us; the launch traced here: 86 us
  Pallas kernels  38.9 us (45%)
  starting transfers between devices  29.5 us (34%)
  waiting for transfers between devices  15.4 us (18%)
  between operations  1.07 us (1%)
  local copies, waits for them, and re-layouts  0.94 us (1%)
    ppermute x22, starting transfers between devices, swap(): return lax.ppermute(value, axis, [(i, i ^ step) for i in range(count)])  24.4 us
    ppermute x22, waiting for transfers between devices, swap(): return lax.ppermute(value, axis, [(i, i ^ step) for i in range(count)])  13.5 us
    pallas_call x4, Pallas kernels, head(): call(functools.partial(head_kernel, own, index), [((rows, LANES), BF), ((...  11.4 us
    pallas_call x1, Pallas kernels, shards(): call(functools.partial(forward_kernel, own), [((16 * D, D), BF), ((own, D...  7.03 us
    pallas_call x1, Pallas kernels, shards(): call(functools.partial(first_kernel, own), [((D, WIDE), BF), ((D, WIDE),...  5.75 us
    ppermute x4, starting transfers between devices, by_both(): return lax.ppermute(value, ('batch', 'module'), pairs)  5.12 us
    pallas_call x1, Pallas kernels, shards(): call(functools.partial(side_kernel, own), [((rows, WIDE), BF), ((D, rows)...  2.66 us
    pallas_call x1, Pallas kernels, shards(): call(functools.partial(rows_kernel, own), [((2 * count, D), BF), ((own, D...  2.5 us
  transfers between devices with their start and end apart: 26, of which 11 were waited for; matrix products, arithmetic and copies ran while one was open for 0% of the time, Pallas kernels for 35%

profile of v4, /device:TPU:0, one launch (start us, length us, event | category | flops | bytes accessed | tf_op | source)
XLA Modules:
  0.0 86.0 jit_solution(14536993415744877294)
XLA Ops:
  1.2 2.6 %collective-permute-start = (bf16[512,256]{1,0:T(8,128)(2,1)}, bf16[512,256]{1,0:T(8,128)(2,1)S(1)}, u32[]{:S(2)}, u32[]{:S(2)}) collective-permute-start(bf16[512,256]{1,0:T(8,128)(2,1)} %tokens.5), channel_id=1, source_target_pairs={{0,2},{1,3},{2,0},{3,1},{4,6},{5,7},{6,4},{7,5},{8,10},{9,11},{10,... | collective-permute-start | bytes 786440 | tf_op jit(solution)/shard_map/ppermute | solution.py:598
  5.3 5.7 %shard_map.281 = (bf16[256,512]{1,0:T(8,128)(2,1)}, bf16[256,512]{1,0:T(8,128)(2,1)S(1)}, bf16[256,512]{1,0:T(8,128)(2,1)S(1)}, bf16[512,256]{1,0:T(8,128)(2,1)S...) custom-call(s32[8,128]{1,0:T(8,128)S(1)} %shard_map.280.spot, ...), custom_call_target="tpu_custom_call" | custom-call | flops 5000000000 | tf_op jit(solution)/shard_map/pallas_call | solution.py:676
  11.3 1.8 %shard_map.282 = (bf16[512,256]{1,0:T(8,128)(2,1)S(1)}, bf16[256,512]{1,0:T(8,128)(2,1)S(1)}, bf16[512,512]{1,0:T(8,128)(2,1)S(1)}, bf16[320,512]{1,0:T(8,128)(2,1)S(1)}, f32[320,512]{1,0:T(8,128)S(1)}) custom-call(bf16[512,256]{1,0:T(8,128)(2,1)S(1)} %collective-permute-done.y_rows, f32[1,256]{1,0:T(1,128)S(1)} %bitcast.16, ...), custom_call_target="tpu_custom_call" | custom-call | flops 2000000000 | tf_op jit(solution)/shard_map/pallas_call | solution.py:691
  13.2 7.0 %shard_map.283 = (bf16[4096,256]{1,0:T(8,128)(2,1)S(1)}, f32[512,256]{1,0:T(8,128)S(1)}, f32[16,256]{1,0:T(8,128)S(1)}, bf16[512,256]{1,0:T(8,128)(2,1)S(1)}, bf...) custom-call(s32[8,128]{1,0:T(8,128)S(1)} %shard_map.280.spot, ...), custom_call_target="tpu_custom_call" | custom-call | flops 8000000000 | tf_op jit(solution)/shard_map/pallas_call | solution.py:699
  20.7 2.7 %shard_map.284 = (bf16[2048,512]{1,0:T(8,128)(2,1)S(1)}, bf16[256,2048]{1,0:T(8,128)(2,1)S(1)}, bf16[512,512]{1,0:T(8,128)(2,1)S(1)}, bf16[512,512]{1,0:T(8,128)...) custom-call(bf16[512,1024]{1,0:T(8,128)(2,1)S(1)} %get-tuple-element.119.d_modules, ...), custom_call_target="tpu_custom_call" | custom-call | flops 3000000000 | tf_op jit(solution)/shard_map/pallas_call | solution.py:717
  23.6 1.6 %collective-permute-start.5 = (bf16[512,256]{1,0:T(8,128)(2,1)S(1)}, bf16[512,256]{1,0:T(8,128)(2,1)S(1)}, u32[]{:S(2)}, u32[]{:S(2)}) collective-permute-start(bf16[512,256]{1,0:T(8,128)(2,1)S(1)} %get-tuple-element.154), channel_id=1, source_target_pairs={{0,4},{4,0},{8,12},{12,8},{16,20},{20,16},{24,28},{28,24},{1,5},{5... | collective-permute-start | bytes 786440 | tf_op jit(solution)/shard_map/ppermute | solution.py:598
  27.2 2.8 %shard_map.286 = (bf16[2048,128]{1,0:T(8,128)(2,1)S(1)}, bf16[2048,128]{1,0:T(8,128)(2,1)S(1)}, bf16[64,512]{1,0:T(8,128)(2,1)S(1)}) custom-call(bf16[512,512]{1,0:T(8,128)(2,1)S(1)} %get-tuple-element.128.q_back, bf16[1024,512]{1,0:T(8,128)(2,1)S(1)} %get-tuple-element.112.k_a, bf16[512,512]{1,0:T(8,128)(2,1)S(1)} %get-tuple-element.113.k_y, ...), custom_call_target="tpu_custom_call" | custom-call | flops 2000000000 | tf_op jit(solution)/shard_map/pallas_call | solution.py:730
  30.0 2.8 %shard_map.287 = (bf16[2048,128]{1,0:T(8,128)(2,1)S(1)}, bf16[2048,128]{1,0:T(8,128)(2,1)S(1)}, bf16[64,512]{1,0:T(8,128)(2,1)S(1)}) custom-call(bf16[512,512]{1,0:T(8,128)(2,1)S(1)} %get-tuple-element.128.q_back, bf16[1024,512]{1,0:T(8,128)(2,1)S(1)} %get-tuple-element.112.k_a, bf16[512,512]{1,0:T(8,128)(2,1)S(1)} %get-tuple-element.113.k_y, ...), custom_call_target="tpu_custom_call" | custom-call | flops 2000000000 | tf_op jit(solution)/shard_map/pallas_call | solution.py:730
  32.8 3.0 %shard_map.288 = (bf16[2048,128]{1,0:T(8,128)(2,1)S(1)}, bf16[2048,128]{1,0:T(8,128)(2,1)S(1)}, bf16[64,512]{1,0:T(8,128)(2,1)S(1)}) custom-call(bf16[512,512]{1,0:T(8,128)(2,1)S(1)} %get-tuple-element.128.q_back, bf16[1024,512]{1,0:T(8,128)(2,1)S(1)} %get-tuple-element.112.k_a, bf16[512,512]{1,0:T(8,128)(2,1)S(1)} %get-tuple-element.113.k_y, ...), custom_call_target="tpu_custom_call" | custom-call | flops 2000000000 | tf_op jit(solution)/shard_map/pallas_call | solution.py:730
  35.8 2.8 %shard_map.289 = (bf16[2048,128]{1,0:T(8,128)(2,1)S(1)}, bf16[2048,128]{1,0:T(8,128)(2,1)S(1)}, bf16[64,512]{1,0:T(8,128)(2,1)S(1)}) custom-call(bf16[512,512]{1,0:T(8,128)(2,1)S(1)} %get-tuple-element.128.q_back, bf16[1024,512]{1,0:T(8,128)(2,1)S(1)} %get-tuple-element.112.k_a, bf16[512,512]{1,0:T(8,128)(2,1)S(1)} %get-tuple-element.113.k_y, ...), custom_call_target="tpu_custom_call" | custom-call | flops 2000000000 | tf_op jit(solution)/shard_map/pallas_call | solution.py:730
  38.6 2.5 %shard_map.290 = (bf16[2080,256]{1,0:T(8,128)(2,1)S(1)}, bf16[512,256]{1,0:T(8,128)(2,1)S(1)}) custom-call(bf16[2048,128]{1,0:T(8,128)(2,1)S(1)} %get-tuple-element.137.dk0, bf16[2048,128]{1,0:T(8,128)(2,1)S(1)} %get-tuple-element.139.dk1, bf16[2048,128]{1,0:T(8,128)(2,1)S(1)} %get-tuple-element.141.dk2, bf16[2048,128]{1,0:T(8,128)(2,1)S(1)} %get-tuple-element.143.dk3, ...), custom_call_target="tpu_custom_call" | custom-call | flops 3000000000 | tf_op jit(solution)/shard_map/pallas_call | solution.py:779
  41.4 1.7 %collective-permute-start.9 = (bf16[256,256]{1,0:T(8,128)(2,1)S(1)}, bf16[256,256]{1,0:T(8,128)(2,1)S(1)}, u32[]{:S(2)}, u32[]{:S(2)}) collective-permute-start(bf16[256,256]{1,0:T(8,128)(2,1)S(1)} %get-tuple-element.164), channel_id=1, source_target_pairs={{0,8},{4,12},{8,0},{12,4},{16,24},{20,28},{24,16},{28,20},{1,9},{5... | collective-permute-start | bytes 393224 | tf_op jit(solution)/shard_map/ppermute | solution.py:598
  44.7 1.6 %collective-permute-start.8 = (bf16[512,256]{1,0:T(8,128)(2,1)S(1)}, bf16[512,256]{1,0:T(8,128)(2,1)S(1)}, u32[]{:S(2)}, u32[]{:S(2)}) collective-permute-start(bf16[512,256]{1,0:T(8,128)(2,1)S(1)} %get-tuple-element.159), channel_id=1, source_target_pairs={{0,2},{1,3},{2,0},{3,1},{4,6},{5,7},{6,4},{7,5},{8,10},{9,11},{10,... | collective-permute-start | bytes 786440 | tf_op jit(solution)/shard_map/ppermute | solution.py:598
  47.5 2.7 %collective-permute-start.14 = (bf16[256,256]{1,0:T(8,128)(2,1)S(1)}, bf16[256,256]{1,0:T(8,128)(2,1)S(1)}, u32[]{:S(2)}, u32[]{:S(2)}) collective-permute-start(bf16[256,256]{1,0:T(8,128)(2,1)S(1)} %shard_map.294.rest_0_.refs_1_.refs_2_.refs_0_), channel_id=1, source_target_pairs={{0,16},{4,20},{8,24},{12,28},{16,0},{20,4},{24,8},{28,12},{1,17},{... | collective-permute-start | bytes 393224 | tf_op jit(solution)/shard_map/ppermute | solution.py:598
  53.9 1.6 %shard_map.295 = (f32[512,256]{1,0:T(8,128)}, f32[512,256]{1,0:T(8,128)}, bf16[16,256]{1,0:T(8,128)(2,1)S(1)}) custom-call(bf16[512,256]{1,0:T(8,128)(2,1)S(1)} %get-tuple-element.158.mine, bf16[512,256]{1,0:T(8,128)(2,1)S(1)} %collective-permute-done.8.other, bf16[512,256]{1,0:T(8,128)(2,1)S(1)} %copy-done.4, f32[512,256]{1,0:T(8,128)S(1)} %get-tuple-element.160.d_first, ...), custom_call_target="tpu_custom_call" | custom-call | flops 6000000000 | tf_op jit(solution)/shard_map/pallas_call | solution.py:801
  55.4 1.7 %collective-permute-done.14.refs_1_ = bf16[256,256]{1,0:T(8,128)(2,1)S(1)} collective-permute-done((bf16[256,256]{1,0:T(8,128)(2,1)S(1)}, bf16[256,256]{1,0:T(8,128)(2,1)S(1)}, u32[]{:S(2)}, u32[]{:S(2)}) %collective-permute-start.14) | collective-permute-done | bytes 131104 | tf_op jit(solution)/shard_map/ppermute | solution.py:598
  58.5 1.6 %collective-permute-start.15 = (bf16[112,256]{1,0:T(8,128)(2,1)S(1)}, bf16[112,256]{1,0:T(8,128)(2,1)S(1)}, u32[]{:S(2)}, u32[]{:S(2)}) collective-permute-start(bf16[112,256]{1,0:T(8,128)(2,1)S(1)} %shard_map.303.refs_2_.refs_0_), channel_id=1, source_target_pairs={{0,8},{4,12},{8,0},{12,4},{16,24},{20,28},{24,16},{28,20},{1,9},{5... | collective-permute-start | bytes 172040 | tf_op jit(solution)/shard_map/ppermute | solution.py:598
  60.2 2.8 %collective-permute-done.16.refs_1_ = bf16[256,256]{1,0:T(8,128)(2,1)S(1)} collective-permute-done((bf16[256,256]{1,0:T(8,128)(2,1)S(1)}, bf16[256,256]{1,0:T(8,128)(2,1)S(1)}, u32[]{:S(2)}, u32[]{:S(2)}) %collective-permute-start.16) | collective-permute-done | bytes 131104 | tf_op jit(solution)/shard_map/ppermute | solution.py:598
  62.9 2.6 %collective-permute-start.23 = (bf16[512,256]{1,0:T(8,128)(2,1)S(1)}, bf16[512,256]{1,0:T(8,128)(2,1)S(1)}, u32[]{:S(2)}, u32[]{:S(2)}) collective-permute-start(bf16[512,256]{1,0:T(8,128)(2,1)S(1)} %shard_map.304.refs_2_.refs_0_), channel_id=1, source_target_pairs={{0,6},{1,7},{2,4},{3,5},{4,2},{5,3},{6,0},{7,1},{8,14},{9,15},{10,... | collective-permute-start | bytes 786440 | tf_op jit(solution)/shard_map/ppermute | solution.py:750
  66.5 2.8 %collective-permute-start.17 = (bf16[112,256]{1,0:T(8,128)(2,1)S(1)}, bf16[112,256]{1,0:T(8,128)(2,1)S(1)}, u32[]{:S(2)}, u32[]{:S(2)}) collective-permute-start(bf16[112,256]{1,0:T(8,128)(2,1)S(1)} %shard_map.305.refs_0_), channel_id=1, source_target_pairs={{0,16},{4,20},{8,24},{12,28},{16,0},{20,4},{24,8},{28,12},{1,17},{... | collective-permute-start | bytes 172040 | tf_op jit(solution)/shard_map/ppermute | solution.py:598
  69.3 2.4 %collective-permute-done.17.refs_1_ = bf16[112,256]{1,0:T(8,128)(2,1)S(1)} collective-permute-done((bf16[112,256]{1,0:T(8,128)(2,1)S(1)}, bf16[112,256]{1,0:T(8,128)(2,1)S(1)}, u32[]{:S(2)}, u32[]{:S(2)}) %collective-permute-start.17) | collective-permute-done | bytes 57376 | tf_op jit(solution)/shard_map/ppermute | solution.py:598
  73.1 2.8 %collective-permute-done.22.refs_2_ = bf16[512,256]{1,0:T(8,128)(2,1)S(1)} collective-permute-done((bf16[512,256]{1,0:T(8,128)(2,1)S(1)}, bf16[512,256]{1,0:T(8,128)(2,1)S(1)}, u32[]{:S(2)}, u32[]{:S(2)}) %collective-permute-start.22) | collective-permute-done | bytes 262176 | tf_op jit(solution)/shard_map/ppermute | solution.py:598
  76.2 1.7 %collective-permute-start.20 = (bf16[96,256]{1,0:T(8,128)(2,1)S(1)}, bf16[96,256]{1,0:T(8,128)(2,1)S(1)}, u32[]{:S(2)}, u32[]{:S(2)}) collective-permute-start(bf16[96,256]{1,0:T(8,128)(2,1)S(1)} %slice.25.refs_0_), channel_id=1, source_target_pairs={{0,6},{1,7},{2,4},{3,5},{4,2},{5,3},{6,0},{7,1},{8,14},{9,15},{10,... | collective-permute-start | bytes 147464 | tf_op jit(solution)/shard_map/ppermute | solution.py:750
  79.7 2.2 %shard_map.308 = (f32[256,256]{1,0:T(8,128)}, f32[256,256]{1,0:T(8,128)}, f32[256,256]{1,0:T(8,128)}, f32[1024,256]{1,0:T(8,128)}, f32[256,1024]{1,0:T(8,128)}, ...) custom-call(s32[8,128]{1,0:T(8,128)S(1)} %shard_map.280.spot, bf16[2048,256]{1,0:T(8,128)(2,1)S(1)} %shard_map.307.mine, ...), custom_call_target="tpu_custom_call" | custom-call | flops 3000000000 | tf_op jit(solution)/shard_map/pallas_call | solution.py:821
  (101 shorter events, 21.4 us)
Async XLA Ops:
  0.6 3.9 %collective-permute-start.1 = (bf16[512,256]{1,0:T(8,128)(2,1)}, bf16[512,256]{1,0:T(8,128)(2,1)S(1)}, u32[]{:S(2)}, u32[]{:S(2)}) collective-permute-start(bf16[512,256]{1,0:T(8,128)(2,1)} %tokens.5), channel_id=1, source_target_pairs={{0,1},{1,0},{2,3},{3,2},{4,5},{5,4},{6,7},{7,6},{8,9},{9,8},{10,11... | collective-permute-start | bytes 786440 | tf_op jit(solution)/shard_map/ppermute | solution.py:598
  1.2 9.9 %collective-permute-start = (bf16[512,256]{1,0:T(8,128)(2,1)}, bf16[512,256]{1,0:T(8,128)(2,1)S(1)}, u32[]{:S(2)}, u32[]{:S(2)}) collective-permute-start(bf16[512,256]{1,0:T(8,128)(2,1)} %tokens.5), channel_id=1, source_target_pairs={{0,2},{1,3},{2,0},{3,1},{4,6},{5,7},{6,4},{7,5},{8,10},{9,11},{10,... | collective-permute-start | bytes 786440 | tf_op jit(solution)/shard_map/ppermute | solution.py:598
  20.3 3.1 %collective-permute-start.3 = (bf16[2048,256]{1,0:T(8,128)(2,1)S(1)}, bf16[2048,256]{1,0:T(8,128)(2,1)S(1)}, u32[]{:S(2)}, u32[]{:S(2)}) collective-permute-start(bf16[2048,256]{1,0:T(8,128)(2,1)S(1)} %slice.19), channel_id=1, source_target_pairs={{0,1},{1,0},{2,3},{3,2},{4,5},{5,4},{6,7},{7,6},{8,9},{9,8},{10,11... | collective-permute-start | bytes 3145736 | tf_op jit(solution)/shard_map/ppermute | solution.py:598
  23.6 17.6 %collective-permute-start.5 = (bf16[512,256]{1,0:T(8,128)(2,1)S(1)}, bf16[512,256]{1,0:T(8,128)(2,1)S(1)}, u32[]{:S(2)}, u32[]{:S(2)}) collective-permute-start(bf16[512,256]{1,0:T(8,128)(2,1)S(1)} %get-tuple-element.154), channel_id=1, source_target_pairs={{0,4},{4,0},{8,12},{12,8},{16,20},{20,16},{24,28},{28,24},{1,5},{5... | collective-permute-start | bytes 786440 | tf_op jit(solution)/shard_map/ppermute | solution.py:598
  25.3 16.0 %collective-permute-start.6 = (bf16[512,256]{1,0:T(8,128)(2,1)S(1)}, bf16[512,256]{1,0:T(8,128)(2,1)S(1)}, u32[]{:S(2)}, u32[]{:S(2)}) collective-permute-start(bf16[512,256]{1,0:T(8,128)(2,1)S(1)} %get-tuple-element.155), channel_id=1, source_target_pairs={{0,2},{1,3},{2,0},{3,1},{4,6},{5,7},{6,4},{7,5},{8,10},{9,11},{10,... | collective-permute-start | bytes 786440 | tf_op jit(solution)/shard_map/ppermute | solution.py:598
  26.8 14.5 %collective-permute-start.7 = (bf16[512,256]{1,0:T(8,128)(2,1)S(1)}, bf16[512,256]{1,0:T(8,128)(2,1)S(1)}, u32[]{:S(2)}, u32[]{:S(2)}) collective-permute-start(bf16[512,256]{1,0:T(8,128)(2,1)S(1)} %get-tuple-element.156), channel_id=1, source_target_pairs={{0,6},{1,7},{2,4},{3,5},{4,2},{5,3},{6,0},{7,1},{8,14},{9,15},{10,... | collective-permute-start | bytes 786440 | tf_op jit(solution)/shard_map/ppermute | solution.py:750
  41.1 3.4 %collective-permute-start.4 = (bf16[1040,256]{1,0:T(8,128)(2,1)S(1)}, bf16[1040,256]{1,0:T(8,128)(2,1)S(1)}, u32[]{:S(2)}, u32[]{:S(2)}) collective-permute-start(bf16[1040,256]{1,0:T(8,128)(2,1)S(1)} %slice.20), channel_id=1, source_target_pairs={{0,1},{1,0},{2,3},{3,2},{4,5},{5,4},{6,7},{7,6},{8,9},{9,8},{10,11... | collective-permute-start | bytes 1597448 | tf_op jit(solution)/shard_map/ppermute | solution.py:598
  41.4 5.9 %collective-permute-start.9 = (bf16[256,256]{1,0:T(8,128)(2,1)S(1)}, bf16[256,256]{1,0:T(8,128)(2,1)S(1)}, u32[]{:S(2)}, u32[]{:S(2)}) collective-permute-start(bf16[256,256]{1,0:T(8,128)(2,1)S(1)} %get-tuple-element.164), channel_id=1, source_target_pairs={{0,8},{4,12},{8,0},{12,4},{16,24},{20,28},{24,16},{28,20},{1,9},{5... | collective-permute-start | bytes 393224 | tf_op jit(solution)/shard_map/ppermute | solution.py:598
  44.7 9.2 %collective-permute-start.8 = (bf16[512,256]{1,0:T(8,128)(2,1)S(1)}, bf16[512,256]{1,0:T(8,128)(2,1)S(1)}, u32[]{:S(2)}, u32[]{:S(2)}) collective-permute-start(bf16[512,256]{1,0:T(8,128)(2,1)S(1)} %get-tuple-element.159), channel_id=1, source_target_pairs={{0,2},{1,3},{2,0},{3,1},{4,6},{5,7},{6,4},{7,5},{8,10},{9,11},{10,... | collective-permute-start | bytes 786440 | tf_op jit(solution)/shard_map/ppermute | solution.py:598
  47.4 2.8 %collective-permute-start.10 = (bf16[384,256]{1,0:T(8,128)(2,1)S(1)}, bf16[384,256]{1,0:T(8,128)(2,1)S(1)}, u32[]{:S(2)}, u32[]{:S(2)}) collective-permute-start(bf16[384,256]{1,0:T(8,128)(2,1)S(1)} %shard_map.296), channel_id=1, source_target_pairs={{0,1},{1,0},{2,3},{3,2},{4,5},{5,4},{6,7},{7,6},{8,9},{9,8},{10,11... | collective-permute-start | bytes 589832 | tf_op jit(solution)/shard_map/ppermute | solution.py:598
  47.5 9.6 %collective-permute-start.14 = (bf16[256,256]{1,0:T(8,128)(2,1)S(1)}, bf16[256,256]{1,0:T(8,128)(2,1)S(1)}, u32[]{:S(2)}, u32[]{:S(2)}) collective-permute-start(bf16[256,256]{1,0:T(8,128)(2,1)S(1)} %shard_map.294.rest_0_.refs_1_.refs_2_.refs_0_), channel_id=1, source_target_pairs={{0,16},{4,20},{8,24},{12,28},{16,0},{20,4},{24,8},{28,12},{1,17},{... | collective-permute-start | bytes 393224 | tf_op jit(solution)/shard_map/ppermute | solution.py:598
  50.3 7.6 %collective-permute-start.11 = (bf16[112,256]{1,0:T(8,128)(2,1)S(1)}, bf16[112,256]{1,0:T(8,128)(2,1)S(1)}, u32[]{:S(2)}, u32[]{:S(2)}) collective-permute-start(bf16[112,256]{1,0:T(8,128)(2,1)S(1)} %shard_map.299), channel_id=1, source_target_pairs={{0,4},{4,0},{8,12},{12,8},{16,20},{20,16},{24,28},{28,24},{1,5},{5... | collective-permute-start | bytes 172040 | tf_op jit(solution)/shard_map/ppermute | solution.py:598
  51.9 6.1 %collective-permute-start.12 = (bf16[112,256]{1,0:T(8,128)(2,1)S(1)}, bf16[112,256]{1,0:T(8,128)(2,1)S(1)}, u32[]{:S(2)}, u32[]{:S(2)}) collective-permute-start(bf16[112,256]{1,0:T(8,128)(2,1)S(1)} %shard_map.300), channel_id=1, source_target_pairs={{0,2},{1,3},{2,0},{3,1},{4,6},{5,7},{6,4},{7,5},{8,10},{9,11},{10,... | collective-permute-start | bytes 172040 | tf_op jit(solution)/shard_map/ppermute | solution.py:598
  53.4 5.1 %collective-permute-start.13 = (bf16[112,256]{1,0:T(8,128)(2,1)S(1)}, bf16[112,256]{1,0:T(8,128)(2,1)S(1)}, u32[]{:S(2)}, u32[]{:S(2)}) collective-permute-start(bf16[112,256]{1,0:T(8,128)(2,1)S(1)} %shard_map.301.refs_2_), channel_id=1, source_target_pairs={{0,6},{1,7},{2,4},{3,5},{4,2},{5,3},{6,0},{7,1},{8,14},{9,15},{10,... | collective-permute-start | bytes 172040 | tf_op jit(solution)/shard_map/ppermute | solution.py:750
  57.1 5.8 %collective-permute-start.16 = (bf16[256,256]{1,0:T(8,128)(2,1)S(1)}, bf16[256,256]{1,0:T(8,128)(2,1)S(1)}, u32[]{:S(2)}, u32[]{:S(2)}) collective-permute-start(bf16[256,256]{1,0:T(8,128)(2,1)S(1)} %shard_map.302.refs_4_.refs_0_), channel_id=1, source_target_pairs={{0,8},{4,12},{8,0},{12,4},{16,24},{20,28},{24,16},{28,20},{1,9},{5... | collective-permute-start | bytes 393224 | tf_op jit(solution)/shard_map/ppermute | solution.py:598
  58.5 8.0 %collective-permute-start.15 = (bf16[112,256]{1,0:T(8,128)(2,1)S(1)}, bf16[112,256]{1,0:T(8,128)(2,1)S(1)}, u32[]{:S(2)}, u32[]{:S(2)}) collective-permute-start(bf16[112,256]{1,0:T(8,128)(2,1)S(1)} %shard_map.303.refs_2_.refs_0_), channel_id=1, source_target_pairs={{0,8},{4,12},{8,0},{12,4},{16,24},{20,28},{24,16},{28,20},{1,9},{5... | collective-permute-start | bytes 172040 | tf_op jit(solution)/shard_map/ppermute | solution.py:598
  62.9 10.2 %collective-permute-start.23 = (bf16[512,256]{1,0:T(8,128)(2,1)S(1)}, bf16[512,256]{1,0:T(8,128)(2,1)S(1)}, u32[]{:S(2)}, u32[]{:S(2)}) collective-permute-start(bf16[512,256]{1,0:T(8,128)(2,1)S(1)} %shard_map.304.refs_2_.refs_0_), channel_id=1, source_target_pairs={{0,6},{1,7},{2,4},{3,5},{4,2},{5,3},{6,0},{7,1},{8,14},{9,15},{10,... | collective-permute-start | bytes 786440 | tf_op jit(solution)/shard_map/ppermute | solution.py:750
  65.5 10.4 %collective-permute-start.22 = (bf16[512,256]{1,0:T(8,128)(2,1)S(1)}, bf16[512,256]{1,0:T(8,128)(2,1)S(1)}, u32[]{:S(2)}, u32[]{:S(2)}) collective-permute-start(bf16[512,256]{1,0:T(8,128)(2,1)S(1)} %shard_map.304.refs_2_.refs_0_), channel_id=1, source_target_pairs={{0,2},{1,3},{2,0},{3,1},{4,6},{5,7},{6,4},{7,5},{8,10},{9,11},{10,... | collective-permute-start | bytes 786440 | tf_op jit(solution)/shard_map/ppermute | solution.py:598
  66.0 10.0 %collective-permute-start.21 = (bf16[512,256]{1,0:T(8,128)(2,1)S(1)}, bf16[512,256]{1,0:T(8,128)(2,1)S(1)}, u32[]{:S(2)}, u32[]{:S(2)}) collective-permute-start(bf16[512,256]{1,0:T(8,128)(2,1)S(1)} %shard_map.304.refs_2_.refs_0_), channel_id=1, source_target_pairs={{0,4},{4,0},{8,12},{12,8},{16,20},{20,16},{24,28},{28,24},{1,5},{5... | collective-permute-start | bytes 786440 | tf_op jit(solution)/shard_map/ppermute | solution.py:598
  66.5 5.1 %collective-permute-start.17 = (bf16[112,256]{1,0:T(8,128)(2,1)S(1)}, bf16[112,256]{1,0:T(8,128)(2,1)S(1)}, u32[]{:S(2)}, u32[]{:S(2)}) collective-permute-start(bf16[112,256]{1,0:T(8,128)(2,1)S(1)} %shard_map.305.refs_0_), channel_id=1, source_target_pairs={{0,16},{4,20},{8,24},{12,28},{16,0},{20,4},{24,8},{28,12},{1,17},{... | collective-permute-start | bytes 172040 | tf_op jit(solution)/shard_map/ppermute | solution.py:598
  76.1 3.6 %collective-permute-start.24 = (bf16[2048,256]{1,0:T(8,128)(2,1)S(1)}, bf16[2048,256]{1,0:T(8,128)(2,1)S(1)}, u32[]{:S(2)}, u32[]{:S(2)}) collective-permute-start(bf16[2048,256]{1,0:T(8,128)(2,1)S(1)} %shard_map.307.mine), channel_id=1, source_target_pairs={{0,1},{1,0},{2,3},{3,2},{4,5},{5,4},{6,7},{7,6},{8,9},{9,8},{10,11... | collective-permute-start | bytes 3145736 | tf_op jit(solution)/shard_map/ppermute | solution.py:598
  76.2 5.8 %collective-permute-start.20 = (bf16[96,256]{1,0:T(8,128)(2,1)S(1)}, bf16[96,256]{1,0:T(8,128)(2,1)S(1)}, u32[]{:S(2)}, u32[]{:S(2)}) collective-permute-start(bf16[96,256]{1,0:T(8,128)(2,1)S(1)} %slice.25.refs_0_), channel_id=1, source_target_pairs={{0,6},{1,7},{2,4},{3,5},{4,2},{5,3},{6,0},{7,1},{8,14},{9,15},{10,... | collective-permute-start | bytes 147464 | tf_op jit(solution)/shard_map/ppermute | solution.py:750
  77.9 4.4 %collective-permute-start.19 = (bf16[96,256]{1,0:T(8,128)(2,1)S(1)}, bf16[96,256]{1,0:T(8,128)(2,1)S(1)}, u32[]{:S(2)}, u32[]{:S(2)}) collective-permute-start(bf16[96,256]{1,0:T(8,128)(2,1)S(1)} %slice.25.refs_0_), channel_id=1, source_target_pairs={{0,2},{1,3},{2,0},{3,1},{4,6},{5,7},{6,4},{7,5},{8,10},{9,11},{10,... | collective-permute-start | bytes 147464 | tf_op jit(solution)/shard_map/ppermute | solution.py:598
  79.2 4.1 %collective-permute-start.18 = (bf16[96,256]{1,0:T(8,128)(2,1)S(1)}, bf16[96,256]{1,0:T(8,128)(2,1)S(1)}, u32[]{:S(2)}, u32[]{:S(2)}) collective-permute-start(bf16[96,256]{1,0:T(8,128)(2,1)S(1)} %slice.25.refs_0_), channel_id=1, source_target_pairs={{0,4},{4,0},{8,12},{12,8},{16,20},{20,16},{24,28},{28,24},{1,5},{5... | collective-permute-start | bytes 147464 | tf_op jit(solution)/shard_map/ppermute | solution.py:598
  (19 other events, 28.3 us)

commit v5 on v4

--- a/solution.py
+++ b/solution.py
@@ -90,12 +90,6 @@
     for head in range(HEADS):
         pieces += [weight[head * HEAD_DIM : (head + 1) * HEAD_DIM], gap]
     return jnp.concatenate(pieces, axis=0)
-
-
-def narrow(wide):
-    return jnp.concatenate(
-        [wide[:, h * LANES : h * LANES + HEAD_DIM] for h in range(HEADS)], axis=1
-    )
 
 
 def narrow_rows(wide):
@@ -429,6 +423,12 @@
     rows_h = slice(h * HEAD_DIM, (h + 1) * HEAD_DIM)
     q_h = q_back[:, lanes]
     g_h = grad_att[:, lanes]
+    lane = lax.broadcasted_iota(jnp.int32, (1, LANES), 1)
+    q_half = jnp.where(lane < HEAD_DIM, high(q_h), 0.0)
+    g_half = jnp.where(lane < HEAD_DIM, high(g_h), 0.0)
+    if h % 2:
+        q_half, g_half = pltpu.roll(q_half, HEAD_DIM, 1), pltpu.roll(g_half, HEAD_DIM, 1)
+    q_low, g_low = low(q_half), low(g_half)
     acc = high(dself[h : h + 1, :]) * high(kt_all[rows_h, :own_rows])
     first = 0
     for k_part in (k_a, k_y, k_f):
@@ -436,11 +436,11 @@
         at = slice(first, first + count)
         p = jnp.exp(dot_nt(k_part[:, lanes], q_h))
         ds = low(p * dot_nt(v_all[at, lanes], g_h))
-        dv = dot(low(p), g_h)
-        dk = dot(ds, q_h)
+        dv = dot(low(p), g_low)
+        dk = dot(ds, q_low)
         if first == 0:
-            dk_self = dot_tn(dself[...], spread) * high(q_h)
-            dv_self = dot_tn(pself[...], spread) * high(g_h)
+            dk_self = dot_tn(dself[...], spread) * q_half
+            dv_self = dot_tn(pself[...], spread) * g_half
             dk_out[:own_rows, :] = low(dk[:own_rows] + dk_self)
             dv_out[:own_rows, :] = low(dv[:own_rows] + dv_self)
             dk_out[own_rows:count, :] = low(dk[own_rows:])
@@ -456,7 +456,7 @@
 def rows_kernel(
     own_rows,
     dk0, dk1, dk2, dk3, dv0, dv1, dv2, dv3, dq0, dq1, dq2, dq3, normed_a, normed_y, normed_f, counted, d_modules, crossed,
-    w_cross, w_mix, own_member, counts, gain_one, wq, wk_pad, wv_pad, vectors,
+    w_cross, w_mix, own_member, counts, gain_one, wq, wk, wv, vectors,
     *rest,
 ):
     out, dq_out, dn = rest[-3:]
@@ -473,19 +473,14 @@
     dq = jnp.concatenate([high(part[...]) for part in (dq0, dq1, dq2, dq3)], axis=0)
     dq_rows = low(dq.T)
     dq_out[...] = dq_rows
-    dk_pairs = [jnp.concatenate([dk0[...], dk1[...]], axis=1), jnp.concatenate([dk2[...], dk3[...]], axis=1)]
-    dv_pairs = [jnp.concatenate([dv0[...], dv1[...]], axis=1), jnp.concatenate([dv2[...], dv3[...]], axis=1)]
+    dk = jnp.concatenate([dk0[...] + dk1[...], dk2[...] + dk3[...]], axis=1)
+    dv = jnp.concatenate([dv0[...] + dv1[...], dv2[...] + dv3[...]], axis=1)
     up = low(seg_grad)
     down = low(seg_grad - high(up))
     for c in range(2):
         at = slice(c * half_keys, (c + 1) * half_keys)
         mixing = dot_tn(counted[:, at], up) + dot_tn(counted[:, at], down)
-        dn[at, :] = mixing + (
-            dot_nt(dk_pairs[0][at, :], wk_pad[:, :256])
-            + dot_nt(dk_pairs[1][at, :], wk_pad[:, 256:])
-            + dot_nt(dv_pairs[0][at, :], wv_pad[:, :256])
-            + dot_nt(dv_pairs[1][at, :], wv_pad[:, 256:])
-        )
+        dn[at, :] = mixing + (dot_nt(dk[at, :], wk[...]) + dot_nt(dv[at, :], wv[...]))
     dn[:own_rows, :] = dn[:own_rows, :] + (dot_nt(dq_rows, wq[...]) + dn_own)
     gain_grad = jnp.sum(dn[:half_keys, :] * high(normed_a[...]), axis=0, keepdims=True)
     for i, normed in enumerate((normed_y, normed_f)):
@@ -512,18 +507,10 @@
     flips = ((normed_ta, 0), (normed_ty, 2), (normed_tf, 3))
 
     def key_grad(parts):
-        pairs = [jnp.concatenate([parts[i][...], parts[i + 1][...]], axis=1) for i in (0, 2)]
-        return narrow(
-            jnp.concatenate(
-                [
-                    sum(
-                        dot(flip[...], pair[at * own_rows : at * own_rows + flip.shape[1]])
-                        for flip, at in flips
-                    )
-                    for pair in pairs
-                ],
-                axis=1,
-            )
+        whole = [parts[i][...] + parts[i + 1][...] for i in (0, 2)]
+        whole = jnp.concatenate(whole, axis=1)
+        return sum(
+            dot(flip[...], whole[at * own_rows : at * own_rows + flip.shape[1]]) for flip, at in flips
         )
 
     core, y_bit, x_bit, _ = bits_of(spot)
@@ -774,7 +761,7 @@
     dk3, dv3, dq3 = head(3, dq2, cost=2)
     args = [
         dk0, dk1, dk2, dk3, dv0, dv1, dv2, dv3, dq0, dq1, dq2, dq3, normed_a, normed_y, normed_f, counted,
-        d_modules, crossed, w_cross, w_mix, own_member, counts, gain_row, w_query, wk_pad, wv_pad, vectors,
+        d_modules, crossed, w_cross, w_mix, own_member, counts, gain_row, w_query, w_key, w_value, vectors,
     ]
     shared, dq_rows = call(
         functools.partial(rows_kernel, own),

time: 86.1 us -> 85.6 us (level)
  Pallas kernels: 38.9 us -> 37.8 us
  transfers between devices with their start and end apart: 26 -> 26, of which waited for: 11 -> 11; matrix products, arithmetic and copies ran while one was open for 0% -> 0% of each run, Pallas kernels for 35% -> 34%
where the time goes in v5:
time: 85.6 us; the launch traced here: 85.5 us
  Pallas kernels  37.8 us (44%)
  starting transfers between devices  29.6 us (35%)
  waiting for transfers between devices  16 us (19%)
  between operations  1.07 us (1%)
  local copies, waits for them, and re-layouts  0.94 us (1%)
    ppermute x22, starting transfers between devices, swap(): return lax.ppermute(value, axis, [(i, i ^ step) for i in range(count)])  24.4 us
    ppermute x22, waiting for transfers between devices, swap(): return lax.ppermute(value, axis, [(i, i ^ step) for i in range(count)])  14.1 us
    pallas_call x4, Pallas kernels, head(): call(functools.partial(head_kernel, own, index), [((rows, LANES), BF), ((...  11.3 us
    pallas_call x1, Pallas kernels, shards(): call(functools.partial(forward_kernel, own), [((16 * D, D), BF), ((own, D...  7.02 us
    pallas_call x1, Pallas kernels, shards(): call(functools.partial(first_kernel, own), [((D, WIDE), BF), ((D, WIDE),...  5.75 us
    ppermute x4, starting transfers between devices, by_both(): return lax.ppermute(value, ('batch', 'module'), pairs)  5.14 us
    pallas_call x1, Pallas kernels, shards(): call(functools.partial(side_kernel, own), [((rows, WIDE), BF), ((D, rows)...  2.66 us
    pallas_call x1, Pallas kernels, shards(): call(unpack_kernel, [wide, wide, wide, ((4 * D, D), F32), ((D, FF), F32),...  2.22 us
  transfers between devices with their start and end apart: 26, of which 11 were waited for; matrix products, arithmetic and copies ran while one was open for 0% of the time, Pallas kernels for 34%

profile of v5, /device:TPU:0, one launch (start us, length us, event | category | flops | bytes accessed | tf_op | source)
XLA Modules:
  0.0 85.5 jit_solution(1237316474504940611)
XLA Ops:
  1.2 2.6 %collective-permute-start = (bf16[512,256]{1,0:T(8,128)(2,1)}, bf16[512,256]{1,0:T(8,128)(2,1)S(1)}, u32[]{:S(2)}, u32[]{:S(2)}) collective-permute-start(bf16[512,256]{1,0:T(8,128)(2,1)} %tokens.5), channel_id=1, source_target_pairs={{0,2},{1,3},{2,0},{3,1},{4,6},{5,7},{6,4},{7,5},{8,10},{9,11},{10,... | collective-permute-start | bytes 786440 | tf_op jit(solution)/shard_map/ppermute | solution.py:585
  5.3 5.7 %shard_map.281 = (bf16[256,512]{1,0:T(8,128)(2,1)}, bf16[256,512]{1,0:T(8,128)(2,1)S(1)}, bf16[256,512]{1,0:T(8,128)(2,1)S(1)}, bf16[512,256]{1,0:T(8,128)(2,1)S...) custom-call(s32[8,128]{1,0:T(8,128)S(1)} %shard_map.280.spot, ...), custom_call_target="tpu_custom_call" | custom-call | flops 5000000000 | tf_op jit(solution)/shard_map/pallas_call | solution.py:663
  11.3 1.8 %shard_map.282 = (bf16[512,256]{1,0:T(8,128)(2,1)S(1)}, bf16[256,512]{1,0:T(8,128)(2,1)S(1)}, bf16[512,512]{1,0:T(8,128)(2,1)S(1)}, bf16[320,512]{1,0:T(8,128)(2,1)S(1)}, f32[320,512]{1,0:T(8,128)S(1)}) custom-call(bf16[512,256]{1,0:T(8,128)(2,1)S(1)} %collective-permute-done.y_rows, f32[1,256]{1,0:T(1,128)S(1)} %bitcast.16, ...), custom_call_target="tpu_custom_call" | custom-call | flops 2000000000 | tf_op jit(solution)/shard_map/pallas_call | solution.py:678
  13.2 7.0 %shard_map.283 = (bf16[4096,256]{1,0:T(8,128)(2,1)S(1)}, f32[512,256]{1,0:T(8,128)S(1)}, f32[16,256]{1,0:T(8,128)S(1)}, bf16[512,256]{1,0:T(8,128)(2,1)S(1)}, bf...) custom-call(s32[8,128]{1,0:T(8,128)S(1)} %shard_map.280.spot, ...), custom_call_target="tpu_custom_call" | custom-call | flops 8000000000 | tf_op jit(solution)/shard_map/pallas_call | solution.py:686
  20.7 2.7 %shard_map.284 = (bf16[2048,512]{1,0:T(8,128)(2,1)S(1)}, bf16[256,2048]{1,0:T(8,128)(2,1)S(1)}, bf16[512,512]{1,0:T(8,128)(2,1)S(1)}, bf16[512,512]{1,0:T(8,128)...) custom-call(bf16[512,1024]{1,0:T(8,128)(2,1)S(1)} %get-tuple-element.119.d_modules, ...), custom_call_target="tpu_custom_call" | custom-call | flops 3000000000 | tf_op jit(solution)/shard_map/pallas_call | solution.py:704
  23.6 1.6 %collective-permute-start.5 = (bf16[512,256]{1,0:T(8,128)(2,1)S(1)}, bf16[512,256]{1,0:T(8,128)(2,1)S(1)}, u32[]{:S(2)}, u32[]{:S(2)}) collective-permute-start(bf16[512,256]{1,0:T(8,128)(2,1)S(1)} %get-tuple-element.154), channel_id=1, source_target_pairs={{0,4},{4,0},{8,12},{12,8},{16,20},{20,16},{24,28},{28,24},{1,5},{5... | collective-permute-start | bytes 786440 | tf_op jit(solution)/shard_map/ppermute | solution.py:585
  27.2 2.8 %shard_map.286 = (bf16[2048,128]{1,0:T(8,128)(2,1)S(1)}, bf16[2048,128]{1,0:T(8,128)(2,1)S(1)}, bf16[64,512]{1,0:T(8,128)(2,1)S(1)}) custom-call(bf16[512,512]{1,0:T(8,128)(2,1)S(1)} %get-tuple-element.128.q_back, bf16[1024,512]{1,0:T(8,128)(2,1)S(1)} %get-tuple-element.112.k_a, bf16[512,512]{1,0:T(8,128)(2,1)S(1)} %get-tuple-element.113.k_y, ...), custom_call_target="tpu_custom_call" | custom-call | flops 2000000000 | tf_op jit(solution)/shard_map/pallas_call | solution.py:717
  29.9 2.8 %shard_map.287 = (bf16[2048,128]{1,0:T(8,128)(2,1)S(1)}, bf16[2048,128]{1,0:T(8,128)(2,1)S(1)}, bf16[64,512]{1,0:T(8,128)(2,1)S(1)}) custom-call(bf16[512,512]{1,0:T(8,128)(2,1)S(1)} %get-tuple-element.128.q_back, bf16[1024,512]{1,0:T(8,128)(2,1)S(1)} %get-tuple-element.112.k_a, bf16[512,512]{1,0:T(8,128)(2,1)S(1)} %get-tuple-element.113.k_y, ...), custom_call_target="tpu_custom_call" | custom-call | flops 2000000000 | tf_op jit(solution)/shard_map/pallas_call | solution.py:717
  32.7 3.0 %shard_map.288 = (bf16[2048,128]{1,0:T(8,128)(2,1)S(1)}, bf16[2048,128]{1,0:T(8,128)(2,1)S(1)}, bf16[64,512]{1,0:T(8,128)(2,1)S(1)}) custom-call(bf16[512,512]{1,0:T(8,128)(2,1)S(1)} %get-tuple-element.128.q_back, bf16[1024,512]{1,0:T(8,128)(2,1)S(1)} %get-tuple-element.112.k_a, bf16[512,512]{1,0:T(8,128)(2,1)S(1)} %get-tuple-element.113.k_y, ...), custom_call_target="tpu_custom_call" | custom-call | flops 2000000000 | tf_op jit(solution)/shard_map/pallas_call | solution.py:717
  35.7 2.8 %shard_map.289 = (bf16[2048,128]{1,0:T(8,128)(2,1)S(1)}, bf16[2048,128]{1,0:T(8,128)(2,1)S(1)}, bf16[64,512]{1,0:T(8,128)(2,1)S(1)}) custom-call(bf16[512,512]{1,0:T(8,128)(2,1)S(1)} %get-tuple-element.128.q_back, bf16[1024,512]{1,0:T(8,128)(2,1)S(1)} %get-tuple-element.112.k_a, bf16[512,512]{1,0:T(8,128)(2,1)S(1)} %get-tuple-element.113.k_y, ...), custom_call_target="tpu_custom_call" | custom-call | flops 2000000000 | tf_op jit(solution)/shard_map/pallas_call | solution.py:717
  38.5 2.1 %shard_map.290 = (bf16[2080,256]{1,0:T(8,128)(2,1)S(1)}, bf16[512,256]{1,0:T(8,128)(2,1)S(1)}) custom-call(bf16[2048,128]{1,0:T(8,128)(2,1)S(1)} %get-tuple-element.137.dk0, bf16[2048,128]{1,0:T(8,128)(2,1)S(1)} %get-tuple-element.139.dk1, bf16[2048,128]{1,0:T(8,128)(2,1)S(1)} %get-tuple-element.141.dk2, bf16[2048,128]{1,0:T(8,128)(2,1)S(1)} %get-tuple-element.143.dk3, ...), custom_call_target="tpu_custom_call" | custom-call | flops 3000000000 | tf_op jit(solution)/shard_map/pallas_call | solution.py:766
  40.9 1.7 %collective-permute-start.9 = (bf16[256,256]{1,0:T(8,128)(2,1)S(1)}, bf16[256,256]{1,0:T(8,128)(2,1)S(1)}, u32[]{:S(2)}, u32[]{:S(2)}) collective-permute-start(bf16[256,256]{1,0:T(8,128)(2,1)S(1)} %get-tuple-element.164), channel_id=1, source_target_pairs={{0,8},{4,12},{8,0},{12,4},{16,24},{20,28},{24,16},{28,20},{1,9},{5... | collective-permute-start | bytes 393224 | tf_op jit(solution)/shard_map/ppermute | solution.py:585
  43.7 1.6 %collective-permute-start.8 = (bf16[512,256]{1,0:T(8,128)(2,1)S(1)}, bf16[512,256]{1,0:T(8,128)(2,1)S(1)}, u32[]{:S(2)}, u32[]{:S(2)}) collective-permute-start(bf16[512,256]{1,0:T(8,128)(2,1)S(1)} %get-tuple-element.159), channel_id=1, source_target_pairs={{0,2},{1,3},{2,0},{3,1},{4,6},{5,7},{6,4},{7,5},{8,10},{9,11},{10,... | collective-permute-start | bytes 786440 | tf_op jit(solution)/shard_map/ppermute | solution.py:585
  45.3 1.6 %collective-permute-done.9.refs_1_ = bf16[256,256]{1,0:T(8,128)(2,1)S(1)} collective-permute-done((bf16[256,256]{1,0:T(8,128)(2,1)S(1)}, bf16[256,256]{1,0:T(8,128)(2,1)S(1)}, u32[]{:S(2)}, u32[]{:S(2)}) %collective-permute-start.9) | collective-permute-done | bytes 131104 | tf_op jit(solution)/shard_map/ppermute | solution.py:585
  47.0 2.7 %collective-permute-start.14 = (bf16[256,256]{1,0:T(8,128)(2,1)S(1)}, bf16[256,256]{1,0:T(8,128)(2,1)S(1)}, u32[]{:S(2)}, u32[]{:S(2)}) collective-permute-start(bf16[256,256]{1,0:T(8,128)(2,1)S(1)} %shard_map.294.rest_0_.refs_1_.refs_2_.refs_0_), channel_id=1, source_target_pairs={{0,16},{4,20},{8,24},{12,28},{16,0},{20,4},{24,8},{28,12},{1,17},{... | collective-permute-start | bytes 393224 | tf_op jit(solution)/shard_map/ppermute | solution.py:585
  54.9 1.7 %collective-permute-done.14.refs_1_ = bf16[256,256]{1,0:T(8,128)(2,1)S(1)} collective-permute-done((bf16[256,256]{1,0:T(8,128)(2,1)S(1)}, bf16[256,256]{1,0:T(8,128)(2,1)S(1)}, u32[]{:S(2)}, u32[]{:S(2)}) %collective-permute-start.14) | collective-permute-done | bytes 131104 | tf_op jit(solution)/shard_map/ppermute | solution.py:585
  58.0 1.7 %collective-permute-start.15 = (bf16[112,256]{1,0:T(8,128)(2,1)S(1)}, bf16[112,256]{1,0:T(8,128)(2,1)S(1)}, u32[]{:S(2)}, u32[]{:S(2)}) collective-permute-start(bf16[112,256]{1,0:T(8,128)(2,1)S(1)} %shard_map.303.refs_2_.refs_0_), channel_id=1, source_target_pairs={{0,8},{4,12},{8,0},{12,4},{16,24},{20,28},{24,16},{28,20},{1,9},{5... | collective-permute-start | bytes 172040 | tf_op jit(solution)/shard_map/ppermute | solution.py:585
  59.7 2.8 %collective-permute-done.16.refs_1_ = bf16[256,256]{1,0:T(8,128)(2,1)S(1)} collective-permute-done((bf16[256,256]{1,0:T(8,128)(2,1)S(1)}, bf16[256,256]{1,0:T(8,128)(2,1)S(1)}, u32[]{:S(2)}, u32[]{:S(2)}) %collective-permute-start.16) | collective-permute-done | bytes 131104 | tf_op jit(solution)/shard_map/ppermute | solution.py:585
  62.4 2.6 %collective-permute-start.23 = (bf16[512,256]{1,0:T(8,128)(2,1)S(1)}, bf16[512,256]{1,0:T(8,128)(2,1)S(1)}, u32[]{:S(2)}, u32[]{:S(2)}) collective-permute-start(bf16[512,256]{1,0:T(8,128)(2,1)S(1)} %shard_map.304.refs_2_.refs_0_), channel_id=1, source_target_pairs={{0,6},{1,7},{2,4},{3,5},{4,2},{5,3},{6,0},{7,1},{8,14},{9,15},{10,... | collective-permute-start | bytes 786440 | tf_op jit(solution)/shard_map/ppermute | solution.py:737
  66.0 2.8 %collective-permute-start.17 = (bf16[112,256]{1,0:T(8,128)(2,1)S(1)}, bf16[112,256]{1,0:T(8,128)(2,1)S(1)}, u32[]{:S(2)}, u32[]{:S(2)}) collective-permute-start(bf16[112,256]{1,0:T(8,128)(2,1)S(1)} %shard_map.305.refs_0_), channel_id=1, source_target_pairs={{0,16},{4,20},{8,24},{12,28},{16,0},{20,4},{24,8},{28,12},{1,17},{... | collective-permute-start | bytes 172040 | tf_op jit(solution)/shard_map/ppermute | solution.py:585
  68.8 2.4 %collective-permute-done.17.refs_1_ = bf16[112,256]{1,0:T(8,128)(2,1)S(1)} collective-permute-done((bf16[112,256]{1,0:T(8,128)(2,1)S(1)}, bf16[112,256]{1,0:T(8,128)(2,1)S(1)}, u32[]{:S(2)}, u32[]{:S(2)}) %collective-permute-start.17) | collective-permute-done | bytes 57376 | tf_op jit(solution)/shard_map/ppermute | solution.py:585
  72.6 2.8 %collective-permute-done.22.refs_2_ = bf16[512,256]{1,0:T(8,128)(2,1)S(1)} collective-permute-done((bf16[512,256]{1,0:T(8,128)(2,1)S(1)}, bf16[512,256]{1,0:T(8,128)(2,1)S(1)}, u32[]{:S(2)}, u32[]{:S(2)}) %collective-permute-start.22) | collective-permute-done | bytes 262176 | tf_op jit(solution)/shard_map/ppermute | solution.py:585
  75.7 1.7 %collective-permute-start.20 = (bf16[96,256]{1,0:T(8,128)(2,1)S(1)}, bf16[96,256]{1,0:T(8,128)(2,1)S(1)}, u32[]{:S(2)}, u32[]{:S(2)}) collective-permute-start(bf16[96,256]{1,0:T(8,128)(2,1)S(1)} %slice.25.refs_0_), channel_id=1, source_target_pairs={{0,6},{1,7},{2,4},{3,5},{4,2},{5,3},{6,0},{7,1},{8,14},{9,15},{10,... | collective-permute-start | bytes 147464 | tf_op jit(solution)/shard_map/ppermute | solution.py:737
  79.2 2.2 %shard_map.308 = (f32[256,256]{1,0:T(8,128)}, f32[256,256]{1,0:T(8,128)}, f32[256,256]{1,0:T(8,128)}, f32[1024,256]{1,0:T(8,128)}, f32[256,1024]{1,0:T(8,128)}, ...) custom-call(s32[8,128]{1,0:T(8,128)S(1)} %shard_map.280.spot, bf16[2048,256]{1,0:T(8,128)(2,1)S(1)} %shard_map.307.mine, ...), custom_call_target="tpu_custom_call" | custom-call | flops 3000000000 | tf_op jit(solution)/shard_map/pallas_call | solution.py:808
  (101 shorter events, 21.4 us)
Async XLA Ops:
  0.6 3.9 %collective-permute-start.1 = (bf16[512,256]{1,0:T(8,128)(2,1)}, bf16[512,256]{1,0:T(8,128)(2,1)S(1)}, u32[]{:S(2)}, u32[]{:S(2)}) collective-permute-start(bf16[512,256]{1,0:T(8,128)(2,1)} %tokens.5), channel_id=1, source_target_pairs={{0,1},{1,0},{2,3},{3,2},{4,5},{5,4},{6,7},{7,6},{8,9},{9,8},{10,11... | collective-permute-start | bytes 786440 | tf_op jit(solution)/shard_map/ppermute | solution.py:585
  1.2 9.9 %collective-permute-start = (bf16[512,256]{1,0:T(8,128)(2,1)}, bf16[512,256]{1,0:T(8,128)(2,1)S(1)}, u32[]{:S(2)}, u32[]{:S(2)}) collective-permute-start(bf16[512,256]{1,0:T(8,128)(2,1)} %tokens.5), channel_id=1, source_target_pairs={{0,2},{1,3},{2,0},{3,1},{4,6},{5,7},{6,4},{7,5},{8,10},{9,11},{10,... | collective-permute-start | bytes 786440 | tf_op jit(solution)/shard_map/ppermute | solution.py:585
  20.3 3.1 %collective-permute-start.3 = (bf16[2048,256]{1,0:T(8,128)(2,1)S(1)}, bf16[2048,256]{1,0:T(8,128)(2,1)S(1)}, u32[]{:S(2)}, u32[]{:S(2)}) collective-permute-start(bf16[2048,256]{1,0:T(8,128)(2,1)S(1)} %slice.19), channel_id=1, source_target_pairs={{0,1},{1,0},{2,3},{3,2},{4,5},{5,4},{6,7},{7,6},{8,9},{9,8},{10,11... | collective-permute-start | bytes 3145736 | tf_op jit(solution)/shard_map/ppermute | solution.py:585
  23.6 17.1 %collective-permute-start.5 = (bf16[512,256]{1,0:T(8,128)(2,1)S(1)}, bf16[512,256]{1,0:T(8,128)(2,1)S(1)}, u32[]{:S(2)}, u32[]{:S(2)}) collective-permute-start(bf16[512,256]{1,0:T(8,128)(2,1)S(1)} %get-tuple-element.154), channel_id=1, source_target_pairs={{0,4},{4,0},{8,12},{12,8},{16,20},{20,16},{24,28},{28,24},{1,5},{5... | collective-permute-start | bytes 786440 | tf_op jit(solution)/shard_map/ppermute | solution.py:585
  25.2 15.5 %collective-permute-start.6 = (bf16[512,256]{1,0:T(8,128)(2,1)S(1)}, bf16[512,256]{1,0:T(8,128)(2,1)S(1)}, u32[]{:S(2)}, u32[]{:S(2)}) collective-permute-start(bf16[512,256]{1,0:T(8,128)(2,1)S(1)} %get-tuple-element.155), channel_id=1, source_target_pairs={{0,2},{1,3},{2,0},{3,1},{4,6},{5,7},{6,4},{7,5},{8,10},{9,11},{10,... | collective-permute-start | bytes 786440 | tf_op jit(solution)/shard_map/ppermute | solution.py:585
  26.8 14.0 %collective-permute-start.7 = (bf16[512,256]{1,0:T(8,128)(2,1)S(1)}, bf16[512,256]{1,0:T(8,128)(2,1)S(1)}, u32[]{:S(2)}, u32[]{:S(2)}) collective-permute-start(bf16[512,256]{1,0:T(8,128)(2,1)S(1)} %get-tuple-element.156), channel_id=1, source_target_pairs={{0,6},{1,7},{2,4},{3,5},{4,2},{5,3},{6,0},{7,1},{8,14},{9,15},{10,... | collective-permute-start | bytes 786440 | tf_op jit(solution)/shard_map/ppermute | solution.py:737
  40.6 2.9 %collective-permute-start.4 = (bf16[1040,256]{1,0:T(8,128)(2,1)S(1)}, bf16[1040,256]{1,0:T(8,128)(2,1)S(1)}, u32[]{:S(2)}, u32[]{:S(2)}) collective-permute-start(bf16[1040,256]{1,0:T(8,128)(2,1)S(1)} %slice.20), channel_id=1, source_target_pairs={{0,1},{1,0},{2,3},{3,2},{4,5},{5,4},{6,7},{7,6},{8,9},{9,8},{10,11... | collective-permute-start | bytes 1597448 | tf_op jit(solution)/shard_map/ppermute | solution.py:585
  40.9 5.9 %collective-permute-start.9 = (bf16[256,256]{1,0:T(8,128)(2,1)S(1)}, bf16[256,256]{1,0:T(8,128)(2,1)S(1)}, u32[]{:S(2)}, u32[]{:S(2)}) collective-permute-start(bf16[256,256]{1,0:T(8,128)(2,1)S(1)} %get-tuple-element.164), channel_id=1, source_target_pairs={{0,8},{4,12},{8,0},{12,4},{16,24},{20,28},{24,16},{28,20},{1,9},{5... | collective-permute-start | bytes 393224 | tf_op jit(solution)/shard_map/ppermute | solution.py:585
  43.7 9.7 %collective-permute-start.8 = (bf16[512,256]{1,0:T(8,128)(2,1)S(1)}, bf16[512,256]{1,0:T(8,128)(2,1)S(1)}, u32[]{:S(2)}, u32[]{:S(2)}) collective-permute-start(bf16[512,256]{1,0:T(8,128)(2,1)S(1)} %get-tuple-element.159), channel_id=1, source_target_pairs={{0,2},{1,3},{2,0},{3,1},{4,6},{5,7},{6,4},{7,5},{8,10},{9,11},{10,... | collective-permute-start | bytes 786440 | tf_op jit(solution)/shard_map/ppermute | solution.py:585
  46.9 2.8 %collective-permute-start.10 = (bf16[384,256]{1,0:T(8,128)(2,1)S(1)}, bf16[384,256]{1,0:T(8,128)(2,1)S(1)}, u32[]{:S(2)}, u32[]{:S(2)}) collective-permute-start(bf16[384,256]{1,0:T(8,128)(2,1)S(1)} %shard_map.296), channel_id=1, source_target_pairs={{0,1},{1,0},{2,3},{3,2},{4,5},{5,4},{6,7},{7,6},{8,9},{9,8},{10,11... | collective-permute-start | bytes 589832 | tf_op jit(solution)/shard_map/ppermute | solution.py:585
  47.0 9.6 %collective-permute-start.14 = (bf16[256,256]{1,0:T(8,128)(2,1)S(1)}, bf16[256,256]{1,0:T(8,128)(2,1)S(1)}, u32[]{:S(2)}, u32[]{:S(2)}) collective-permute-start(bf16[256,256]{1,0:T(8,128)(2,1)S(1)} %shard_map.294.rest_0_.refs_1_.refs_2_.refs_0_), channel_id=1, source_target_pairs={{0,16},{4,20},{8,24},{12,28},{16,0},{20,4},{24,8},{28,12},{1,17},{... | collective-permute-start | bytes 393224 | tf_op jit(solution)/shard_map/ppermute | solution.py:585
  49.8 7.6 %collective-permute-start.11 = (bf16[112,256]{1,0:T(8,128)(2,1)S(1)}, bf16[112,256]{1,0:T(8,128)(2,1)S(1)}, u32[]{:S(2)}, u32[]{:S(2)}) collective-permute-start(bf16[112,256]{1,0:T(8,128)(2,1)S(1)} %shard_map.299), channel_id=1, source_target_pairs={{0,4},{4,0},{8,12},{12,8},{16,20},{20,16},{24,28},{28,24},{1,5},{5... | collective-permute-start | bytes 172040 | tf_op jit(solution)/shard_map/ppermute | solution.py:585
  51.4 6.1 %collective-permute-start.12 = (bf16[112,256]{1,0:T(8,128)(2,1)S(1)}, bf16[112,256]{1,0:T(8,128)(2,1)S(1)}, u32[]{:S(2)}, u32[]{:S(2)}) collective-permute-start(bf16[112,256]{1,0:T(8,128)(2,1)S(1)} %shard_map.300), channel_id=1, source_target_pairs={{0,2},{1,3},{2,0},{3,1},{4,6},{5,7},{6,4},{7,5},{8,10},{9,11},{10,... | collective-permute-start | bytes 172040 | tf_op jit(solution)/shard_map/ppermute | solution.py:585
  52.9 5.1 %collective-permute-start.13 = (bf16[112,256]{1,0:T(8,128)(2,1)S(1)}, bf16[112,256]{1,0:T(8,128)(2,1)S(1)}, u32[]{:S(2)}, u32[]{:S(2)}) collective-permute-start(bf16[112,256]{1,0:T(8,128)(2,1)S(1)} %shard_map.301.refs_2_), channel_id=1, source_target_pairs={{0,6},{1,7},{2,4},{3,5},{4,2},{5,3},{6,0},{7,1},{8,14},{9,15},{10,... | collective-permute-start | bytes 172040 | tf_op jit(solution)/shard_map/ppermute | solution.py:737
  56.6 5.8 %collective-permute-start.16 = (bf16[256,256]{1,0:T(8,128)(2,1)S(1)}, bf16[256,256]{1,0:T(8,128)(2,1)S(1)}, u32[]{:S(2)}, u32[]{:S(2)}) collective-permute-start(bf16[256,256]{1,0:T(8,128)(2,1)S(1)} %shard_map.302.refs_4_.refs_0_), channel_id=1, source_target_pairs={{0,8},{4,12},{8,0},{12,4},{16,24},{20,28},{24,16},{28,20},{1,9},{5... | collective-permute-start | bytes 393224 | tf_op jit(solution)/shard_map/ppermute | solution.py:585
  58.0 8.0 %collective-permute-start.15 = (bf16[112,256]{1,0:T(8,128)(2,1)S(1)}, bf16[112,256]{1,0:T(8,128)(2,1)S(1)}, u32[]{:S(2)}, u32[]{:S(2)}) collective-permute-start(bf16[112,256]{1,0:T(8,128)(2,1)S(1)} %shard_map.303.refs_2_.refs_0_), channel_id=1, source_target_pairs={{0,8},{4,12},{8,0},{12,4},{16,24},{20,28},{24,16},{28,20},{1,9},{5... | collective-permute-start | bytes 172040 | tf_op jit(solution)/shard_map/ppermute | solution.py:585
  62.4 10.2 %collective-permute-start.23 = (bf16[512,256]{1,0:T(8,128)(2,1)S(1)}, bf16[512,256]{1,0:T(8,128)(2,1)S(1)}, u32[]{:S(2)}, u32[]{:S(2)}) collective-permute-start(bf16[512,256]{1,0:T(8,128)(2,1)S(1)} %shard_map.304.refs_2_.refs_0_), channel_id=1, source_target_pairs={{0,6},{1,7},{2,4},{3,5},{4,2},{5,3},{6,0},{7,1},{8,14},{9,15},{10,... | collective-permute-start | bytes 786440 | tf_op jit(solution)/shard_map/ppermute | solution.py:737
  65.0 10.4 %collective-permute-start.22 = (bf16[512,256]{1,0:T(8,128)(2,1)S(1)}, bf16[512,256]{1,0:T(8,128)(2,1)S(1)}, u32[]{:S(2)}, u32[]{:S(2)}) collective-permute-start(bf16[512,256]{1,0:T(8,128)(2,1)S(1)} %shard_map.304.refs_2_.refs_0_), channel_id=1, source_target_pairs={{0,2},{1,3},{2,0},{3,1},{4,6},{5,7},{6,4},{7,5},{8,10},{9,11},{10,... | collective-permute-start | bytes 786440 | tf_op jit(solution)/shard_map/ppermute | solution.py:585
  65.5 10.0 %collective-permute-start.21 = (bf16[512,256]{1,0:T(8,128)(2,1)S(1)}, bf16[512,256]{1,0:T(8,128)(2,1)S(1)}, u32[]{:S(2)}, u32[]{:S(2)}) collective-permute-start(bf16[512,256]{1,0:T(8,128)(2,1)S(1)} %shard_map.304.refs_2_.refs_0_), channel_id=1, source_target_pairs={{0,4},{4,0},{8,12},{12,8},{16,20},{20,16},{24,28},{28,24},{1,5},{5... | collective-permute-start | bytes 786440 | tf_op jit(solution)/shard_map/ppermute | solution.py:585
  66.0 5.1 %collective-permute-start.17 = (bf16[112,256]{1,0:T(8,128)(2,1)S(1)}, bf16[112,256]{1,0:T(8,128)(2,1)S(1)}, u32[]{:S(2)}, u32[]{:S(2)}) collective-permute-start(bf16[112,256]{1,0:T(8,128)(2,1)S(1)} %shard_map.305.refs_0_), channel_id=1, source_target_pairs={{0,16},{4,20},{8,24},{12,28},{16,0},{20,4},{24,8},{28,12},{1,17},{... | collective-permute-start | bytes 172040 | tf_op jit(solution)/shard_map/ppermute | solution.py:585
  75.6 3.6 %collective-permute-start.24 = (bf16[2048,256]{1,0:T(8,128)(2,1)S(1)}, bf16[2048,256]{1,0:T(8,128)(2,1)S(1)}, u32[]{:S(2)}, u32[]{:S(2)}) collective-permute-start(bf16[2048,256]{1,0:T(8,128)(2,1)S(1)} %shard_map.307.mine), channel_id=1, source_target_pairs={{0,1},{1,0},{2,3},{3,2},{4,5},{5,4},{6,7},{7,6},{8,9},{9,8},{10,11... | collective-permute-start | bytes 3145736 | tf_op jit(solution)/shard_map/ppermute | solution.py:585
  75.7 5.8 %collective-permute-start.20 = (bf16[96,256]{1,0:T(8,128)(2,1)S(1)}, bf16[96,256]{1,0:T(8,128)(2,1)S(1)}, u32[]{:S(2)}, u32[]{:S(2)}) collective-permute-start(bf16[96,256]{1,0:T(8,128)(2,1)S(1)} %slice.25.refs_0_), channel_id=1, source_target_pairs={{0,6},{1,7},{2,4},{3,5},{4,2},{5,3},{6,0},{7,1},{8,14},{9,15},{10,... | collective-permute-start | bytes 147464 | tf_op jit(solution)/shard_map/ppermute | solution.py:737
  77.4 4.4 %collective-permute-start.19 = (bf16[96,256]{1,0:T(8,128)(2,1)S(1)}, bf16[96,256]{1,0:T(8,128)(2,1)S(1)}, u32[]{:S(2)}, u32[]{:S(2)}) collective-permute-start(bf16[96,256]{1,0:T(8,128)(2,1)S(1)} %slice.25.refs_0_), channel_id=1, source_target_pairs={{0,2},{1,3},{2,0},{3,1},{4,6},{5,7},{6,4},{7,5},{8,10},{9,11},{10,... | collective-permute-start | bytes 147464 | tf_op jit(solution)/shard_map/ppermute | solution.py:585
  78.7 4.1 %collective-permute-start.18 = (bf16[96,256]{1,0:T(8,128)(2,1)S(1)}, bf16[96,256]{1,0:T(8,128)(2,1)S(1)}, u32[]{:S(2)}, u32[]{:S(2)}) collective-permute-start(bf16[96,256]{1,0:T(8,128)(2,1)S(1)} %slice.25.refs_0_), channel_id=1, source_target_pairs={{0,4},{4,0},{8,12},{12,8},{16,20},{20,16},{24,28},{28,24},{1,5},{5... | collective-permute-start | bytes 147464 | tf_op jit(solution)/shard_map/ppermute | solution.py:585
  (19 other events, 28.4 us)

commit v6 on v5

--- a/solution.py
+++ b/solution.py
@@ -190,14 +190,11 @@
     upper = low(rows16)
     rest = rows16 - high(upper)
     middle = low(rest)
-    parts = (upper, middle, low(rest - high(middle)))
-    rows = lax.broadcasted_iota(jnp.int32, (16, WIDE), 0)
-    lanes = lax.broadcasted_iota(jnp.int32, (16, WIDE), 1)
-    total = 0.0
-    for i, piece in enumerate(parts):
-        picked = ((lanes >> 7) == rows) & ((lanes & (LANES - 1)) == first + i)
-        total = total + dot_tn(piece, low(jnp.where(picked, 1.0, 0.0)))
-    return low(total)
+    parts = jnp.concatenate([upper, middle, low(rest - high(middle))], axis=0)
+    rows = lax.broadcasted_iota(jnp.int32, (48, WIDE), 0)
+    lanes = lax.broadcasted_iota(jnp.int32, (48, WIDE), 1)
+    picked = ((lanes >> 7) == (rows & 15)) & ((lanes & (LANES - 1)) == first + (rows >> 4))
+    return low(dot_tn(parts, low(jnp.where(picked, 1.0, 0.0))))
 
 
 def lane_codes(rows_code):
@@ -476,10 +473,10 @@
     dk = jnp.concatenate([dk0[...] + dk1[...], dk2[...] + dk3[...]], axis=1)
     dv = jnp.concatenate([dv0[...] + dv1[...], dv2[...] + dv3[...]], axis=1)
     up = low(seg_grad)
-    down = low(seg_grad - high(up))
+    both = jnp.concatenate([up, low(seg_grad - high(up))], axis=0)
     for c in range(2):
         at = slice(c * half_keys, (c + 1) * half_keys)
-        mixing = dot_tn(counted[:, at], up) + dot_tn(counted[:, at], down)
+        mixing = dot_tn(jnp.concatenate([counted[:, at], counted[:, at]], axis=0), both)
         dn[at, :] = mixing + (dot_nt(dk[at, :], wk[...]) + dot_nt(dv[at, :], wv[...]))
     dn[:own_rows, :] = dn[:own_rows, :] + (dot_nt(dq_rows, wq[...]) + dn_own)
     gain_grad = jnp.sum(dn[:half_keys, :] * high(normed_a[...]), axis=0, keepdims=True)

time: 85.6 us -> 85 us (level)
  transfers between devices with their start and end apart: 26 -> 26, of which waited for: 11 -> 12; matrix products, arithmetic and copies ran while one was open for 0% -> 0% of each run, Pallas kernels for 34% -> 34%
where the time goes in v6:
time: 85 us; the launch traced here: 84.9 us
  Pallas kernels  37.1 us (44%)
  starting transfers between devices  29.6 us (35%)
  waiting for transfers between devices  16.1 us (19%)
  between operations  1.07 us (1%)
  local copies, waits for them, and re-layouts  0.94 us (1%)
    ppermute x22, starting transfers between devices, swap(): return lax.ppermute(value, axis, [(i, i ^ step) for i in range(count)])  24.4 us
    ppermute x22, waiting for transfers between devices, swap(): return lax.ppermute(value, axis, [(i, i ^ step) for i in range(count)])  14.2 us
    pallas_call x4, Pallas kernels, head(): call(functools.partial(head_kernel, own, index), [((rows, LANES), BF), ((...  11.3 us
    pallas_call x1, Pallas kernels, shards(): call(functools.partial(forward_kernel, own), [((16 * D, D), BF), ((own, D...  7.02 us
    pallas_call x1, Pallas kernels, shards(): call(functools.partial(first_kernel, own), [((D, WIDE), BF), ((D, WIDE),...  5.75 us
    ppermute x4, starting transfers between devices, by_both(): return lax.ppermute(value, ('batch', 'module'), pairs)  5.14 us
    pallas_call x1, Pallas kernels, shards(): call(unpack_kernel, [wide, wide, wide, ((4 * D, D), F32), ((D, FF), F32),...  2.22 us
    pallas_call x1, Pallas kernels, shards(): call(functools.partial(side_kernel, own), [((rows, WIDE), BF), ((D, rows)...  2.16 us
  transfers between devices with their start and end apart: 26, of which 12 were waited for; matrix products, arithmetic and copies ran while one was open for 0% of the time, Pallas kernels for 34%

profile of v6, /device:TPU:0, one launch (start us, length us, event | category | flops | bytes accessed | tf_op | source)
XLA Modules:
  0.0 84.9 jit_solution(4322662499705834928)
XLA Ops:
  1.2 2.6 %collective-permute-start = (bf16[512,256]{1,0:T(8,128)(2,1)}, bf16[512,256]{1,0:T(8,128)(2,1)S(1)}, u32[]{:S(2)}, u32[]{:S(2)}) collective-permute-start(bf16[512,256]{1,0:T(8,128)(2,1)} %tokens.5), channel_id=1, source_target_pairs={{0,2},{1,3},{2,0},{3,1},{4,6},{5,7},{6,4},{7,5},{8,10},{9,11},{10,... | collective-permute-start | bytes 786440 | tf_op jit(solution)/shard_map/ppermute | solution.py:582
  5.3 5.7 %shard_map.281 = (bf16[256,512]{1,0:T(8,128)(2,1)}, bf16[256,512]{1,0:T(8,128)(2,1)S(1)}, bf16[256,512]{1,0:T(8,128)(2,1)S(1)}, bf16[512,256]{1,0:T(8,128)(2,1)S...) custom-call(s32[8,128]{1,0:T(8,128)S(1)} %shard_map.280.spot, ...), custom_call_target="tpu_custom_call" | custom-call | flops 5000000000 | tf_op jit(solution)/shard_map/pallas_call | solution.py:660
  11.3 1.8 %shard_map.282 = (bf16[512,256]{1,0:T(8,128)(2,1)S(1)}, bf16[256,512]{1,0:T(8,128)(2,1)S(1)}, bf16[512,512]{1,0:T(8,128)(2,1)S(1)}, bf16[320,512]{1,0:T(8,128)(2,1)S(1)}, f32[320,512]{1,0:T(8,128)S(1)}) custom-call(bf16[512,256]{1,0:T(8,128)(2,1)S(1)} %collective-permute-done.y_rows, f32[1,256]{1,0:T(1,128)S(1)} %bitcast.16, ...), custom_call_target="tpu_custom_call" | custom-call | flops 2000000000 | tf_op jit(solution)/shard_map/pallas_call | solution.py:675
  13.2 7.0 %shard_map.283 = (bf16[4096,256]{1,0:T(8,128)(2,1)S(1)}, f32[512,256]{1,0:T(8,128)S(1)}, f32[16,256]{1,0:T(8,128)S(1)}, bf16[512,256]{1,0:T(8,128)(2,1)S(1)}, bf...) custom-call(s32[8,128]{1,0:T(8,128)S(1)} %shard_map.280.spot, ...), custom_call_target="tpu_custom_call" | custom-call | flops 8000000000 | tf_op jit(solution)/shard_map/pallas_call | solution.py:683
  20.7 2.2 %shard_map.284 = (bf16[2048,512]{1,0:T(8,128)(2,1)S(1)}, bf16[256,2048]{1,0:T(8,128)(2,1)S(1)}, bf16[512,512]{1,0:T(8,128)(2,1)S(1)}, bf16[512,512]{1,0:T(8,128)...) custom-call(bf16[512,1024]{1,0:T(8,128)(2,1)S(1)} %get-tuple-element.119.d_modules, ...), custom_call_target="tpu_custom_call" | custom-call | flops 3000000000 | tf_op jit(solution)/shard_map/pallas_call | solution.py:701
  23.2 1.6 %collective-permute-start.5 = (bf16[512,256]{1,0:T(8,128)(2,1)S(1)}, bf16[512,256]{1,0:T(8,128)(2,1)S(1)}, u32[]{:S(2)}, u32[]{:S(2)}) collective-permute-start(bf16[512,256]{1,0:T(8,128)(2,1)S(1)} %get-tuple-element.154), channel_id=1, source_target_pairs={{0,4},{4,0},{8,12},{12,8},{16,20},{20,16},{24,28},{28,24},{1,5},{5... | collective-permute-start | bytes 786440 | tf_op jit(solution)/shard_map/ppermute | solution.py:582
  26.8 2.8 %shard_map.286 = (bf16[2048,128]{1,0:T(8,128)(2,1)S(1)}, bf16[2048,128]{1,0:T(8,128)(2,1)S(1)}, bf16[64,512]{1,0:T(8,128)(2,1)S(1)}) custom-call(bf16[512,512]{1,0:T(8,128)(2,1)S(1)} %get-tuple-element.128.q_back, bf16[1024,512]{1,0:T(8,128)(2,1)S(1)} %get-tuple-element.112.k_a, bf16[512,512]{1,0:T(8,128)(2,1)S(1)} %get-tuple-element.113.k_y, ...), custom_call_target="tpu_custom_call" | custom-call | flops 2000000000 | tf_op jit(solution)/shard_map/pallas_call | solution.py:714
  29.6 2.8 %shard_map.287 = (bf16[2048,128]{1,0:T(8,128)(2,1)S(1)}, bf16[2048,128]{1,0:T(8,128)(2,1)S(1)}, bf16[64,512]{1,0:T(8,128)(2,1)S(1)}) custom-call(bf16[512,512]{1,0:T(8,128)(2,1)S(1)} %get-tuple-element.128.q_back, bf16[1024,512]{1,0:T(8,128)(2,1)S(1)} %get-tuple-element.112.k_a, bf16[512,512]{1,0:T(8,128)(2,1)S(1)} %get-tuple-element.113.k_y, ...), custom_call_target="tpu_custom_call" | custom-call | flops 2000000000 | tf_op jit(solution)/shard_map/pallas_call | solution.py:714
  32.3 3.0 %shard_map.288 = (bf16[2048,128]{1,0:T(8,128)(2,1)S(1)}, bf16[2048,128]{1,0:T(8,128)(2,1)S(1)}, bf16[64,512]{1,0:T(8,128)(2,1)S(1)}) custom-call(bf16[512,512]{1,0:T(8,128)(2,1)S(1)} %get-tuple-element.128.q_back, bf16[1024,512]{1,0:T(8,128)(2,1)S(1)} %get-tuple-element.112.k_a, bf16[512,512]{1,0:T(8,128)(2,1)S(1)} %get-tuple-element.113.k_y, ...), custom_call_target="tpu_custom_call" | custom-call | flops 2000000000 | tf_op jit(solution)/shard_map/pallas_call | solution.py:714
  35.4 2.8 %shard_map.289 = (bf16[2048,128]{1,0:T(8,128)(2,1)S(1)}, bf16[2048,128]{1,0:T(8,128)(2,1)S(1)}, bf16[64,512]{1,0:T(8,128)(2,1)S(1)}) custom-call(bf16[512,512]{1,0:T(8,128)(2,1)S(1)} %get-tuple-element.128.q_back, bf16[1024,512]{1,0:T(8,128)(2,1)S(1)} %get-tuple-element.112.k_a, bf16[512,512]{1,0:T(8,128)(2,1)S(1)} %get-tuple-element.113.k_y, ...), custom_call_target="tpu_custom_call" | custom-call | flops 2000000000 | tf_op jit(solution)/shard_map/pallas_call | solution.py:714
  38.1 1.9 %shard_map.290 = (bf16[2080,256]{1,0:T(8,128)(2,1)S(1)}, bf16[512,256]{1,0:T(8,128)(2,1)S(1)}) custom-call(bf16[2048,128]{1,0:T(8,128)(2,1)S(1)} %get-tuple-element.137.dk0, bf16[2048,128]{1,0:T(8,128)(2,1)S(1)} %get-tuple-element.139.dk1, bf16[2048,128]{1,0:T(8,128)(2,1)S(1)} %get-tuple-element.141.dk2, bf16[2048,128]{1,0:T(8,128)(2,1)S(1)} %get-tuple-element.143.dk3, ...), custom_call_target="tpu_custom_call" | custom-call | flops 3000000000 | tf_op jit(solution)/shard_map/pallas_call | solution.py:763
  40.3 1.7 %collective-permute-start.9 = (bf16[256,256]{1,0:T(8,128)(2,1)S(1)}, bf16[256,256]{1,0:T(8,128)(2,1)S(1)}, u32[]{:S(2)}, u32[]{:S(2)}) collective-permute-start(bf16[256,256]{1,0:T(8,128)(2,1)S(1)} %get-tuple-element.164), channel_id=1, source_target_pairs={{0,8},{4,12},{8,0},{12,4},{16,24},{20,28},{24,16},{28,20},{1,9},{5... | collective-permute-start | bytes 393224 | tf_op jit(solution)/shard_map/ppermute | solution.py:582
  43.1 1.6 %collective-permute-start.8 = (bf16[512,256]{1,0:T(8,128)(2,1)S(1)}, bf16[512,256]{1,0:T(8,128)(2,1)S(1)}, u32[]{:S(2)}, u32[]{:S(2)}) collective-permute-start(bf16[512,256]{1,0:T(8,128)(2,1)S(1)} %get-tuple-element.159), channel_id=1, source_target_pairs={{0,2},{1,3},{2,0},{3,1},{4,6},{5,7},{6,4},{7,5},{8,10},{9,11},{10,... | collective-permute-start | bytes 786440 | tf_op jit(solution)/shard_map/ppermute | solution.py:582
  44.7 1.6 %collective-permute-done.9.refs_1_ = bf16[256,256]{1,0:T(8,128)(2,1)S(1)} collective-permute-done((bf16[256,256]{1,0:T(8,128)(2,1)S(1)}, bf16[256,256]{1,0:T(8,128)(2,1)S(1)}, u32[]{:S(2)}, u32[]{:S(2)}) %collective-permute-start.9) | collective-permute-done | bytes 131104 | tf_op jit(solution)/shard_map/ppermute | solution.py:582
  46.4 2.7 %collective-permute-start.14 = (bf16[256,256]{1,0:T(8,128)(2,1)S(1)}, bf16[256,256]{1,0:T(8,128)(2,1)S(1)}, u32[]{:S(2)}, u32[]{:S(2)}) collective-permute-start(bf16[256,256]{1,0:T(8,128)(2,1)S(1)} %shard_map.294.rest_0_.refs_1_.refs_2_.refs_0_), channel_id=1, source_target_pairs={{0,16},{4,20},{8,24},{12,28},{16,0},{20,4},{24,8},{28,12},{1,17},{... | collective-permute-start | bytes 393224 | tf_op jit(solution)/shard_map/ppermute | solution.py:582
  54.4 1.7 %collective-permute-done.14.refs_1_ = bf16[256,256]{1,0:T(8,128)(2,1)S(1)} collective-permute-done((bf16[256,256]{1,0:T(8,128)(2,1)S(1)}, bf16[256,256]{1,0:T(8,128)(2,1)S(1)}, u32[]{:S(2)}, u32[]{:S(2)}) %collective-permute-start.14) | collective-permute-done | bytes 131104 | tf_op jit(solution)/shard_map/ppermute | solution.py:582
  57.4 1.7 %collective-permute-start.15 = (bf16[112,256]{1,0:T(8,128)(2,1)S(1)}, bf16[112,256]{1,0:T(8,128)(2,1)S(1)}, u32[]{:S(2)}, u32[]{:S(2)}) collective-permute-start(bf16[112,256]{1,0:T(8,128)(2,1)S(1)} %shard_map.303.refs_2_.refs_0_), channel_id=1, source_target_pairs={{0,8},{4,12},{8,0},{12,4},{16,24},{20,28},{24,16},{28,20},{1,9},{5... | collective-permute-start | bytes 172040 | tf_op jit(solution)/shard_map/ppermute | solution.py:582
  59.1 2.7 %collective-permute-done.16.refs_1_ = bf16[256,256]{1,0:T(8,128)(2,1)S(1)} collective-permute-done((bf16[256,256]{1,0:T(8,128)(2,1)S(1)}, bf16[256,256]{1,0:T(8,128)(2,1)S(1)}, u32[]{:S(2)}, u32[]{:S(2)}) %collective-permute-start.16) | collective-permute-done | bytes 131104 | tf_op jit(solution)/shard_map/ppermute | solution.py:582
  61.9 2.6 %collective-permute-start.23 = (bf16[512,256]{1,0:T(8,128)(2,1)S(1)}, bf16[512,256]{1,0:T(8,128)(2,1)S(1)}, u32[]{:S(2)}, u32[]{:S(2)}) collective-permute-start(bf16[512,256]{1,0:T(8,128)(2,1)S(1)} %shard_map.304.refs_2_.refs_0_), channel_id=1, source_target_pairs={{0,6},{1,7},{2,4},{3,5},{4,2},{5,3},{6,0},{7,1},{8,14},{9,15},{10,... | collective-permute-start | bytes 786440 | tf_op jit(solution)/shard_map/ppermute | solution.py:734
  65.4 2.8 %collective-permute-start.17 = (bf16[112,256]{1,0:T(8,128)(2,1)S(1)}, bf16[112,256]{1,0:T(8,128)(2,1)S(1)}, u32[]{:S(2)}, u32[]{:S(2)}) collective-permute-start(bf16[112,256]{1,0:T(8,128)(2,1)S(1)} %shard_map.305.refs_0_), channel_id=1, source_target_pairs={{0,16},{4,20},{8,24},{12,28},{16,0},{20,4},{24,8},{28,12},{1,17},{... | collective-permute-start | bytes 172040 | tf_op jit(solution)/shard_map/ppermute | solution.py:582
  68.2 2.4 %collective-permute-done.17.refs_1_ = bf16[112,256]{1,0:T(8,128)(2,1)S(1)} collective-permute-done((bf16[112,256]{1,0:T(8,128)(2,1)S(1)}, bf16[112,256]{1,0:T(8,128)(2,1)S(1)}, u32[]{:S(2)}, u32[]{:S(2)}) %collective-permute-start.17) | collective-permute-done | bytes 57376 | tf_op jit(solution)/shard_map/ppermute | solution.py:582
  72.0 2.8 %collective-permute-done.22.refs_2_ = bf16[512,256]{1,0:T(8,128)(2,1)S(1)} collective-permute-done((bf16[512,256]{1,0:T(8,128)(2,1)S(1)}, bf16[512,256]{1,0:T(8,128)(2,1)S(1)}, u32[]{:S(2)}, u32[]{:S(2)}) %collective-permute-start.22) | collective-permute-done | bytes 262176 | tf_op jit(solution)/shard_map/ppermute | solution.py:582
  75.1 1.7 %collective-permute-start.20 = (bf16[96,256]{1,0:T(8,128)(2,1)S(1)}, bf16[96,256]{1,0:T(8,128)(2,1)S(1)}, u32[]{:S(2)}, u32[]{:S(2)}) collective-permute-start(bf16[96,256]{1,0:T(8,128)(2,1)S(1)} %slice.25.refs_0_), channel_id=1, source_target_pairs={{0,6},{1,7},{2,4},{3,5},{4,2},{5,3},{6,0},{7,1},{8,14},{9,15},{10,... | collective-permute-start | bytes 147464 | tf_op jit(solution)/shard_map/ppermute | solution.py:734
  78.7 2.2 %shard_map.308 = (f32[256,256]{1,0:T(8,128)}, f32[256,256]{1,0:T(8,128)}, f32[256,256]{1,0:T(8,128)}, f32[1024,256]{1,0:T(8,128)}, f32[256,1024]{1,0:T(8,128)}, ...) custom-call(s32[8,128]{1,0:T(8,128)S(1)} %shard_map.280.spot, bf16[2048,256]{1,0:T(8,128)(2,1)S(1)} %shard_map.307.mine, ...), custom_call_target="tpu_custom_call" | custom-call | flops 3000000000 | tf_op jit(solution)/shard_map/pallas_call | solution.py:805
  (101 shorter events, 21.6 us)
Async XLA Ops:
  0.6 3.9 %collective-permute-start.1 = (bf16[512,256]{1,0:T(8,128)(2,1)}, bf16[512,256]{1,0:T(8,128)(2,1)S(1)}, u32[]{:S(2)}, u32[]{:S(2)}) collective-permute-start(bf16[512,256]{1,0:T(8,128)(2,1)} %tokens.5), channel_id=1, source_target_pairs={{0,1},{1,0},{2,3},{3,2},{4,5},{5,4},{6,7},{7,6},{8,9},{9,8},{10,11... | collective-permute-start | bytes 786440 | tf_op jit(solution)/shard_map/ppermute | solution.py:582
  1.2 9.9 %collective-permute-start = (bf16[512,256]{1,0:T(8,128)(2,1)}, bf16[512,256]{1,0:T(8,128)(2,1)S(1)}, u32[]{:S(2)}, u32[]{:S(2)}) collective-permute-start(bf16[512,256]{1,0:T(8,128)(2,1)} %tokens.5), channel_id=1, source_target_pairs={{0,2},{1,3},{2,0},{3,1},{4,6},{5,7},{6,4},{7,5},{8,10},{9,11},{10,... | collective-permute-start | bytes 786440 | tf_op jit(solution)/shard_map/ppermute | solution.py:582
  20.3 2.7 %collective-permute-start.3 = (bf16[2048,256]{1,0:T(8,128)(2,1)S(1)}, bf16[2048,256]{1,0:T(8,128)(2,1)S(1)}, u32[]{:S(2)}, u32[]{:S(2)}) collective-permute-start(bf16[2048,256]{1,0:T(8,128)(2,1)S(1)} %slice.19), channel_id=1, source_target_pairs={{0,1},{1,0},{2,3},{3,2},{4,5},{5,4},{6,7},{7,6},{8,9},{9,8},{10,11... | collective-permute-start | bytes 3145736 | tf_op jit(solution)/shard_map/ppermute | solution.py:582
  23.2 16.9 %collective-permute-start.5 = (bf16[512,256]{1,0:T(8,128)(2,1)S(1)}, bf16[512,256]{1,0:T(8,128)(2,1)S(1)}, u32[]{:S(2)}, u32[]{:S(2)}) collective-permute-start(bf16[512,256]{1,0:T(8,128)(2,1)S(1)} %get-tuple-element.154), channel_id=1, source_target_pairs={{0,4},{4,0},{8,12},{12,8},{16,20},{20,16},{24,28},{28,24},{1,5},{5... | collective-permute-start | bytes 786440 | tf_op jit(solution)/shard_map/ppermute | solution.py:582
  24.9 15.3 %collective-permute-start.6 = (bf16[512,256]{1,0:T(8,128)(2,1)S(1)}, bf16[512,256]{1,0:T(8,128)(2,1)S(1)}, u32[]{:S(2)}, u32[]{:S(2)}) collective-permute-start(bf16[512,256]{1,0:T(8,128)(2,1)S(1)} %get-tuple-element.155), channel_id=1, source_target_pairs={{0,2},{1,3},{2,0},{3,1},{4,6},{5,7},{6,4},{7,5},{8,10},{9,11},{10,... | collective-permute-start | bytes 786440 | tf_op jit(solution)/shard_map/ppermute | solution.py:582
  26.4 13.8 %collective-permute-start.7 = (bf16[512,256]{1,0:T(8,128)(2,1)S(1)}, bf16[512,256]{1,0:T(8,128)(2,1)S(1)}, u32[]{:S(2)}, u32[]{:S(2)}) collective-permute-start(bf16[512,256]{1,0:T(8,128)(2,1)S(1)} %get-tuple-element.156), channel_id=1, source_target_pairs={{0,6},{1,7},{2,4},{3,5},{4,2},{5,3},{6,0},{7,1},{8,14},{9,15},{10,... | collective-permute-start | bytes 786440 | tf_op jit(solution)/shard_map/ppermute | solution.py:734
  40.1 2.9 %collective-permute-start.4 = (bf16[1040,256]{1,0:T(8,128)(2,1)S(1)}, bf16[1040,256]{1,0:T(8,128)(2,1)S(1)}, u32[]{:S(2)}, u32[]{:S(2)}) collective-permute-start(bf16[1040,256]{1,0:T(8,128)(2,1)S(1)} %slice.20), channel_id=1, source_target_pairs={{0,1},{1,0},{2,3},{3,2},{4,5},{5,4},{6,7},{7,6},{8,9},{9,8},{10,11... | collective-permute-start | bytes 1597448 | tf_op jit(solution)/shard_map/ppermute | solution.py:582
  40.3 5.9 %collective-permute-start.9 = (bf16[256,256]{1,0:T(8,128)(2,1)S(1)}, bf16[256,256]{1,0:T(8,128)(2,1)S(1)}, u32[]{:S(2)}, u32[]{:S(2)}) collective-permute-start(bf16[256,256]{1,0:T(8,128)(2,1)S(1)} %get-tuple-element.164), channel_id=1, source_target_pairs={{0,8},{4,12},{8,0},{12,4},{16,24},{20,28},{24,16},{28,20},{1,9},{5... | collective-permute-start | bytes 393224 | tf_op jit(solution)/shard_map/ppermute | solution.py:582
  43.1 9.7 %collective-permute-start.8 = (bf16[512,256]{1,0:T(8,128)(2,1)S(1)}, bf16[512,256]{1,0:T(8,128)(2,1)S(1)}, u32[]{:S(2)}, u32[]{:S(2)}) collective-permute-start(bf16[512,256]{1,0:T(8,128)(2,1)S(1)} %get-tuple-element.159), channel_id=1, source_target_pairs={{0,2},{1,3},{2,0},{3,1},{4,6},{5,7},{6,4},{7,5},{8,10},{9,11},{10,... | collective-permute-start | bytes 786440 | tf_op jit(solution)/shard_map/ppermute | solution.py:582
  46.3 2.8 %collective-permute-start.10 = (bf16[384,256]{1,0:T(8,128)(2,1)S(1)}, bf16[384,256]{1,0:T(8,128)(2,1)S(1)}, u32[]{:S(2)}, u32[]{:S(2)}) collective-permute-start(bf16[384,256]{1,0:T(8,128)(2,1)S(1)} %shard_map.296), channel_id=1, source_target_pairs={{0,1},{1,0},{2,3},{3,2},{4,5},{5,4},{6,7},{7,6},{8,9},{9,8},{10,11... | collective-permute-start | bytes 589832 | tf_op jit(solution)/shard_map/ppermute | solution.py:582
  46.4 9.6 %collective-permute-start.14 = (bf16[256,256]{1,0:T(8,128)(2,1)S(1)}, bf16[256,256]{1,0:T(8,128)(2,1)S(1)}, u32[]{:S(2)}, u32[]{:S(2)}) collective-permute-start(bf16[256,256]{1,0:T(8,128)(2,1)S(1)} %shard_map.294.rest_0_.refs_1_.refs_2_.refs_0_), channel_id=1, source_target_pairs={{0,16},{4,20},{8,24},{12,28},{16,0},{20,4},{24,8},{28,12},{1,17},{... | collective-permute-start | bytes 393224 | tf_op jit(solution)/shard_map/ppermute | solution.py:582
  49.3 7.6 %collective-permute-start.11 = (bf16[112,256]{1,0:T(8,128)(2,1)S(1)}, bf16[112,256]{1,0:T(8,128)(2,1)S(1)}, u32[]{:S(2)}, u32[]{:S(2)}) collective-permute-start(bf16[112,256]{1,0:T(8,128)(2,1)S(1)} %shard_map.299), channel_id=1, source_target_pairs={{0,4},{4,0},{8,12},{12,8},{16,20},{20,16},{24,28},{28,24},{1,5},{5... | collective-permute-start | bytes 172040 | tf_op jit(solution)/shard_map/ppermute | solution.py:582
  50.8 6.1 %collective-permute-start.12 = (bf16[112,256]{1,0:T(8,128)(2,1)S(1)}, bf16[112,256]{1,0:T(8,128)(2,1)S(1)}, u32[]{:S(2)}, u32[]{:S(2)}) collective-permute-start(bf16[112,256]{1,0:T(8,128)(2,1)S(1)} %shard_map.300), channel_id=1, source_target_pairs={{0,2},{1,3},{2,0},{3,1},{4,6},{5,7},{6,4},{7,5},{8,10},{9,11},{10,... | collective-permute-start | bytes 172040 | tf_op jit(solution)/shard_map/ppermute | solution.py:582
  52.3 5.1 %collective-permute-start.13 = (bf16[112,256]{1,0:T(8,128)(2,1)S(1)}, bf16[112,256]{1,0:T(8,128)(2,1)S(1)}, u32[]{:S(2)}, u32[]{:S(2)}) collective-permute-start(bf16[112,256]{1,0:T(8,128)(2,1)S(1)} %shard_map.301.refs_2_), channel_id=1, source_target_pairs={{0,6},{1,7},{2,4},{3,5},{4,2},{5,3},{6,0},{7,1},{8,14},{9,15},{10,... | collective-permute-start | bytes 172040 | tf_op jit(solution)/shard_map/ppermute | solution.py:734
  56.1 5.8 %collective-permute-start.16 = (bf16[256,256]{1,0:T(8,128)(2,1)S(1)}, bf16[256,256]{1,0:T(8,128)(2,1)S(1)}, u32[]{:S(2)}, u32[]{:S(2)}) collective-permute-start(bf16[256,256]{1,0:T(8,128)(2,1)S(1)} %shard_map.302.refs_4_.refs_0_), channel_id=1, source_target_pairs={{0,8},{4,12},{8,0},{12,4},{16,24},{20,28},{24,16},{28,20},{1,9},{5... | collective-permute-start | bytes 393224 | tf_op jit(solution)/shard_map/ppermute | solution.py:582
  57.4 8.0 %collective-permute-start.15 = (bf16[112,256]{1,0:T(8,128)(2,1)S(1)}, bf16[112,256]{1,0:T(8,128)(2,1)S(1)}, u32[]{:S(2)}, u32[]{:S(2)}) collective-permute-start(bf16[112,256]{1,0:T(8,128)(2,1)S(1)} %shard_map.303.refs_2_.refs_0_), channel_id=1, source_target_pairs={{0,8},{4,12},{8,0},{12,4},{16,24},{20,28},{24,16},{28,20},{1,9},{5... | collective-permute-start | bytes 172040 | tf_op jit(solution)/shard_map/ppermute | solution.py:582
  61.9 10.2 %collective-permute-start.23 = (bf16[512,256]{1,0:T(8,128)(2,1)S(1)}, bf16[512,256]{1,0:T(8,128)(2,1)S(1)}, u32[]{:S(2)}, u32[]{:S(2)}) collective-permute-start(bf16[512,256]{1,0:T(8,128)(2,1)S(1)} %shard_map.304.refs_2_.refs_0_), channel_id=1, source_target_pairs={{0,6},{1,7},{2,4},{3,5},{4,2},{5,3},{6,0},{7,1},{8,14},{9,15},{10,... | collective-permute-start | bytes 786440 | tf_op jit(solution)/shard_map/ppermute | solution.py:734
  64.4 10.4 %collective-permute-start.22 = (bf16[512,256]{1,0:T(8,128)(2,1)S(1)}, bf16[512,256]{1,0:T(8,128)(2,1)S(1)}, u32[]{:S(2)}, u32[]{:S(2)}) collective-permute-start(bf16[512,256]{1,0:T(8,128)(2,1)S(1)} %shard_map.304.refs_2_.refs_0_), channel_id=1, source_target_pairs={{0,2},{1,3},{2,0},{3,1},{4,6},{5,7},{6,4},{7,5},{8,10},{9,11},{10,... | collective-permute-start | bytes 786440 | tf_op jit(solution)/shard_map/ppermute | solution.py:582
  64.9 10.0 %collective-permute-start.21 = (bf16[512,256]{1,0:T(8,128)(2,1)S(1)}, bf16[512,256]{1,0:T(8,128)(2,1)S(1)}, u32[]{:S(2)}, u32[]{:S(2)}) collective-permute-start(bf16[512,256]{1,0:T(8,128)(2,1)S(1)} %shard_map.304.refs_2_.refs_0_), channel_id=1, source_target_pairs={{0,4},{4,0},{8,12},{12,8},{16,20},{20,16},{24,28},{28,24},{1,5},{5... | collective-permute-start | bytes 786440 | tf_op jit(solution)/shard_map/ppermute | solution.py:582
  65.4 5.1 %collective-permute-start.17 = (bf16[112,256]{1,0:T(8,128)(2,1)S(1)}, bf16[112,256]{1,0:T(8,128)(2,1)S(1)}, u32[]{:S(2)}, u32[]{:S(2)}) collective-permute-start(bf16[112,256]{1,0:T(8,128)(2,1)S(1)} %shard_map.305.refs_0_), channel_id=1, source_target_pairs={{0,16},{4,20},{8,24},{12,28},{16,0},{20,4},{24,8},{28,12},{1,17},{... | collective-permute-start | bytes 172040 | tf_op jit(solution)/shard_map/ppermute | solution.py:582
  75.0 3.6 %collective-permute-start.24 = (bf16[2048,256]{1,0:T(8,128)(2,1)S(1)}, bf16[2048,256]{1,0:T(8,128)(2,1)S(1)}, u32[]{:S(2)}, u32[]{:S(2)}) collective-permute-start(bf16[2048,256]{1,0:T(8,128)(2,1)S(1)} %shard_map.307.mine), channel_id=1, source_target_pairs={{0,1},{1,0},{2,3},{3,2},{4,5},{5,4},{6,7},{7,6},{8,9},{9,8},{10,11... | collective-permute-start | bytes 3145736 | tf_op jit(solution)/shard_map/ppermute | solution.py:582
  75.1 5.8 %collective-permute-start.20 = (bf16[96,256]{1,0:T(8,128)(2,1)S(1)}, bf16[96,256]{1,0:T(8,128)(2,1)S(1)}, u32[]{:S(2)}, u32[]{:S(2)}) collective-permute-start(bf16[96,256]{1,0:T(8,128)(2,1)S(1)} %slice.25.refs_0_), channel_id=1, source_target_pairs={{0,6},{1,7},{2,4},{3,5},{4,2},{5,3},{6,0},{7,1},{8,14},{9,15},{10,... | collective-permute-start | bytes 147464 | tf_op jit(solution)/shard_map/ppermute | solution.py:734
  76.8 4.4 %collective-permute-start.19 = (bf16[96,256]{1,0:T(8,128)(2,1)S(1)}, bf16[96,256]{1,0:T(8,128)(2,1)S(1)}, u32[]{:S(2)}, u32[]{:S(2)}) collective-permute-start(bf16[96,256]{1,0:T(8,128)(2,1)S(1)} %slice.25.refs_0_), channel_id=1, source_target_pairs={{0,2},{1,3},{2,0},{3,1},{4,6},{5,7},{6,4},{7,5},{8,10},{9,11},{10,... | collective-permute-start | bytes 147464 | tf_op jit(solution)/shard_map/ppermute | solution.py:582
  78.1 4.1 %collective-permute-start.18 = (bf16[96,256]{1,0:T(8,128)(2,1)S(1)}, bf16[96,256]{1,0:T(8,128)(2,1)S(1)}, u32[]{:S(2)}, u32[]{:S(2)}) collective-permute-start(bf16[96,256]{1,0:T(8,128)(2,1)S(1)} %slice.25.refs_0_), channel_id=1, source_target_pairs={{0,4},{4,0},{8,12},{12,8},{16,20},{20,16},{24,28},{28,24},{1,5},{5... | collective-permute-start | bytes 147464 | tf_op jit(solution)/shard_map/ppermute | solution.py:582
  (19 other events, 28.4 us)
